TPU v7x, 32 devices: a whole 2x2x4 slice. The times are simulated.
32 devices in a mesh: tower: 2 (over y), batch: 16 (over z, x, core).
Axes of the slice: x: 2, y: 2, z: 4, core: 2. Of those that a mesh axis runs over, the one named last changes fastest.
Arguments:
- img_feat: bfloat16 [3072, 1536], P('batch'), may hold values from -6 to 6
- txt_feat: bfloat16 [3072, 1152], P('batch'), may hold values from -6 to 6
- img_proj: bfloat16 [1536, 1152], P('batch', 'tower'), may hold values from -0.15625 to 0.15625
- txt_proj: bfloat16 [1152, 1152], P('batch', 'tower'), may hold values from -0.1875 to 0.1875
- valid_rows: int32 [16], P('batch'), may hold values from 1 to 192, 2304 in all
Outputs:
- img_grad: bfloat16 [3072, 1536], P('batch', 'tower')
- txt_grad: bfloat16 [3072, 1152], P('batch', 'tower')
- img_proj_grad: float32 [1536, 1152], P('batch', 'tower')
- txt_proj_grad: float32 [1152, 1152], P('batch', 'tower')
Inputs may be any that keep to these rules, and one draw needn't show every extreme that they name: valid_rows[c] counts the valid leading rows of batch shard c; the entries sum to 2304.
All inputs are finite; a program needn't handle non-finite values.
Results may differ from a plain program's by a relative error of at most 0.0064.
Values may be sent and summed in bfloat16 or wider, within the bound.
No kernel may reach another device: no remote copies, remote signals or barrier semaphores. Data moves between devices by JAX's collectives and lax.ppermute only.
A program may use at most 128 MiB of HBM per device.

v0:
```python
import jax
import jax.numpy as jnp
from jax import lax
from jax.sharding import PartitionSpec as P

similarity_sharpness = 10.0
similarity_shift = -4.0
objective_multiplier = 262144.0
epsilon = 1e-06


def transpose_product(left, right):
    return lax.dot_general(
        left, right, (((0,), (0,)), ((), ())), preferred_element_type=jnp.float32
    )


def shards(img_feat, txt_feat, img_proj, txt_proj, valid_rows):
    tower_index = lax.axis_index("tower")
    shard_rows = img_feat.shape[0]
    half_cols = img_proj.shape[1]
    img_rows, txt_rows = (
        lax.all_gather(img_proj, "batch", axis=0, tiled=True),
        lax.all_gather(txt_proj, "batch", axis=0, tiled=True),
    )
    img_half, txt_half = (img_rows, txt_rows)
    p_img = jnp.dot(img_feat, img_half, preferred_element_type=jnp.float32)
    p_txt = jnp.dot(txt_feat, txt_half, preferred_element_type=jnp.float32)
    sq_img, sq_txt = lax.psum(
        (jnp.sum(p_img * p_img, axis=1), jnp.sum(p_txt * p_txt, axis=1)), "tower"
    )
    n_img = jnp.sqrt(sq_img + epsilon)
    n_txt = jnp.sqrt(sq_txt + epsilon)
    u_part = (p_img / n_img[:, None]).astype(jnp.bfloat16)
    v_part = (p_txt / n_txt[:, None]).astype(jnp.bfloat16)
    u_emb, v_emb = (
        lax.all_gather(u_part, "tower", axis=1, tiled=True),
        lax.all_gather(v_part, "tower", axis=1, tiled=True),
    )
    is_image = tower_index == 0
    local_embedding = jnp.where(is_image, u_emb, v_emb)
    foreign_feature_vector = jnp.where(is_image, v_emb, u_emb)
    mine_norm = jnp.where(is_image, n_img, n_txt)
    local_ids = jnp.arange(shard_rows, dtype=jnp.int32)
    mine_mask = (local_ids < valid_rows[0]).astype(jnp.float32)
    mine_ids = lax.axis_index("batch") * shard_rows + local_ids
    group_number = lax.all_gather(foreign_feature_vector, "batch", axis=0, tiled=True)
    group_mask = lax.all_gather(mine_mask.astype(jnp.bfloat16), "batch", axis=0, tiled=True)
    group_valid = group_mask.astype(jnp.float32)
    group_ids = jnp.arange(group_number.shape[0], dtype=jnp.int32)
    similarity_matrix = (
        similarity_sharpness
        * jnp.dot(local_embedding, group_number.T, preferred_element_type=jnp.float32)
        + similarity_shift
    )
    signs = jnp.where(mine_ids[:, None] == group_ids[None, :], 1.0, -1.0).astype(jnp.float32)
    pair_grad = (
        -signs
        * jax.nn.sigmoid(-signs * similarity_matrix)
        * mine_mask[:, None]
        * group_valid[None, :]
    )
    accumulated_aggregate = jnp.dot(
        pair_grad.astype(jnp.bfloat16), group_number, preferred_element_type=jnp.float32
    )
    accumulated_aggregate, matched_tally = (accumulated_aggregate, jnp.sum(group_valid))
    resident_derivative = accumulated_aggregate * (
        similarity_sharpness * objective_multiplier / matched_tally
    )
    mine_f = local_embedding.astype(jnp.float32)
    along = jnp.sum(mine_f * resident_derivative, axis=1, keepdims=True)
    dp_mine = ((resident_derivative - mine_f * along) / mine_norm[:, None]).astype(jnp.bfloat16)
    received = lax.all_to_all(
        dp_mine.reshape(shard_rows, 2, half_cols), "tower", split_axis=1, concat_axis=1, tiled=True
    )
    dp_img = received[:, 0, :]
    dp_txt = received[:, 1, :]
    img_terms = jnp.dot(dp_img, img_half.T, preferred_element_type=jnp.float32)
    txt_terms = jnp.dot(dp_txt, txt_half.T, preferred_element_type=jnp.float32)
    img_sum, txt_sum = (
        lax.psum_scatter(img_terms, "tower", scatter_dimension=1, tiled=True),
        lax.psum_scatter(txt_terms, "tower", scatter_dimension=1, tiled=True),
    )
    img_proj_grad = lax.psum_scatter(
        transpose_product(img_feat, dp_img), "batch", scatter_dimension=0, tiled=True
    )
    txt_proj_grad = lax.psum_scatter(
        transpose_product(txt_feat, dp_txt), "batch", scatter_dimension=0, tiled=True
    )
    return (
        img_sum.astype(jnp.bfloat16),
        txt_sum.astype(jnp.bfloat16),
        img_proj_grad,
        txt_proj_grad,
    )


def solution(mesh):
    in_specs = (
        P("batch", None),
        P("batch", None),
        P("batch", "tower"),
        P("batch", "tower"),
        P("batch"),
    )
    out_specs = (P("batch", "tower"), P("batch", "tower"), P("batch", "tower"), P("batch", "tower"))
    return jax.shard_map(shards, mesh=mesh, in_specs=in_specs, out_specs=out_specs, check_vma=False)
```

profile of v0, /device:TPU:0, one launch (start us, length us, event | category | flops | bytes accessed | tf_op | source)
XLA Modules:
  0.0 434.3 jit_solution(11718740370147818599)
XLA Ops:
  8.7 43.5 %all-gather.8.cloned.1.call-done = bf16[1152,576]{1,0:T(8,128)(2,1)} async-done(((bf16[72,576]{1,0:T(8,128)(2,1)}), bf16[1152,576]{1,0:T(8,128)(2,1)}) %all-gather.8.cloned.1.call-update) | async-done | bytes 1327120 | tf_op jit(solution)/shard_map/all_gather | solution.py:24
  52.2 2.2 multiply_reduce_fusion
  54.4 39.8 %all-gather.6.cloned.1.call-done = bf16[1536,576]{1,0:T(8,128)(2,1)} async-done(((bf16[96,576]{1,0:T(8,128)(2,1)}), bf16[1536,576]{1,0:T(8,128)(2,1)}) %all-gather.6.cloned.1.call-update) | async-done | bytes 1769488 | tf_op jit(solution)/shard_map/all_gather | solution.py:23
  94.2 2.3 multiply_reduce_fusion.1
  96.5 4.9 %all-reduce.2 = (f32[192]{0:T(256)S(1)}, f32[192]{0:T(256)S(1)}) all-reduce(f32[192]{0:T(256)S(1)} %get-tuple-element.25, f32[192]{0:T(256)S(1)} %get-tuple-element.27), channel_id=1, replica_groups=mesh['tower'=2,'batch'=16] {'tower'}, use_global_device_ids=true, to_apply=%region_3.0 | all-reduce | flops 384 | bytes 3072 | tf_op jit(solution)/shard_map/psum | solution.py:29
  101.6 7.6 %all-gather.1 = bf16[2,576,192]{1,2,0:T(8,128)(2,1)S(1)} all-gather(bf16[1,576,192]{1,2,0:T(8,128)(2,1)S(1)} %fusion.22), channel_id=1, replica_groups=mesh['tower'=2,'batch'=16] {'tower'}, dimensions={0}, use_global_device_ids=true | all-gather | bytes 663552 | tf_op jit(solution)/shard_map/all_gather | solution.py:38
  109.3 6.9 %all-gather = bf16[2,576,192]{1,2,0:T(8,128)(2,1)S(1)} all-gather(bf16[1,576,192]{1,2,0:T(8,128)(2,1)S(1)} %fusion.21), channel_id=1, replica_groups=mesh['tower'=2,'batch'=16] {'tower'}, dimensions={0}, use_global_device_ids=true | all-gather | bytes 663552 | tf_op jit(solution)/shard_map/all_gather | solution.py:37
  116.8 1.1 reshape.38
  120.2 30.9 %all-reduce = bf16[3072]{0:T(1024)(128)(2,1)S(1)} all-reduce(bf16[3072]{0:T(1024)(128)(2,1)S(1)} %dynamic-update-slice), channel_id=1, replica_groups=mesh['tower'=2,'batch'=16] {'batch'}, use_global_device_ids=true, to_apply=%add | all-reduce | flops 3072 | bytes 12288
  153.3 30.8 %all-gather.10.cloned.1.call-done = bf16[3072,1152]{1,0:T(8,128)(2,1)} async-done(((bf16[192,1152]{1,0:T(8,128)(2,1)}), bf16[3072,1152]{1,0:T(8,128)(2,1)}) %all-gather.10.cloned.1.call-update) | async-done | bytes 7077904 | tf_op jit(solution)/shard_map/all_gather | solution.py:47
  184.1 9.3 %fusion.17 = (f32[192]{0:T(256)S(1)}, f32[192,1152]{1,0:T(8,128)S(1)}) fusion(bf16[1152,192]{0,1:T(8,128)(2,1)S(1)} %reshape.36, f32[]{:T(128)S(6)} %div.35, bf16[3072,1152]{1,0:T(8,128)(2,1)} %all-gather.10.cloned.1.call-done, f32[3072]{0:T(1024)S(1)} %convert_element_type.38, f32[192]{0:T(256)S(1)} %compare_convert_fusion, s32[192]{0:T(256)S(1)} %iota_add_fusion), kind=kOutput, calls=%fused_computation.25 | convolution fusion | flops 2726461184 | bytes 8419588 | tf_op jit(solution)/shard_map/dot_general | solution.py:63
  194.2 10.7 %all_to_all.5 = bf16[192,2,576]{2,0,1:T(8,128)(2,1)S(1)} all-to-all(bf16[192,2,576]{2,0,1:T(8,128)(2,1)S(1)} %copy.18), channel_id=1, replica_groups=mesh['tower'=2,'batch'=16] {'tower'}, dimensions={1} | all-to-all | bytes 884736 | tf_op jit(solution)/shard_map/all_to_all | solution.py:73
  204.9 2.1 convolution_bitcast_fusion.1
  207.1 3.2 convolution_bitcast_fusion.2
  210.4 1.8 fusion.23
  212.3 2.4 convolution_bitcast_fusion
  214.7 5.4 %copy.23 = f32[1536,576]{1,0:T(8,128)} copy(f32[1536,576]{0,1:T(8,128)} %convolution_bitcast_fusion) | data formatting | bytes 7077888
  220.7 85.0 %all-reduce.5.cloned.1.call-done = f32[1152,576]{0,1:T(8,128)} async-done(((f32[1152,576]{0,1:T(8,128)}), f32[1152,576]{0,1:T(8,128)}) %all-reduce.5.cloned.1.call-update) | async-done | bytes 2654224
  305.7 1.2 constant_dynamic-slice_fusion
  307.7 20.9 %reduce-scatter.11.cloned.1.call-done = f32[576,192]{1,0:T(8,128)} async-done(((f32[1152,192]{1,0:T(8,128)}), f32[576,192]{1,0:T(8,128)}) %reduce-scatter.11.cloned.1.call-update) | async-done | bytes 442384
  328.6 1.9 copy.22
  330.5 22.1 %reduce-scatter.9.cloned.1.call-done = f32[192,768]{1,0:T(8,128)} async-done(((f32[192,1536]{1,0:T(8,128)}), f32[192,768]{1,0:T(8,128)}) %reduce-scatter.9.cloned.1.call-update) | async-done | bytes 589840 | tf_op jit(solution)/shard_map/reduce_scatter | solution.py:81
  352.6 1.8 convert_element_type.42
  354.4 73.1 %reduce-scatter.13.cloned.1.call-done = f32[96,576]{1,0:T(8,128)} async-done(((f32[1536,576]{1,0:T(8,128)}), f32[96,576]{1,0:T(8,128)}) %reduce-scatter.13.cloned.1.call-update) | async-done | bytes 221200
  (41 shorter events, 6.5 us)
Async XLA Ops:
  7.2 87.1 %copy-start = (bf16[192,1536]{1,0:T(8,128)(2,1)S(1)}, bf16[192,1536]{1,0:T(8,128)(2,1)}, u32[]{:S(2)}) copy-start(bf16[192,1536]{1,0:T(8,128)(2,1)} %param.5) | copy-start | bytes 1769476
  7.2 45.1 %all-gather.8.cloned.1.call-start = ((), (), s32[]{:S(2)}) async-start(), calls=%async_computation.5 | async-start | bytes 1566720 | tf_op jit(solution)/shard_map/all_gather | solution.py:24
  7.9 86.3 %all-gather.6.cloned.1.call-start = ((), (), s32[]{:S(2)}) async-start(), calls=%async_computation.4 | async-start | bytes 2088960 | tf_op jit(solution)/shard_map/all_gather | solution.py:23
  8.7 175.4 %all-gather.10.cloned.1.call-start = ((), (), s32[]{:S(2)}) async-start(), calls=%async_computation.6 | async-start | bytes 7520256 | tf_op jit(solution)/shard_map/all_gather | solution.py:47
  116.2 2.5 copy-start.3
  117.9 187.8 %all-reduce.5.cloned.1.call-start = ((), (), s32[]{:S(2)}) async-start(), calls=%async_computation.10 | async-start | bytes 5308416
  193.4 11.5 %copy-start.2 = (bf16[192,1152]{1,0:T(8,128)(2,1)S(1)}, bf16[192,1152]{1,0:T(8,128)(2,1)}, u32[]{:S(2)}) copy-start(bf16[192,1152]{1,0:T(8,128)(2,1)} %param.6) | copy-start | bytes 1327108
  207.0 3.3 copy-start.1
  207.0 121.6 %reduce-scatter.11.cloned.1.call-start = ((), (), s32[]{:S(2)}) async-start(), calls=%async_computation.8 | async-start | bytes 1769472
  210.3 142.3 %reduce-scatter.9.cloned.1.call-start = ((), (), s32[]{:S(2)}) async-start(), calls=%async_computation.7 | async-start | bytes 1769472 | tf_op jit(solution)/shard_map/reduce_scatter | solution.py:81
  212.2 215.2 %reduce-scatter.13.cloned.1.call-start = ((), (), s32[]{:S(2)}) async-start(), calls=%async_computation.9 | async-start | bytes 4177920
Sparse Core Ops, SparseCore 0:
  10.2 42.0 all-gather.7
  54.5 39.6 all-gather.5
  118.1 65.9 all-gather.9
  207.1 98.5 all-reduce.4
  307.8 20.7 reduce-scatter.10
  330.8 21.7 reduce-scatter.8
  357.1 70.3 reduce-scatter.12
where the time goes:
time: 435 us; the launch traced here: 434 us
  waiting for transfers between devices  317 us (73%)
  blocking collectives  61.1 us (14%)
  matrix products  23.3 us (5%)
  between operations  17 us (4%)
  local copies, waits for them, and re-layouts  13.2 us (3%)
    unnamed x10, waiting for transfers between devices  180 us
    all_gather x1, waiting for transfers between devices, shards(): lax.all_gather(txt_proj, 'batch', axis=0, tiled=True)  43.5 us
    all_gather x1, waiting for transfers between devices, shards(): lax.all_gather(img_proj, 'batch', axis=0, tiled=True)  39.8 us
    unnamed x1, blocking collectives  30.9 us
    all_gather x1, waiting for transfers between devices, shards(): lax.all_gather(foreign_feature_vector, 'batch', axis=0, tiled=True)  30.8 us
    reduce_scatter x1, waiting for transfers between devices, shards(): lax.psum_scatter(img_terms, 'tower', scatter_dimension=1, tiled=True)  22.1 us
    all_to_all x1, blocking collectives, shards(): lax.all_to_all(dp_mine.reshape(shard_rows, 2, half_cols), 'tower', split_...  10.7 us
    unnamed x15, local copies, waits for them, and re-layouts  10.2 us
  transfers between devices with their start and end apart: 7, of which 7 were waited for; matrix products, arithmetic and copies ran while one was open for 5% of the time, Pallas kernels for 0%

commit v1 on v0

v1 whole, which is shorter than its diff:
```python
import jax
import jax.numpy as jnp
from jax import lax
from jax.sharding import PartitionSpec as P

sharpness = 10.0
shift = -4.0
multiplier = 262144.0
epsilon = 1e-06

F32, BF16 = jnp.float32, jnp.bfloat16


def dot(a, b, dims):
    return lax.dot_general(a, b, (dims, ((), ())), preferred_element_type=F32)


class Ring:
    def __init__(self, batch_size):
        n = self.n = batch_size // 2
        half = n // 2
        self.order = [2 * r if r < half else 2 * (n - 1 - r) + 1 for r in range(n)]
        place = {chip: r for r, chip in enumerate(self.order)}
        self.place = [place[chip] for chip in range(n)]
        self.fwd = self._perm(1)
        self.bwd = self._perm(-1)
        self.core = [(b, b ^ 1) for b in range(batch_size)]
        chip = lax.axis_index("batch") // 2
        self.pos = jnp.where(chip % 2 == 0, chip // 2, n - 1 - chip // 2)

    def _perm(self, step):
        pairs = []
        for r, chip in enumerate(self.order):
            to = self.order[(r + step) % self.n]
            pairs += [(2 * chip + c, 2 * to + c) for c in range(2)]
        return pairs

    def right(self, x):
        return lax.ppermute(x, "batch", self.fwd)

    def left(self, x):
        return lax.ppermute(x, "batch", self.bwd)

    def other_core(self, x):
        return lax.ppermute(x, "batch", self.core)

    def relative(self, stack):
        by_place = jnp.stack([stack[chip] for chip in self.order])
        twice = jnp.concatenate([by_place, by_place])
        return lax.dynamic_slice_in_dim(twice, self.pos, self.n, 0)

    def absolute(self, stack):
        twice = jnp.concatenate([stack, stack])
        by_place = lax.dynamic_slice_in_dim(twice, self.n - self.pos, self.n, 0)
        return jnp.stack([by_place[r] for r in self.place])

    def gather_steps(self, x, cut):
        n = self.n
        f = b = x
        for k in range(1, n // 2):
            f, b = self.right(f), self.left(b)
            yield [(n - k, f), (k, b)]
        f, b = self.right(f[:cut]), self.left(b[cut:])
        yield [(n // 2, jnp.concatenate([f, b]))]


def swap(x):
    return lax.ppermute(x, "tower", [(0, 1), (1, 0)])


def shards(img_feat, txt_feat, img_proj, txt_proj, valid_rows):
    nb = lax.axis_size("batch")
    ring = Ring(nb)
    n = ring.n
    tower = lax.axis_index("tower")
    is_image = tower == 0
    core = lax.axis_index("batch") % 2
    rows = img_feat.shape[0]
    ri, half = img_proj.shape
    rt = txt_proj.shape[0]

    count_rows = jnp.broadcast_to(valid_rows.astype(BF16)[:, None], (8, half))
    w = jnp.concatenate([img_proj, txt_proj, count_rows])
    got = {0: w}
    for step in ring.gather_steps(w, ri):
        got.update(step)

    def columns(feat, width):
        t = feat.T.reshape(n, 2, width, rows)
        keep = lax.dynamic_index_in_dim(t, core, 1, keepdims=False)
        give = lax.dynamic_index_in_dim(t, 1 - core, 1, keepdims=False)
        return ring.relative(jnp.concatenate([keep, ring.other_core(give)], axis=2))

    img_t = columns(img_feat, ri).reshape(n * ri, 2 * rows)
    txt_t = columns(txt_feat, rt).reshape(n * rt, 2 * rows)

    w_img = jnp.stack([got[d][:ri] for d in range(n)])
    w_txt = jnp.stack([got[d][ri : ri + rt] for d in range(n)])
    count = sum(got[d][ri + rt, 0].astype(F32) for d in range(n))
    count = jnp.broadcast_to(count, (8, 128))
    count = (count + ring.other_core(count))[0, 0]

    p_img2 = dot(img_t, w_img.reshape(n * ri, half), ((0,), (0,)))
    p_txt2 = dot(txt_t, w_txt.reshape(n * rt, half), ((0,), (0,)))
    p_give = jnp.concatenate([p_img2[rows:], p_txt2[rows:]], axis=0)
    p_got = ring.other_core(p_give)
    p_img = p_img2[:rows] + p_got[:rows]
    p_txt = p_txt2[:rows] + p_got[rows:]

    sq = jnp.stack([jnp.sum(p_img * p_img, axis=1), jnp.sum(p_txt * p_txt, axis=1)])
    sq = sq + swap(sq)
    norms = jnp.sqrt(sq + epsilon)
    n_img, n_txt = norms[0], norms[1]
    mask = jnp.arange(rows, dtype=jnp.int32) < valid_rows[0]
    u = jnp.where(mask[:, None], p_img / n_img[:, None], 0.0).astype(BF16)
    v = jnp.where(mask[:, None], p_txt / n_txt[:, None], 0.0).astype(BF16)
    mine_norm = jnp.where(is_image, n_img, n_txt)

    mine_o = jnp.where(is_image, u, v)
    other_o = jnp.where(is_image, v, u)
    other_x = swap(mine_o)
    mine_x = swap(other_o)
    own = jnp.concatenate([mine_o, mine_x], axis=1)
    own2 = jnp.concatenate([own, ring.other_core(own)], axis=0)
    own2_o, own2_x = own2[:, :half], own2[:, half:]

    def logits(fo, fx):
        s = dot(own2_o, fo, ((1,), (1,))) + dot(own2_x, fx, ((1,), (1,)))
        return sharpness * s + shift

    s = logits(other_o, other_x)
    diag = (
        lax.broadcasted_iota(jnp.int32, s.shape, 0) == lax.broadcasted_iota(jnp.int32, s.shape, 1)
    )
    g = jax.nn.sigmoid(jnp.where(diag, -s, s))
    qb = jnp.where(diag, -g, g).astype(BF16)
    acc_o = dot(qb, other_o, ((1,), (0,)))
    acc_x = dot(qb, other_x, ((1,), (0,)))
    cut = rows // 2
    for so, sx in zip(ring.gather_steps(other_o, cut), ring.gather_steps(other_x, cut)):
        fo = jnp.concatenate([c for _, c in so])
        fx = jnp.concatenate([c for _, c in sx])
        qb = jax.nn.sigmoid(logits(fo, fx)).astype(BF16)
        acc_o = acc_o + dot(qb, fo, ((1,), (0,)))
        acc_x = acc_x + dot(qb, fx, ((1,), (0,)))
    acc = jnp.concatenate([acc_o, acc_x], axis=1)
    acc = acc[:rows] + ring.other_core(acc[rows:])

    du = acc * (sharpness * multiplier / count)
    mine_f = own.astype(F32)
    along = jnp.sum(mine_f * du, axis=1, keepdims=True)
    dp = jnp.where(mask[:, None], (du - mine_f * along) / mine_norm[:, None], 0.0).astype(BF16)
    dp_mine, dp_give = dp[:, :half], dp[:, half:]
    dp_got = swap(dp_give)
    dp_img = jnp.where(is_image, dp_mine, dp_got)
    dp_txt = jnp.where(is_image, dp_got, dp_mine)
    dp_both = jnp.concatenate([dp_img, dp_txt], axis=1)
    dp2 = jnp.concatenate([dp_both, ring.other_core(dp_both)], axis=0)

    g_img = dot(img_t, dp2[:, :half], ((1,), (0,))).reshape(n, ri, half)
    g_txt = dot(txt_t, dp2[:, half:], ((1,), (0,))).reshape(n, rt, half)

    def part(d):
        return jnp.concatenate([g_img[d], g_txt[d]])

    h = n // 2
    f = ring.right(g_img[h].astype(BF16))
    b = ring.left(g_txt[h].astype(BF16))
    for k in range(h - 1, 0, -1):
        pf, pb = part(k), part(n - k)
        if k == h - 1:
            f = jnp.concatenate([g_img[k] + f.astype(F32), g_txt[k]])
            b = jnp.concatenate([g_img[n - k], g_txt[n - k] + b.astype(F32)])
        else:
            f, b = pf + f.astype(F32), pb + b.astype(F32)
        f, b = ring.right(f.astype(BF16)), ring.left(b.astype(BF16))
    total = part(0) + f.astype(F32) + b.astype(F32)

    w_all = jnp.concatenate([w_img.reshape(n * ri, half), w_txt.reshape(n * rt, half)])
    w_sib = ring.other_core(w_all)

    def weights(at, width):
        a = ring.absolute(w_all[at : at + n * width].reshape(n, width, half))
        s = ring.absolute(w_sib[at : at + n * width].reshape(n, width, half))
        both = jnp.stack([jnp.where(core == 0, a, s), jnp.where(core == 0, s, a)], axis=1)
        return both.reshape(2 * n * width, half)

    wi, wt = weights(0, ri), weights(n * ri, rt)

    def halves(wm):
        m = wm.shape[0] // 2
        keep = lax.dynamic_slice_in_dim(wm, tower * m, m, 0)
        give = lax.dynamic_slice_in_dim(wm, (1 - tower) * m, m, 0)
        return keep, give

    (ki, gi), (kt, gt) = halves(wi), halves(wt)
    give = jnp.concatenate(
        [
            dot(dp_img, gi, ((1,), (1,))).astype(BF16),
            dot(dp_txt, gt, ((1,), (1,))).astype(BF16),
        ],
        axis=1,
    )
    recv = swap(give).astype(F32)
    mi = ki.shape[0]
    img_grad = dot(dp_img, ki, ((1,), (1,))) + recv[:, :mi]
    txt_grad = dot(dp_txt, kt, ((1,), (1,))) + recv[:, mi:]
    return (img_grad.astype(BF16), txt_grad.astype(BF16), total[:ri], total[ri:])


def solution(mesh):
    in_specs = (
        P("batch", None),
        P("batch", None),
        P("batch", "tower"),
        P("batch", "tower"),
        P("batch"),
    )
    out_specs = (P("batch", "tower"),) * 4
    return jax.shard_map(shards, mesh=mesh, in_specs=in_specs, out_specs=out_specs, check_vma=False)
```

time: 435 us -> 248 us (0.57)
  waiting for transfers between devices: 317 us -> 54.1 us
  local copies, waits for them, and re-layouts: 13.2 us -> 93.5 us
  blocking collectives: 61.1 us -> 0 us
  starting transfers between devices: 0.28 us -> 40.8 us
  other arithmetic: 2.96 us -> 26.1 us
  between operations: 17 us -> 7.5 us
    unnamed x10 -> x0, waiting for transfers between devices: 180 us -> none
    all_gather x3 -> x0, waiting for transfers between devices: 114 us -> none  [the longest x1 43.5 us: shards(): lax.all_gather(txt_proj, 'batch', axis=0, tiled=True)]
    ppermute x0 -> x45, waiting for transfers between devices: none -> 54.1 us  [the longest x16 25.8 us: left(): return lax.ppermute(x, 'batch', self.bwd)]
    unnamed x15 -> x129, local copies, waits for them, and re-layouts: 10.2 us -> 52.9 us
    ppermute x0 -> x45, starting transfers between devices: none -> 40.8 us  [the longest x16 22.5 us: left(): return lax.ppermute(x, 'batch', self.bwd)]
    unnamed x1 -> x0, blocking collectives: 30.9 us -> none
    reduce_scatter x1 -> x0, waiting for transfers between devices: 22.1 us -> none  [shards(): lax.psum_scatter(img_terms, 'tower', scatter_dimension=1, tiled=True)]
    slice x0 -> x27, local copies, waits for them, and re-layouts: none -> 16.8 us  [the longest x7 5.87 us: shards(): count = sum((got[d][ri + rt, 0].astype(F32) for d in range(n)))]
  transfers between devices with their start and end apart: 7 -> 45, of which waited for: 7 -> 16; matrix products, arithmetic and copies ran while one was open for 5% -> 49% of each run, Pallas kernels for 0% -> 0%
where the time goes in v1:
time: 248 us; the launch traced here: 246 us
  local copies, waits for them, and re-layouts  93.5 us (38%)
  waiting for transfers between devices  54.1 us (22%)
  starting transfers between devices  40.8 us (16%)
  other arithmetic  26.1 us (11%)
  matrix products  23.9 us (10%)
  between operations  7.5 us (3%)
    unnamed x129, local copies, waits for them, and re-layouts  52.9 us
    ppermute x16, waiting for transfers between devices, left(): return lax.ppermute(x, 'batch', self.bwd)  25.8 us
    ppermute x5, waiting for transfers between devices, swap(): return lax.ppermute(x, 'tower', [(0, 1), (1, 0)])  24 us
    dot_general x28, matrix products, dot(): return lax.dot_general(a, b, (dims, ((), ())), preferred_element_type=F32)  23.9 us
    ppermute x16, starting transfers between devices, left(): return lax.ppermute(x, 'batch', self.bwd)  22.5 us
    ppermute x16, starting transfers between devices, right(): return lax.ppermute(x, 'batch', self.fwd)  13 us
    ppermute x3, local copies, waits for them, and re-layouts, other_core(): return lax.ppermute(x, 'batch', self.core)  5.9 us
    slice x7, local copies, waits for them, and re-layouts, shards(): count = sum((got[d][ri + rt, 0].astype(F32) for d in range(n)))  5.87 us
  transfers between devices with their start and end apart: 45, of which 16 were waited for; matrix products, arithmetic and copies ran while one was open for 49% of the time, Pallas kernels for 0%

profile of v1, /device:TPU:0, one launch (start us, length us, event | category | flops | bytes accessed | tf_op | source)
XLA Modules:
  0.0 245.9 jit_solution(2296095112581127575)
XLA Ops:
  3.2 2.9 %collective-permute-start.1 = (bf16[176,576]{1,0:T(8,128)(2,1)}, bf16[176,576]{1,0:T(8,128)(2,1)}, u32[]{:S(2)}, u32[]{:S(2)}) collective-permute-start(bf16[176,576]{1,0:T(8,128)(2,1)} %maximum_maximum_fusion), channel_id=1, source_target_pairs={{0,2},{1,3},{4,0},{5,1},{8,4},{9,5},{12,8},{13,9},{14,12},{15,13},... | collective-permute-start | bytes 608264 | tf_op jit(solution)/shard_map/ppermute | solution.py:42
  10.6 1.9 copy.98
  17.2 2.0 collective-permute-start.2
  27.1 1.9 collective-permute-start.3
  31.1 3.3 %collective-permute-done.3 = bf16[176,576]{1,0:T(8,128)(2,1)S(1)} collective-permute-done((bf16[176,576]{1,0:T(8,128)(2,1)S(1)}, bf16[176,576]{1,0:T(8,128)(2,1)S(1)}, u32[]{:S(2)}, u32[]{:S(2)}) %collective-permute-start.3) | collective-permute-done | bytes 202784 | tf_op jit(solution)/shard_map/ppermute | solution.py:42
  62.3 1.7 constant_dynamic-update-slice_fusion.55
  78.8 2.2 copy.67
  81.0 2.7 %pad_maximum_fusion.1 = bf16[1344,576]{0,1:T(8,128)(2,1)} fusion(bf16[576,576]{0,1:T(8,128)(2,1)} %copy.68, bf16[768,576]{0,1:T(8,128)(2,1)} %copy.67), kind=kLoop, calls=%fused_computation.5 | loop fusion | flops 3096576 | bytes 3096576 | tf_op jit(solution)/shard_map/concatenate | solution.py:179
  96.8 11.3 %collective-permute-done.14 = bf16[192,576]{0,1:T(8,128)(2,1)S(1)} collective-permute-done((bf16[192,576]{0,1:T(8,128)(2,1)S(1)}, bf16[192,576]{0,1:T(8,128)(2,1)S(1)}, u32[]{:S(2)}, u32[]{:S(2)}) %collective-permute-start.14) | collective-permute-done | bytes 221216 | tf_op jit(solution)/shard_map/ppermute | solution.py:68
  113.3 4.9 %collective-permute-done.18 = bf16[192,576]{0,1:T(8,128)(2,1)} collective-permute-done((bf16[192,576]{0,1:T(8,128)(2,1)S(1)}, bf16[192,576]{0,1:T(8,128)(2,1)}, u32[]{:S(2)}, u32[]{:S(2)}) %collective-permute-start.18) | collective-permute-done | bytes 221216 | tf_op jit(solution)/shard_map/ppermute | solution.py:42
  121.2 2.5 %collective-permute-done.20 = bf16[192,576]{0,1:T(8,128)(2,1)} collective-permute-done((bf16[192,576]{0,1:T(8,128)(2,1)S(1)}, bf16[192,576]{0,1:T(8,128)(2,1)}, u32[]{:S(2)}, u32[]{:S(2)}) %collective-permute-start.20) | collective-permute-done | bytes 221216 | tf_op jit(solution)/shard_map/ppermute | solution.py:42
  163.6 2.2 collective-permute-done.30
  172.1 2.5 %copy.65 = f32[192,1152]{1,0:T(8,128)} copy(f32[192,1152]{0,1:T(8,128)} %pad_maximum_fusion.3) | data formatting | bytes 1769472 | tf_op jit(solution)/shard_map/slice | solution.py:147
  176.3 1.9 fusion.64
  178.2 2.6 %broadcast_select_fusion.3 = (bf16[8,1,72,576]{3,2,0,1:T(8,128)(2,1)}, bf16[8,1,72,576]{3,2,0,1:T(8,128)(2,1)}) fusion(bf16[8,1,72,576]{3,2,0,1:T(8,128)(2,1)S(1)} %copy-done.19, bf16[8,1,72,576]{3,2,0,1:T(8,128)(2,1)} %copy-done.20, pred[]{:T(512)S(6)} %eq.23), kind=kLoop, calls=%fused_computation.83 | loop fusion | flops 663552 | bytes 2654209 | tf_op jit(solution)/shard_map/jit(_where)/select_n | solution.py:185
  180.8 2.7 %broadcast_select_fusion.1 = (bf16[8,1,96,576]{3,2,0,1:T(8,128)(2,1)}, bf16[8,1,96,576]{3,2,0,1:T(8,128)(2,1)}) fusion(bf16[8,1,96,576]{3,2,0,1:T(8,128)(2,1)S(1)} %copy-done.13, bf16[8,1,96,576]{3,2,0,1:T(8,128)(2,1)} %get-tuple-element.103, pred[]{:T(512)S(6)} %eq.23), kind=kLoop, calls=%fused_computation.75 | loop fusion | flops 884736 | bytes 3538945 | tf_op jit(solution)/shard_map/jit(_where)/select_n | solution.py:185
  183.5 2.6 %copy.66 = f32[192,1152]{0,1:T(8,128)} copy(f32[192,1152]{1,0:T(8,128)} %collective-permute-done.31) | data formatting | bytes 1769472 | tf_op jit(solution)/shard_map/ppermute | solution.py:45
  192.2 5.1 %collective-permute-done.33 = bf16[192,576]{0,1:T(8,128)(2,1)S(1)} collective-permute-done((bf16[192,576]{0,1:T(8,128)(2,1)S(1)}, bf16[192,576]{0,1:T(8,128)(2,1)S(1)}, u32[]{:S(2)}, u32[]{:S(2)}) %collective-permute-start.33) | collective-permute-done | bytes 221216 | tf_op jit(solution)/shard_map/ppermute | solution.py:68
  198.2 2.1 copy.85
  203.3 2.1 copy.86
  210.5 6.6 %collective-permute-done.35 = bf16[192,1344]{1,0:T(8,128)(2,1)} collective-permute-done((bf16[192,1344]{1,0:T(8,128)(2,1)}, bf16[192,1344]{1,0:T(8,128)(2,1)}, u32[]{:S(2)}, u32[]{:S(2)}) %collective-permute-start.35) | collective-permute-done | bytes 516128 | tf_op jit(solution)/shard_map/ppermute | solution.py:68
  222.8 5.0 %collective-permute-done.42 = bf16[168,576]{0,1:T(8,128)(2,1)S(1)} collective-permute-done((bf16[168,576]{0,1:T(8,128)(2,1)S(1)}, bf16[168,576]{0,1:T(8,128)(2,1)S(1)}, u32[]{:S(2)}, u32[]{:S(2)}) %collective-permute-start.42) | collective-permute-done | bytes 193568 | tf_op jit(solution)/shard_map/ppermute | solution.py:42
  230.5 4.7 %collective-permute-done.43 = bf16[168,576]{0,1:T(8,128)(2,1)S(1)} collective-permute-done((bf16[168,576]{0,1:T(8,128)(2,1)S(1)}, bf16[168,576]{0,1:T(8,128)(2,1)S(1)}, u32[]{:S(2)}, u32[]{:S(2)}) %collective-permute-start.43) | collective-permute-done | bytes 193568 | tf_op jit(solution)/shard_map/ppermute | solution.py:42
  239.0 3.2 %collective-permute-done.44 = bf16[168,576]{0,1:T(8,128)(2,1)S(1)} collective-permute-done((bf16[168,576]{0,1:T(8,128)(2,1)S(1)}, bf16[168,576]{0,1:T(8,128)(2,1)S(1)}, u32[]{:S(2)}, u32[]{:S(2)}) %collective-permute-start.44) | collective-permute-done | bytes 193568 | tf_op jit(solution)/shard_map/ppermute | solution.py:42
  (329 shorter events, 157.8 us)
Async XLA Ops:
  3.2 12.2 %collective-permute-start.1 = (bf16[176,576]{1,0:T(8,128)(2,1)}, bf16[176,576]{1,0:T(8,128)(2,1)}, u32[]{:S(2)}, u32[]{:S(2)}) collective-permute-start(bf16[176,576]{1,0:T(8,128)(2,1)} %maximum_maximum_fusion), channel_id=1, source_target_pairs={{0,2},{1,3},{4,0},{5,1},{8,4},{9,5},{12,8},{13,9},{14,12},{15,13},... | collective-permute-start | bytes 608264 | tf_op jit(solution)/shard_map/ppermute | solution.py:42
  6.1 13.0 %collective-permute-start.4 = (bf16[176,576]{1,0:T(8,128)(2,1)}, bf16[176,576]{1,0:T(8,128)(2,1)}, u32[]{:S(2)}, u32[]{:S(2)}) collective-permute-start(bf16[176,576]{1,0:T(8,128)(2,1)} %maximum_maximum_fusion), channel_id=1, source_target_pairs={{0,4},{1,5},{4,8},{5,9},{8,12},{9,13},{12,14},{13,15},{14,10},{15,... | collective-permute-start | bytes 608264 | tf_op jit(solution)/shard_map/ppermute | solution.py:39
  8.2 15.4 %collective-permute-start.8 = (bf16[8,72,192]{2,1,0:T(8,128)(2,1)}, bf16[8,72,192]{2,1,0:T(8,128)(2,1)S(1)}, u32[]{:S(2)}, u32[]{:S(2)}) collective-permute-start(bf16[8,72,192]{2,1,0:T(8,128)(2,1)} %get-tuple-element.64), channel_id=1, source_target_pairs={{0,1},{1,0},{2,3},{3,2},{4,5},{5,4},{6,7},{7,6},{8,9},{9,8},{10,11... | collective-permute-start | bytes 663560 | tf_op jit(solution)/shard_map/ppermute | solution.py:45
  12.4 12.3 %collective-permute-start = (bf16[8,96,192]{2,1,0:T(8,128)(2,1)}, bf16[8,96,192]{2,1,0:T(8,128)(2,1)S(1)}, u32[]{:S(2)}, u32[]{:S(2)}) collective-permute-start(bf16[8,96,192]{2,1,0:T(8,128)(2,1)} %bitcast.3), channel_id=1, source_target_pairs={{0,1},{1,0},{2,3},{3,2},{4,5},{5,4},{6,7},{7,6},{8,9},{9,8},{10,11... | collective-permute-start | bytes 884744 | tf_op jit(solution)/shard_map/ppermute | solution.py:45
  36.6 25.6 %collective-permute-start.7 = (bf16[96,576]{1,0:T(8,128)(2,1)}, bf16[96,576]{1,0:T(8,128)(2,1)}, u32[]{:S(2)}, u32[]{:S(2)}) collective-permute-start(bf16[96,576]{1,0:T(8,128)(2,1)} %slice.484), channel_id=1, source_target_pairs={{0,4},{1,5},{4,8},{5,9},{8,12},{9,13},{12,14},{13,15},{14,10},{15,... | collective-permute-start | bytes 331784 | tf_op jit(solution)/shard_map/ppermute | solution.py:39
  55.4 22.2 %collective-permute-start.32 = (f32[8,128]{1,0:T(8,128)S(1)}, f32[8,128]{1,0:T(8,128)S(1)}, u32[]{:S(2)}, u32[]{:S(2)}) collective-permute-start(f32[8,128]{1,0:T(8,128)S(1)} %broadcast_in_dim.49), channel_id=1, source_target_pairs={{0,1},{1,0},{2,3},{3,2},{4,5},{5,4},{6,7},{7,6},{8,9},{9,8},{10,11... | collective-permute-start | bytes 12296 | tf_op jit(solution)/shard_map/ppermute | solution.py:45
  83.8 42.0 %collective-permute-start.34 = (bf16[1344,576]{0,1:T(8,128)(2,1)}, bf16[1344,576]{0,1:T(8,128)(2,1)}, u32[]{:S(2)}, u32[]{:S(2)}) collective-permute-start(bf16[1344,576]{0,1:T(8,128)(2,1)} %pad_maximum_fusion.1), channel_id=1, source_target_pairs={{0,1},{1,0},{2,3},{3,2},{4,5},{5,4},{6,7},{7,6},{8,9},{9,8},{10,11... | collective-permute-start | bytes 4644872 | tf_op jit(solution)/shard_map/ppermute | solution.py:45
  92.7 16.9 %collective-permute-start.12 = (bf16[192,576]{0,1:T(8,128)(2,1)S(1)}, bf16[192,576]{0,1:T(8,128)(2,1)S(1)}, u32[]{:S(2)}, u32[]{:S(2)}) collective-permute-start(bf16[192,576]{0,1:T(8,128)(2,1)S(1)} %broadcast_select_fusion.6), channel_id=1, source_target_pairs={{0,16},{16,0},{1,17},{17,1},{2,18},{18,2},{3,19},{19,3},{4,20},{20... | collective-permute-start | bytes 663560 | tf_op jit(solution)/shard_map/ppermute | solution.py:68
  94.4 15.7 %collective-permute-start.16 = (bf16[192,576]{0,1:T(8,128)(2,1)S(1)}, bf16[192,576]{0,1:T(8,128)(2,1)S(1)}, u32[]{:S(2)}, u32[]{:S(2)}) collective-permute-start(bf16[192,576]{0,1:T(8,128)(2,1)S(1)} %broadcast_select_fusion.6), channel_id=1, source_target_pairs={{0,2},{1,3},{4,0},{5,1},{8,4},{9,5},{12,8},{13,9},{14,12},{15,13},... | collective-permute-start | bytes 663560 | tf_op jit(solution)/shard_map/ppermute | solution.py:42
  95.9 15.8 %collective-permute-start.15 = (bf16[192,576]{0,1:T(8,128)(2,1)S(1)}, bf16[192,576]{0,1:T(8,128)(2,1)S(1)}, u32[]{:S(2)}, u32[]{:S(2)}) collective-permute-start(bf16[192,576]{0,1:T(8,128)(2,1)S(1)} %broadcast_select_fusion.6), channel_id=1, source_target_pairs={{0,4},{1,5},{4,8},{5,9},{8,12},{9,13},{12,14},{13,15},{14,10},{15,... | collective-permute-start | bytes 663560 | tf_op jit(solution)/shard_map/ppermute | solution.py:39
  110.1 13.6 %collective-permute-start.20 = (bf16[192,576]{0,1:T(8,128)(2,1)S(1)}, bf16[192,576]{0,1:T(8,128)(2,1)}, u32[]{:S(2)}, u32[]{:S(2)}) collective-permute-start(bf16[192,576]{0,1:T(8,128)(2,1)S(1)} %collective-permute-done.16), channel_id=1, source_target_pairs={{0,2},{1,3},{4,0},{5,1},{8,4},{9,5},{12,8},{13,9},{14,12},{15,13},... | collective-permute-start | bytes 663560 | tf_op jit(solution)/shard_map/ppermute | solution.py:42
  111.6 13.5 %collective-permute-start.19 = (bf16[192,576]{0,1:T(8,128)(2,1)S(1)}, bf16[192,576]{0,1:T(8,128)(2,1)}, u32[]{:S(2)}, u32[]{:S(2)}) collective-permute-start(bf16[192,576]{0,1:T(8,128)(2,1)S(1)} %collective-permute-done.15), channel_id=1, source_target_pairs={{0,4},{1,5},{4,8},{5,9},{8,12},{9,13},{12,14},{13,15},{14,10},{15,... | collective-permute-start | bytes 663560 | tf_op jit(solution)/shard_map/ppermute | solution.py:39
  118.1 24.5 %collective-permute-start.13 = (bf16[192,1152]{1,0:T(8,128)(2,1)}, bf16[192,1152]{1,0:T(8,128)(2,1)}, u32[]{:S(2)}, u32[]{:S(2)}) collective-permute-start(bf16[192,1152]{1,0:T(8,128)(2,1)} %copy.63), channel_id=1, source_target_pairs={{0,1},{1,0},{2,3},{3,2},{4,5},{5,4},{6,7},{7,6},{8,9},{9,8},{10,11... | collective-permute-start | bytes 1327112 | tf_op jit(solution)/shard_map/ppermute | solution.py:45
  119.6 27.0 %collective-permute-start.22 = (bf16[192,576]{0,1:T(8,128)(2,1)}, bf16[192,576]{0,1:T(8,128)(2,1)}, u32[]{:S(2)}, u32[]{:S(2)}) collective-permute-start(bf16[192,576]{0,1:T(8,128)(2,1)} %collective-permute-done.18), channel_id=1, source_target_pairs={{0,2},{1,3},{4,0},{5,1},{8,4},{9,5},{12,8},{13,9},{14,12},{15,13},... | collective-permute-start | bytes 663560 | tf_op jit(solution)/shard_map/ppermute | solution.py:42
  123.8 25.2 %collective-permute-start.21 = (bf16[192,576]{0,1:T(8,128)(2,1)}, bf16[192,576]{0,1:T(8,128)(2,1)}, u32[]{:S(2)}, u32[]{:S(2)}) collective-permute-start(bf16[192,576]{0,1:T(8,128)(2,1)} %collective-permute-done.17), channel_id=1, source_target_pairs={{0,4},{1,5},{4,8},{5,9},{8,12},{9,13},{12,14},{13,15},{14,10},{15,... | collective-permute-start | bytes 663560 | tf_op jit(solution)/shard_map/ppermute | solution.py:39
  125.1 13.4 %collective-permute-start.24 = (bf16[192,576]{0,1:T(8,128)(2,1)}, bf16[192,576]{0,1:T(8,128)(2,1)}, u32[]{:S(2)}, u32[]{:S(2)}) collective-permute-start(bf16[192,576]{0,1:T(8,128)(2,1)} %collective-permute-done.20), channel_id=1, source_target_pairs={{0,2},{1,3},{4,0},{5,1},{8,4},{9,5},{12,8},{13,9},{14,12},{15,13},... | collective-permute-start | bytes 663560 | tf_op jit(solution)/shard_map/ppermute | solution.py:42
  125.8 14.5 %collective-permute-start.23 = (bf16[192,576]{0,1:T(8,128)(2,1)}, bf16[192,576]{0,1:T(8,128)(2,1)}, u32[]{:S(2)}, u32[]{:S(2)}) collective-permute-start(bf16[192,576]{0,1:T(8,128)(2,1)} %collective-permute-done.19), channel_id=1, source_target_pairs={{0,4},{1,5},{4,8},{5,9},{8,12},{9,13},{12,14},{13,15},{14,10},{15,... | collective-permute-start | bytes 663560 | tf_op jit(solution)/shard_map/ppermute | solution.py:39
  139.6 27.7 %collective-permute-start.28 = (bf16[96,576]{0,1:T(8,128)(2,1)S(1)}, bf16[96,576]{0,1:T(8,128)(2,1)S(1)}, u32[]{:S(2)}, u32[]{:S(2)}) collective-permute-start(bf16[96,576]{0,1:T(8,128)(2,1)S(1)} %slice.497), channel_id=1, source_target_pairs={{0,2},{1,3},{4,0},{5,1},{8,4},{9,5},{12,8},{13,9},{14,12},{15,13},... | collective-permute-start | bytes 331784 | tf_op jit(solution)/shard_map/ppermute | solution.py:42
  141.2 26.1 %collective-permute-start.27 = (bf16[96,576]{0,1:T(8,128)(2,1)S(1)}, bf16[96,576]{0,1:T(8,128)(2,1)S(1)}, u32[]{:S(2)}, u32[]{:S(2)}) collective-permute-start(bf16[96,576]{0,1:T(8,128)(2,1)S(1)} %slice.496), channel_id=1, source_target_pairs={{0,4},{1,5},{4,8},{5,9},{8,12},{9,13},{12,14},{13,15},{14,10},{15,... | collective-permute-start | bytes 331784 | tf_op jit(solution)/shard_map/ppermute | solution.py:39
  146.7 13.8 %collective-permute-start.26 = (bf16[192,576]{0,1:T(8,128)(2,1)}, bf16[192,576]{0,1:T(8,128)(2,1)S(1)}, u32[]{:S(2)}, u32[]{:S(2)}) collective-permute-start(bf16[192,576]{0,1:T(8,128)(2,1)} %collective-permute-done.22), channel_id=1, source_target_pairs={{0,2},{1,3},{4,0},{5,1},{8,4},{9,5},{12,8},{13,9},{14,12},{15,13},... | collective-permute-start | bytes 663560 | tf_op jit(solution)/shard_map/ppermute | solution.py:42
  149.0 12.4 %collective-permute-start.25 = (bf16[192,576]{0,1:T(8,128)(2,1)}, bf16[192,576]{0,1:T(8,128)(2,1)S(1)}, u32[]{:S(2)}, u32[]{:S(2)}) collective-permute-start(bf16[192,576]{0,1:T(8,128)(2,1)} %collective-permute-done.21), channel_id=1, source_target_pairs={{0,4},{1,5},{4,8},{5,9},{8,12},{9,13},{12,14},{13,15},{14,10},{15,... | collective-permute-start | bytes 663560 | tf_op jit(solution)/shard_map/ppermute | solution.py:39
  203.0 14.1 %collective-permute-start.35 = (bf16[192,1344]{1,0:T(8,128)(2,1)}, bf16[192,1344]{1,0:T(8,128)(2,1)}, u32[]{:S(2)}, u32[]{:S(2)}) collective-permute-start(bf16[192,1344]{1,0:T(8,128)(2,1)} %pad_maximum_fusion.9), channel_id=1, source_target_pairs={{0,16},{16,0},{1,17},{17,1},{2,18},{18,2},{3,19},{19,3},{4,20},{20... | collective-permute-start | bytes 1548296 | tf_op jit(solution)/shard_map/ppermute | solution.py:68
  207.6 11.9 %collective-permute-start.41 = (bf16[72,576]{0,1:T(8,128)(2,1)S(1)}, bf16[72,576]{0,1:T(8,128)(2,1)S(1)}, u32[]{:S(2)}, u32[]{:S(2)}) collective-permute-start(bf16[72,576]{0,1:T(8,128)(2,1)S(1)} %get-tuple-element.62), channel_id=1, source_target_pairs={{0,2},{1,3},{4,0},{5,1},{8,4},{9,5},{12,8},{13,9},{14,12},{15,13},... | collective-permute-start | bytes 248840 | tf_op jit(solution)/shard_map/ppermute | solution.py:42
  209.7 11.7 %collective-permute-start.37 = (bf16[96,576]{0,1:T(8,128)(2,1)S(1)}, bf16[96,576]{0,1:T(8,128)(2,1)S(1)}, u32[]{:S(2)}, u32[]{:S(2)}) collective-permute-start(bf16[96,576]{0,1:T(8,128)(2,1)S(1)} %get-tuple-element.55), channel_id=1, source_target_pairs={{0,4},{1,5},{4,8},{5,9},{8,12},{9,13},{12,14},{13,15},{14,10},{15,... | collective-permute-start | bytes 331784 | tf_op jit(solution)/shard_map/ppermute | solution.py:39
  (53 other events, 413.7 us)

commit v2 on v1

v2 whole, which is shorter than its diff:
```python
import functools

import jax
import jax.numpy as jnp
from jax import lax
from jax.experimental import pallas as pl
from jax.experimental.pallas import tpu as pltpu
from jax.sharding import PartitionSpec as P

sharpness = 10.0
shift = -4.0
multiplier = 262144.0
epsilon = 1e-06

F32, BF16 = jnp.float32, jnp.bfloat16


def dot(a, b, dims):
    return lax.dot_general(a, b, (dims, ((), ())), preferred_element_type=F32)


def nt(a, b):
    return dot(a, b, ((1,), (1,)))


def nn(a, b):
    return dot(a, b, ((1,), (0,)))


def up16(k):
    return -(-k // 16) * 16


def call(body, outs, scalars, arrays, alias=None):
    smem = pl.BlockSpec(memory_space=pltpu.SMEM)
    vmem = pl.BlockSpec(memory_space=pltpu.VMEM)
    return pl.pallas_call(
        body,
        out_shape=[jax.ShapeDtypeStruct(s, t) for s, t in outs],
        in_specs=[smem] * len(scalars) + [vmem] * len(arrays),
        out_specs=[vmem] * len(outs),
        input_output_aliases=alias or {},
        compiler_params=pltpu.CompilerParams(vmem_limit_bytes=48 * 1024 * 1024),
    )(*scalars, *arrays)


class Ring:
    def __init__(self, batch_size):
        n = self.n = batch_size // 2
        half = n // 2
        self.order = [2 * r if r < half else 2 * (n - 1 - r) + 1 for r in range(n)]
        self.fwd = self._perm(1)
        self.bwd = self._perm(-1)
        self.core = [(b, b ^ 1) for b in range(batch_size)]
        chip = lax.axis_index("batch") // 2
        self.pos = jnp.where(chip % 2 == 0, chip // 2, n - 1 - chip // 2)
        place = (self.pos + jnp.arange(n, dtype=jnp.int32)) % n
        self.chips = jnp.where(place < half, 2 * place, 2 * (n - 1 - place) + 1).astype(jnp.int32)

    def _perm(self, step):
        pairs = []
        for r, chip in enumerate(self.order):
            to = self.order[(r + step) % self.n]
            pairs += [(2 * chip + c, 2 * to + c) for c in range(2)]
        return pairs

    def right(self, x):
        return lax.ppermute(x, "batch", self.fwd)

    def left(self, x):
        return lax.ppermute(x, "batch", self.bwd)

    def other_core(self, x):
        return lax.ppermute(x, "batch", self.core)

    def gather(self, x, cut):
        f = b = x
        for _ in range(1, self.n // 2):
            f, b = self.right(f), self.left(b)
            yield f, b
        yield self.right(f[:cut]), self.left(b[cut:])


def swap(x):
    return lax.ppermute(x, "tower", [(0, 1), (1, 0)])


def project(n, rpi, rpt, half, slot_ref, img_ref, txt_ref, *refs):
    chunks, (wi_ref, wt_ref, pi_ref, pt_ref, sq_ref) = refs[:-5], refs[-5:]
    it = iter(chunks)
    h = n // 2
    for sibling in range(2):
        for d in range(n):
            b = slot_ref[sibling, d]
            if d == h:
                wi_ref[b] = next(it)[...]
                wt_ref[b] = next(it)[...]
            else:
                c = next(it)
                wi_ref[b] = c[:rpi]
                wt_ref[b] = c[rpi:]
    pi = nn(img_ref[...], wi_ref[...].reshape(2 * n * rpi, half))
    pt = nn(txt_ref[...], wt_ref[...].reshape(2 * n * rpt, half))
    pi_ref[...] = pi
    pt_ref[...] = pt
    si = jnp.sum(pi * pi, axis=1, keepdims=True)
    st = jnp.sum(pt * pt, axis=1, keepdims=True)
    lane = lax.broadcasted_iota(jnp.int32, (pi.shape[0], 128), 1)
    sq_ref[...] = jnp.where(lane == 0, si, st).T[:8]


def normalize(s_ref, pi_ref, pt_ref, sq_ref, got_ref, mine_ref, other_ref, norm_ref):
    tower, valid = s_ref[0], s_ref[1]
    rows = pi_ref.shape[0]
    sq = sq_ref[...] + got_ref[...]
    norm = jnp.sqrt(sq + epsilon).T
    ni, nt_ = norm[:, 0:1], norm[:, 1:2]
    keep = lax.broadcasted_iota(jnp.int32, (rows, 1), 0) < valid
    u = jnp.where(keep, pi_ref[...] / ni, 0.0)
    v = jnp.where(keep, pt_ref[...] / nt_, 0.0)
    image = tower == 0
    mine_ref[...] = jnp.where(image, u, v).astype(BF16)
    other_ref[...] = jnp.where(image, v, u).astype(BF16)
    norm_ref[...] = jnp.where(image, ni, nt_)


def pairs(chunks, first, *refs):
    half = refs[0].shape[1]
    mine, refs = refs[:4], refs[4:]
    fs, refs = refs[: 2 * chunks], refs[2 * chunks :]
    fo = jnp.concatenate([f[...] for f in fs[:chunks]]) if chunks > 1 else fs[0][...]
    fx = jnp.concatenate([f[...] for f in fs[chunks:]]) if chunks > 1 else fs[1][...]
    ins, outs = (None, refs) if first else (refs[:2], refs[2:])
    for side in range(2):
        mo, mx = mine[2 * side], mine[2 * side + 1]
        s = sharpness * (nt(mo[...], fo) + nt(mx[...], fx)) + shift
        if first and side == 0:
            r = lax.broadcasted_iota(jnp.int32, s.shape, 0)
            c = lax.broadcasted_iota(jnp.int32, s.shape, 1)
            g = jax.nn.sigmoid(jnp.where(r == c, -s, s))
            g = jnp.where(r == c, -g, g)
        else:
            g = jax.nn.sigmoid(s)
        qb = g.astype(BF16)
        for at, f in ((0, fo), (half, fx)):
            part = nn(qb, f)
            cols = slice(at, at + half)
            outs[side][:, cols] = part if first else ins[side][:, cols] + part


def back_norm(s_ref, c_ref, acc_ref, got_ref, mo_ref, mx_ref, norm_ref, do_ref, dx_ref):
    valid, coef = s_ref[1], c_ref[0]
    rows, half = mo_ref.shape
    du = (acc_ref[...] + got_ref[...]) * coef
    duo, dux = du[:, :half], du[:, half:]
    mo, mx = mo_ref[...].astype(F32), mx_ref[...].astype(F32)
    along = jnp.sum(mo * duo, axis=1, keepdims=True) + jnp.sum(mx * dux, axis=1, keepdims=True)
    keep = lax.broadcasted_iota(jnp.int32, (rows, 1), 0) < valid
    norm = norm_ref[...]
    do_ref[...] = jnp.where(keep, (duo - mo * along) / norm, 0.0).astype(BF16)
    dx_ref[...] = jnp.where(keep, (dux - mx * along) / norm, 0.0).astype(BF16)


def products(n, first, s_ref, chip_ref, do_ref, dg_ref, so_ref, sg_ref, ai, bi, at, bt, *outs):
    image = s_ref[0] == 0
    do, dg, so, sg = do_ref[...], dg_ref[...], so_ref[...], sg_ref[...]
    img, img_s = jnp.where(image, do, dg), jnp.where(image, so, sg)
    txt, txt_s = jnp.where(image, dg, do), jnp.where(image, sg, so)
    rpi = ai.shape[1]
    h = n // 2
    for d in [h] if first else [d for d in range(n) if d != h]:
        q = chip_ref[d]
        gi = nn(ai[q], img) + nn(bi[q], img_s)
        gt = nn(at[q], txt) + nn(bt[q], txt_s)
        if first:
            outs[0][...] = gi.astype(BF16)
            outs[1][...] = gt.astype(BF16)
        else:
            outs[0][d, :rpi] = gi
            outs[0][d, rpi:] = gt


def shards(img_feat, txt_feat, img_proj, txt_proj, valid_rows):
    nb = lax.axis_size("batch")
    ring = Ring(nb)
    n, h = ring.n, ring.n // 2
    tower = lax.axis_index("tower")
    core = lax.axis_index("batch") % 2
    rows = img_feat.shape[0]
    ri, half = img_proj.shape
    rt = txt_proj.shape[0]
    rpi, rpt = up16(ri), up16(rt + 1)
    flags = jnp.stack([tower.astype(jnp.int32), valid_rows[0]])

    count_rows = jnp.broadcast_to(valid_rows.astype(BF16)[:, None], (rpt - rt, half))
    pad = jnp.zeros((rpi - ri, half), BF16)
    w = jnp.concatenate([img_proj] + [pad] * (rpi > ri) + [txt_proj, count_rows])
    at = {0: w}
    sib = {0: ring.other_core(w)}
    for k, (f, b) in enumerate(ring.gather(w, rpi), 1):
        if k < h:
            at[n - k], at[k] = f, b
            sib[n - k], sib[k] = ring.other_core(f), ring.other_core(b)
        else:
            at[h], sib[h] = (f, b), (ring.other_core(f), ring.other_core(b))

    def flat(chunks):
        out = []
        for d in range(n):
            out += list(chunks[d]) if d == h else [chunks[d]]
        return out

    def spread(feat, r, rp):
        if rp == r:
            return feat
        f = feat.reshape(rows, nb, r)
        return jnp.pad(f, ((0, 0), (0, 0), (0, rp - r))).reshape(rows, nb * rp)

    slots = jnp.stack([2 * ring.chips + core, 2 * ring.chips + 1 - core]).astype(jnp.int32)
    wi, wt, p_img, p_txt, sq = call(
        functools.partial(project, n, rpi, rpt, half),
        [
            ((nb, rpi, half), BF16),
            ((nb, rpt, half), BF16),
            ((rows, half), F32),
            ((rows, half), F32),
            ((8, rows), F32),
        ],
        [slots],
        [spread(img_feat, ri, rpi), spread(txt_feat, rt, rpt)] + flat(at) + flat(sib),
    )
    mine_o, other_o, norm = call(
        normalize,
        [((rows, half), BF16), ((rows, half), BF16), ((rows, 1), F32)],
        [flags],
        [p_img, p_txt, sq, swap(sq)],
    )

    other_x = swap(mine_o)
    mine_x = swap(other_o)
    mine = [mine_o, mine_x, ring.other_core(mine_o), ring.other_core(mine_x)]
    acc_type = [((rows, 2 * half), F32)] * 2
    acc = call(functools.partial(pairs, 1, True), acc_type, [], mine + [other_o, other_x])
    cut = rows // 2
    for so, sx in zip(ring.gather(other_o, cut), ring.gather(other_x, cut)):
        acc = call(
            functools.partial(pairs, 2, False),
            acc_type,
            [],
            mine + list(so) + list(sx) + list(acc),
            {8: 0, 9: 1},
        )
    count = jnp.sum(wt[:, rt, 0].astype(F32))
    coef = (sharpness * multiplier / count).reshape(1)
    dp_o, dp_x = call(
        back_norm,
        [((rows, half), BF16)] * 2,
        [flags, coef],
        [acc[0], ring.other_core(acc[1]), mine_o, mine_x, norm],
    )
    dp_got = swap(dp_x)
    dps = [dp_o, dp_got, ring.other_core(dp_o), ring.other_core(dp_got)]

    def columns(feat, r, rp):
        t = feat.T.reshape(n, 2, r, rows)
        t = jnp.pad(t, ((0, 0), (0, 0), (0, rp - r), (0, 0)))
        keep = lax.dynamic_index_in_dim(t, core, 1, keepdims=False)
        give = lax.dynamic_index_in_dim(t, 1 - core, 1, keepdims=False)
        return [keep, ring.other_core(give)]

    feats = columns(img_feat, ri, rpi) + columns(txt_feat, rt, rpt)

    def product(first, outs, ds):
        return call(functools.partial(products, n, first), outs, [flags, ring.chips], ds + feats)

    f, b = product(True, [((rpi, half), BF16), ((rpt, half), BF16)], dps)
    dp_o, dp_got, f, b = lax.optimization_barrier((dp_o, dp_got, f, b))
    (g,) = product(False, [((n, rpi + rpt, half), F32)], [dp_o, dp_got] + dps[2:])
    f, b = ring.right(f), ring.left(b)
    for k in range(h - 1, 0, -1):
        pf, pb = g[k], g[n - k]
        if k == h - 1:
            f = jnp.concatenate([pf[:rpi] + f.astype(F32), pf[rpi:]])
            b = jnp.concatenate([pb[:rpi], pb[rpi:] + b.astype(F32)])
        else:
            f, b = pf + f.astype(F32), pb + b.astype(F32)
        f, b = ring.right(f.astype(BF16)), ring.left(b.astype(BF16))
    total = g[0] + f.astype(F32) + b.astype(F32)

    is_image = tower == 0
    dp_img = jnp.where(is_image, dp_o, dp_got)
    dp_txt = jnp.where(is_image, dp_got, dp_o)

    def halves(wm, r):
        wm = wm[:, :r].reshape(nb * r, half)
        m = nb * r // 2
        keep = lax.dynamic_slice_in_dim(wm, tower * m, m, 0)
        give = lax.dynamic_slice_in_dim(wm, (1 - tower) * m, m, 0)
        return keep, give

    (ki, gi), (kt, gt) = halves(wi, ri), halves(wt, rt)
    img_got = swap(nt(dp_img, gi).astype(BF16)).astype(F32)
    txt_got = swap(nt(dp_txt, gt).astype(BF16)).astype(F32)
    img_grad = nt(dp_img, ki) + img_got
    txt_grad = nt(dp_txt, kt) + txt_got
    return (img_grad.astype(BF16), txt_grad.astype(BF16), total[:ri], total[rpi : rpi + rt])


def solution(mesh):
    in_specs = (
        P("batch", None),
        P("batch", None),
        P("batch", "tower"),
        P("batch", "tower"),
        P("batch"),
    )
    out_specs = (P("batch", "tower"),) * 4
    return jax.shard_map(shards, mesh=mesh, in_specs=in_specs, out_specs=out_specs, check_vma=False)
```

time: 248 us -> 146 us (0.59)
  local copies, waits for them, and re-layouts: 93.5 us -> 15.6 us
  other arithmetic: 26.1 us -> 3.12 us
  matrix products: 23.9 us -> 3.2 us
  Pallas kernels: 0 us -> 19 us
  starting transfers between devices: 40.8 us -> 46.6 us
  between operations: 7.5 us -> 2.4 us
    unnamed x129 -> x13, local copies, waits for them, and re-layouts: 52.9 us -> 5.29 us
    ppermute x16, waiting for transfers between devices: 4.21 us -> 36.6 us  [right(): return lax.ppermute(x, 'batch', self.fwd)]
    dot_general x28 -> x4, matrix products: 23.9 us -> 3.2 us  [dot(): return lax.dot_general(a, b, (dims, ((), ())), preferred_element_type=F32)]
    pallas_call x0 -> x10, Pallas kernels: none -> 19 us  [call(): pl.pallas_call(body, out_shape=[jax.ShapeDtypeStruct(s, t) for s, t in ou...]
    ppermute x5 -> x6, waiting for transfers between devices: 24 us -> 5.77 us  [swap(): return lax.ppermute(x, 'tower', [(0, 1), (1, 0)])]
    slice x26 -> x10, local copies, waits for them, and re-layouts: 16.8 us -> 2.28 us  [the longest x1 1.51 us: halves(): wm = wm[:, :r].reshape(nb * r, half)]
    ppermute x16, waiting for transfers between devices: 25.8 us -> 12.2 us  [left(): return lax.ppermute(x, 'batch', self.bwd)]
    ppermute x16, starting transfers between devices: 22.5 us -> 10.2 us  [left(): return lax.ppermute(x, 'batch', self.bwd)]
  transfers between devices with their start and end apart: 45 -> 54, of which waited for: 16 -> 20; matrix products, arithmetic and copies ran while one was open for 49% -> 13% of each run, Pallas kernels for 0% -> 6%
where the time goes in v2:
time: 146 us
  waiting for transfers between devices  55.5 us (38%)
  starting transfers between devices  46.6 us (32%)
  Pallas kernels  19 us (13%)
  local copies, waits for them, and re-layouts  15.6 us (11%)
  matrix products  3.2 us (2%)
  other arithmetic  3.12 us (2%)
  between operations  2.4 us (2%)
    ppermute x16, waiting for transfers between devices, right(): return lax.ppermute(x, 'batch', self.fwd)  36.6 us
    ppermute x16, starting transfers between devices, right(): return lax.ppermute(x, 'batch', self.fwd)  25.1 us
    pallas_call x10, Pallas kernels, call(): pl.pallas_call(body, out_shape=[jax.ShapeDtypeStruct(s, t) for s, t in ou...  19 us
    ppermute x16, waiting for transfers between devices, left(): return lax.ppermute(x, 'batch', self.bwd)  12.2 us
    ppermute x16, starting transfers between devices, left(): return lax.ppermute(x, 'batch', self.bwd)  10.2 us
    ppermute x6, starting transfers between devices, swap(): return lax.ppermute(x, 'tower', [(0, 1), (1, 0)])  8.26 us
    ppermute x6, waiting for transfers between devices, swap(): return lax.ppermute(x, 'tower', [(0, 1), (1, 0)])  5.77 us
    unnamed x13, local copies, waits for them, and re-layouts  5.29 us
  transfers between devices with their start and end apart: 54, of which 20 were waited for; matrix products, arithmetic and copies ran while one was open for 13% of the time, Pallas kernels for 6%

profile of v2, /device:TPU:0, one launch (start us, length us, event | category | flops | bytes accessed | tf_op | source)
XLA Modules:
  0.0 145.5 jit_solution(11687234741126316862)
XLA Ops:
  2.4 3.1 %collective-permute-start.3 = (bf16[176,576]{1,0:T(8,128)(2,1)S(1)}, bf16[176,576]{1,0:T(8,128)(2,1)S(1)}, u32[]{:S(2)}, u32[]{:S(2)}) collective-permute-start(bf16[176,576]{1,0:T(8,128)(2,1)S(1)} %maximum_maximum_fusion.refs_0_), channel_id=1, source_target_pairs={{0,4},{1,5},{4,8},{5,9},{8,12},{9,13},{12,14},{13,15},{14,10},{15,... | collective-permute-start | bytes 608264 | tf_op jit(solution)/shard_map/ppermute | solution.py:68
  5.5 5.4 %collective-permute-done.3.refs_8_ = bf16[176,576]{1,0:T(8,128)(2,1)S(1)} collective-permute-done((bf16[176,576]{1,0:T(8,128)(2,1)S(1)}, bf16[176,576]{1,0:T(8,128)(2,1)S(1)}, u32[]{:S(2)}, u32[]{:S(2)}) %collective-permute-start.3) | collective-permute-done | bytes 202784 | tf_op jit(solution)/shard_map/ppermute | solution.py:68
  13.0 4.7 %collective-permute-done.4.refs_7_ = bf16[176,576]{1,0:T(8,128)(2,1)S(1)} collective-permute-done((bf16[176,576]{1,0:T(8,128)(2,1)S(1)}, bf16[176,576]{1,0:T(8,128)(2,1)S(1)}, u32[]{:S(2)}, u32[]{:S(2)}) %collective-permute-start.4) | collective-permute-done | bytes 202784 | tf_op jit(solution)/shard_map/ppermute | solution.py:68
  20.2 3.4 %collective-permute-done.5.refs_6_ = bf16[176,576]{1,0:T(8,128)(2,1)S(1)} collective-permute-done((bf16[176,576]{1,0:T(8,128)(2,1)S(1)}, bf16[176,576]{1,0:T(8,128)(2,1)S(1)}, u32[]{:S(2)}, u32[]{:S(2)}) %collective-permute-start.5) | collective-permute-done | bytes 202784 | tf_op jit(solution)/shard_map/ppermute | solution.py:68
  30.6 3.6 %collective-permute-done.7.refs_5_ = bf16[80,576]{1,0:T(8,128)(2,1)S(1)} collective-permute-done((bf16[80,576]{1,0:T(8,128)(2,1)S(1)}, bf16[80,576]{1,0:T(8,128)(2,1)S(1)}, u32[]{:S(2)}, u32[]{:S(2)}) %collective-permute-start.7) | collective-permute-done | bytes 92192 | tf_op jit(solution)/shard_map/ppermute | solution.py:71
  35.7 3.6 %shard_map.84 = (bf16[16,96,576]{2,1,0:T(8,128)(2,1)}, bf16[16,80,576]{2,1,0:T(8,128)(2,1)}, f32[192,576]{1,0:T(8,128)S(1)}, f32[192,576]{1,0:T(8,128)S(1)}, f32[8,192]{1,0:T(8,128)S(1)}) custom-call(s32[2,8]{1,0:T(2,128)S(1)} %pad_add_fusion.slot_ref, bf16[192,1536]{1,0:T(8,128)(2,1)S(1)} %copy-done, bf16[192,1280]{1,0:T(8,128)(2,1)S(1)} %copy.21.txt_ref, ...), custom_call_target="tpu_custom_call" | custom-call | tf_op jit(solution)/shard_map/pallas_call | solution.py:37
  40.9 2.0 %collective-permute-done.17.got_ref = f32[8,192]{1,0:T(8,128)S(1)} collective-permute-done((f32[8,192]{1,0:T(8,128)S(1)}, f32[8,192]{1,0:T(8,128)S(1)}, u32[]{:S(2)}, u32[]{:S(2)}) %collective-permute-start.17) | collective-permute-done | bytes 6176 | tf_op jit(solution)/shard_map/ppermute | solution.py:85
  47.4 3.5 %collective-permute-done.29.refs_5_ = bf16[192,576]{1,0:T(8,128)(2,1)S(1)} collective-permute-done((bf16[192,576]{1,0:T(8,128)(2,1)S(1)}, bf16[192,576]{1,0:T(8,128)(2,1)S(1)}, u32[]{:S(2)}, u32[]{:S(2)}) %collective-permute-start.29) | collective-permute-done | bytes 221216 | tf_op jit(solution)/shard_map/ppermute | solution.py:85
  55.0 4.8 %collective-permute-done.30.refs_6_ = bf16[192,576]{1,0:T(8,128)(2,1)S(1)} collective-permute-done((bf16[192,576]{1,0:T(8,128)(2,1)S(1)}, bf16[192,576]{1,0:T(8,128)(2,1)S(1)}, u32[]{:S(2)}, u32[]{:S(2)}) %collective-permute-start.30) | collective-permute-done | bytes 221216 | tf_op jit(solution)/shard_map/ppermute | solution.py:68
  67.1 3.2 %collective-permute-done.31.refs_6_ = bf16[192,576]{1,0:T(8,128)(2,1)S(1)} collective-permute-done((bf16[192,576]{1,0:T(8,128)(2,1)S(1)}, bf16[192,576]{1,0:T(8,128)(2,1)S(1)}, u32[]{:S(2)}, u32[]{:S(2)}) %collective-permute-start.31) | collective-permute-done | bytes 221216 | tf_op jit(solution)/shard_map/ppermute | solution.py:68
  72.4 3.2 %collective-permute-done.23.refs_4_ = bf16[192,576]{1,0:T(8,128)(2,1)S(1)} collective-permute-done((bf16[192,576]{1,0:T(8,128)(2,1)S(1)}, bf16[192,576]{1,0:T(8,128)(2,1)S(1)}, u32[]{:S(2)}, u32[]{:S(2)}) %collective-permute-start.23) | collective-permute-done | bytes 221216 | tf_op jit(solution)/shard_map/ppermute | solution.py:68
  83.7 2.2 %shard_map.87 = (f32[192,1152]{1,0:T(8,128)S(1)}, f32[192,1152]{1,0:T(8,128)S(1)}) custom-call(bf16[192,576]{1,0:T(8,128)(2,1)S(1)} %get-tuple-element.34.refs_0_.mo_ref, bf16[192,576]{1,0:T(8,128)(2,1)S(1)} %collective-permute-done.18.refs_1_.mx_ref, ...), custom_call_target="tpu_custom_call", output_to_operand_aliasing={{0}: (8, {}), {1}: (9, {})} | custom-call | tf_op jit(solution)/shard_map/pallas_call | solution.py:37
  85.9 2.2 %shard_map.88 = (f32[192,1152]{1,0:T(8,128)S(1)}, f32[192,1152]{1,0:T(8,128)S(1)}) custom-call(bf16[192,576]{1,0:T(8,128)(2,1)S(1)} %get-tuple-element.34.refs_0_.mo_ref, bf16[192,576]{1,0:T(8,128)(2,1)S(1)} %collective-permute-done.18.refs_1_.mx_ref, ...), custom_call_target="tpu_custom_call", output_to_operand_aliasing={{0}: (8, {}), {1}: (9, {})} | custom-call | tf_op jit(solution)/shard_map/pallas_call | solution.py:37
  88.1 2.2 %shard_map.89 = (f32[192,1152]{1,0:T(8,128)S(1)}, f32[192,1152]{1,0:T(8,128)S(1)}) custom-call(bf16[192,576]{1,0:T(8,128)(2,1)S(1)} %get-tuple-element.34.refs_0_.mo_ref, bf16[192,576]{1,0:T(8,128)(2,1)S(1)} %collective-permute-done.18.refs_1_.mx_ref, ...), custom_call_target="tpu_custom_call", output_to_operand_aliasing={{0}: (8, {}), {1}: (9, {})} | custom-call | tf_op jit(solution)/shard_map/pallas_call | solution.py:37
  90.3 1.8 %shard_map.90 = (f32[192,1152]{1,0:T(8,128)S(1)}, f32[192,1152]{1,0:T(8,128)S(1)}) custom-call(bf16[192,576]{1,0:T(8,128)(2,1)S(1)} %get-tuple-element.34.refs_0_.mo_ref, bf16[192,576]{1,0:T(8,128)(2,1)S(1)} %collective-permute-done.18.refs_1_.mx_ref, ...), custom_call_target="tpu_custom_call", output_to_operand_aliasing={{0}: (8, {}), {1}: (9, {})} | custom-call | tf_op jit(solution)/shard_map/pallas_call | solution.py:37
  95.9 1.9 %shard_map.91 = (bf16[192,576]{1,0:T(8,128)(2,1)S(1)}, bf16[192,576]{1,0:T(8,128)(2,1)S(1)}) custom-call(s32[2]{0:T(128)S(1)} %pad_add_fusion.1.s_ref, f32[1]{0:T(128)} %bitcast.4.c_ref, f32[192,1152]{1,0:T(8,128)S(1)} %get-tuple-element.44.acc_ref, f32[192,1152]{1,0:T(8,128)} %collective-permute-done.38.got_ref, ...), custom_call_target="tpu_custom_call" | custom-call | tf_op jit(solution)/shard_map/pallas_call | solution.py:37
  99.0 2.5 %constant_dynamic-slice_fusion = (bf16[8,1,96,192]{2,1,0,3:T(2,128)(2,1)}, bf16[8,1,96,192]{2,1,0,3:T(2,128)(2,1)S(1)}) fusion(bf16[8,2,96,192]{2,1,0,3:T(2,128)(2,1)S(1)} %copy-done.1, s32[]{:T(128)S(6)} %select_n.92, s32[]{:T(128)S(6)} %select_n.91), kind=kLoop, calls=%fused_computation.51 | loop fusion | bytes 1179656 | tf_op jit(solution)/shard_map/jit(dynamic_index_in_dim)/dynamic_slice | solution.py:268
  101.5 2.9 %copy.26 = bf16[8,1,96,192]{3,2,0,1:T(8,128)(2,1)} copy(bf16[8,1,96,192]{2,1,0,3:T(2,128)(2,1)} %get-tuple-element.58) | data formatting | bytes 589824
  115.5 2.5 %collective-permute-done.46 = bf16[96,576]{1,0:T(8,128)(2,1)S(1)} collective-permute-done((bf16[96,576]{1,0:T(8,128)(2,1)S(1)}, bf16[96,576]{1,0:T(8,128)(2,1)S(1)}, u32[]{:S(2)}, u32[]{:S(2)}) %collective-permute-start.46) | collective-permute-done | bytes 110624 | tf_op jit(solution)/shard_map/ppermute | solution.py:68
  120.3 4.6 %collective-permute-done.47 = bf16[176,576]{1,0:T(8,128)(2,1)S(1)} collective-permute-done((bf16[176,576]{1,0:T(8,128)(2,1)S(1)}, bf16[176,576]{1,0:T(8,128)(2,1)S(1)}, u32[]{:S(2)}, u32[]{:S(2)}) %collective-permute-start.47) | collective-permute-done | bytes 202784 | tf_op jit(solution)/shard_map/ppermute | solution.py:68
  128.1 2.9 %collective-permute-done.48 = bf16[176,576]{1,0:T(8,128)(2,1)S(1)} collective-permute-done((bf16[176,576]{1,0:T(8,128)(2,1)S(1)}, bf16[176,576]{1,0:T(8,128)(2,1)S(1)}, u32[]{:S(2)}, u32[]{:S(2)}) %collective-permute-start.48) | collective-permute-done | bytes 202784 | tf_op jit(solution)/shard_map/ppermute | solution.py:68
  134.3 3.7 %collective-permute-done.52 = bf16[176,576]{1,0:T(8,128)(2,1)S(1)} collective-permute-done((bf16[176,576]{1,0:T(8,128)(2,1)S(1)}, bf16[176,576]{1,0:T(8,128)(2,1)S(1)}, u32[]{:S(2)}, u32[]{:S(2)}) %collective-permute-start.52) | collective-permute-done | bytes 202784 | tf_op jit(solution)/shard_map/ppermute | solution.py:71
  138.0 2.0 %collective-permute-start.53 = (bf16[176,576]{1,0:T(8,128)(2,1)S(1)}, bf16[176,576]{1,0:T(8,128)(2,1)S(1)}, u32[]{:S(2)}, u32[]{:S(2)}) collective-permute-start(bf16[176,576]{1,0:T(8,128)(2,1)S(1)} %fusion.9), channel_id=1, source_target_pairs={{0,2},{1,3},{4,0},{5,1},{8,4},{9,5},{12,8},{13,9},{14,12},{15,13},... | collective-permute-start | bytes 608264 | tf_op jit(solution)/shard_map/ppermute | solution.py:71
  141.2 2.9 %collective-permute-done.53 = bf16[176,576]{1,0:T(8,128)(2,1)S(1)} collective-permute-done((bf16[176,576]{1,0:T(8,128)(2,1)S(1)}, bf16[176,576]{1,0:T(8,128)(2,1)S(1)}, u32[]{:S(2)}, u32[]{:S(2)}) %collective-permute-start.53) | collective-permute-done | bytes 202784 | tf_op jit(solution)/shard_map/ppermute | solution.py:71
  (144 shorter events, 68.3 us)
Async XLA Ops:
  2.4 8.5 %collective-permute-start.3 = (bf16[176,576]{1,0:T(8,128)(2,1)S(1)}, bf16[176,576]{1,0:T(8,128)(2,1)S(1)}, u32[]{:S(2)}, u32[]{:S(2)}) collective-permute-start(bf16[176,576]{1,0:T(8,128)(2,1)S(1)} %maximum_maximum_fusion.refs_0_), channel_id=1, source_target_pairs={{0,4},{1,5},{4,8},{5,9},{8,12},{9,13},{12,14},{13,15},{14,10},{15,... | collective-permute-start | bytes 608264 | tf_op jit(solution)/shard_map/ppermute | solution.py:68
  19.1 8.2 %collective-permute-start.2 = (bf16[176,576]{1,0:T(8,128)(2,1)S(1)}, bf16[176,576]{1,0:T(8,128)(2,1)S(1)}, u32[]{:S(2)}, u32[]{:S(2)}) collective-permute-start(bf16[176,576]{1,0:T(8,128)(2,1)S(1)} %collective-permute-done.1.refs_2_), channel_id=1, source_target_pairs={{0,2},{1,3},{4,0},{5,1},{8,4},{9,5},{12,8},{13,9},{14,12},{15,13},... | collective-permute-start | bytes 608264 | tf_op jit(solution)/shard_map/ppermute | solution.py:71
  19.7 8.3 %collective-permute-start.8 = (bf16[176,576]{1,0:T(8,128)(2,1)S(1)}, bf16[176,576]{1,0:T(8,128)(2,1)S(1)}, u32[]{:S(2)}, u32[]{:S(2)}) collective-permute-start(bf16[176,576]{1,0:T(8,128)(2,1)S(1)} %maximum_maximum_fusion.refs_0_), channel_id=1, source_target_pairs={{0,1},{1,0},{2,3},{3,2},{4,5},{5,4},{6,7},{7,6},{8,9},{9,8},{10,11... | collective-permute-start | bytes 608264 | tf_op jit(solution)/shard_map/ppermute | solution.py:74
  19.7 9.9 %collective-permute-start.16 = (bf16[176,576]{1,0:T(8,128)(2,1)S(1)}, bf16[176,576]{1,0:T(8,128)(2,1)S(1)}, u32[]{:S(2)}, u32[]{:S(2)}) collective-permute-start(bf16[176,576]{1,0:T(8,128)(2,1)S(1)} %collective-permute-done.3.refs_8_), channel_id=1, source_target_pairs={{0,1},{1,0},{2,3},{3,2},{4,5},{5,4},{6,7},{7,6},{8,9},{9,8},{10,11... | collective-permute-start | bytes 608264 | tf_op jit(solution)/shard_map/ppermute | solution.py:74
  20.2 9.9 %collective-permute-start.9 = (bf16[176,576]{1,0:T(8,128)(2,1)S(1)}, bf16[176,576]{1,0:T(8,128)(2,1)S(1)}, u32[]{:S(2)}, u32[]{:S(2)}) collective-permute-start(bf16[176,576]{1,0:T(8,128)(2,1)S(1)} %collective-permute-done.refs_1_), channel_id=1, source_target_pairs={{0,1},{1,0},{2,3},{3,2},{4,5},{5,4},{6,7},{7,6},{8,9},{9,8},{10,11... | collective-permute-start | bytes 608264 | tf_op jit(solution)/shard_map/ppermute | solution.py:74
  50.9 8.9 %collective-permute-start.30 = (bf16[192,576]{1,0:T(8,128)(2,1)S(1)}, bf16[192,576]{1,0:T(8,128)(2,1)S(1)}, u32[]{:S(2)}, u32[]{:S(2)}) collective-permute-start(bf16[192,576]{1,0:T(8,128)(2,1)S(1)} %collective-permute-done.29.refs_5_), channel_id=1, source_target_pairs={{0,4},{1,5},{4,8},{5,9},{8,12},{9,13},{12,14},{13,15},{14,10},{15,... | collective-permute-start | bytes 663560 | tf_op jit(solution)/shard_map/ppermute | solution.py:68
  52.5 8.9 %collective-permute-start.34 = (bf16[192,576]{1,0:T(8,128)(2,1)S(1)}, bf16[192,576]{1,0:T(8,128)(2,1)S(1)}, u32[]{:S(2)}, u32[]{:S(2)}) collective-permute-start(bf16[192,576]{1,0:T(8,128)(2,1)S(1)} %collective-permute-done.29.refs_5_), channel_id=1, source_target_pairs={{0,2},{1,3},{4,0},{5,1},{8,4},{9,5},{12,8},{13,9},{14,12},{15,13},... | collective-permute-start | bytes 663560 | tf_op jit(solution)/shard_map/ppermute | solution.py:71
  52.9 12.1 %collective-permute-start.22 = (bf16[192,576]{1,0:T(8,128)(2,1)S(1)}, bf16[192,576]{1,0:T(8,128)(2,1)S(1)}, u32[]{:S(2)}, u32[]{:S(2)}) collective-permute-start(bf16[192,576]{1,0:T(8,128)(2,1)S(1)} %collective-permute-done.21.refs_4_), channel_id=1, source_target_pairs={{0,4},{1,5},{4,8},{5,9},{8,12},{9,13},{12,14},{13,15},{14,10},{15,... | collective-permute-start | bytes 663560 | tf_op jit(solution)/shard_map/ppermute | solution.py:68
  54.5 12.1 %collective-permute-start.26 = (bf16[192,576]{1,0:T(8,128)(2,1)S(1)}, bf16[192,576]{1,0:T(8,128)(2,1)S(1)}, u32[]{:S(2)}, u32[]{:S(2)}) collective-permute-start(bf16[192,576]{1,0:T(8,128)(2,1)S(1)} %collective-permute-done.25.refs_5_), channel_id=1, source_target_pairs={{0,2},{1,3},{4,0},{5,1},{8,4},{9,5},{12,8},{13,9},{14,12},{15,13},... | collective-permute-start | bytes 663560 | tf_op jit(solution)/shard_map/ppermute | solution.py:71
  59.8 10.5 %collective-permute-start.31 = (bf16[192,576]{1,0:T(8,128)(2,1)S(1)}, bf16[192,576]{1,0:T(8,128)(2,1)S(1)}, u32[]{:S(2)}, u32[]{:S(2)}) collective-permute-start(bf16[192,576]{1,0:T(8,128)(2,1)S(1)} %collective-permute-done.30.refs_6_), channel_id=1, source_target_pairs={{0,4},{1,5},{4,8},{5,9},{8,12},{9,13},{12,14},{13,15},{14,10},{15,... | collective-permute-start | bytes 663560 | tf_op jit(solution)/shard_map/ppermute | solution.py:68
  61.4 10.5 %collective-permute-start.35 = (bf16[192,576]{1,0:T(8,128)(2,1)S(1)}, bf16[192,576]{1,0:T(8,128)(2,1)S(1)}, u32[]{:S(2)}, u32[]{:S(2)}) collective-permute-start(bf16[192,576]{1,0:T(8,128)(2,1)S(1)} %collective-permute-done.34.refs_7_), channel_id=1, source_target_pairs={{0,2},{1,3},{4,0},{5,1},{8,4},{9,5},{12,8},{13,9},{14,12},{15,13},... | collective-permute-start | bytes 663560 | tf_op jit(solution)/shard_map/ppermute | solution.py:71
  61.8 10.5 %collective-permute-start.18 = (bf16[192,576]{1,0:T(8,128)(2,1)S(1)}, bf16[192,576]{1,0:T(8,128)(2,1)S(1)}, u32[]{:S(2)}, u32[]{:S(2)}) collective-permute-start(bf16[192,576]{1,0:T(8,128)(2,1)S(1)} %get-tuple-element.35.refs_4_), channel_id=1, source_target_pairs={{0,16},{16,0},{1,17},{17,1},{2,18},{18,2},{3,19},{19,3},{4,20},{20... | collective-permute-start | bytes 663560 | tf_op jit(solution)/shard_map/ppermute | solution.py:85
  65.1 10.5 %collective-permute-start.23 = (bf16[192,576]{1,0:T(8,128)(2,1)S(1)}, bf16[192,576]{1,0:T(8,128)(2,1)S(1)}, u32[]{:S(2)}, u32[]{:S(2)}) collective-permute-start(bf16[192,576]{1,0:T(8,128)(2,1)S(1)} %collective-permute-done.22.refs_4_), channel_id=1, source_target_pairs={{0,4},{1,5},{4,8},{5,9},{8,12},{9,13},{12,14},{13,15},{14,10},{15,... | collective-permute-start | bytes 663560 | tf_op jit(solution)/shard_map/ppermute | solution.py:68
  66.7 10.5 %collective-permute-start.27 = (bf16[192,576]{1,0:T(8,128)(2,1)S(1)}, bf16[192,576]{1,0:T(8,128)(2,1)S(1)}, u32[]{:S(2)}, u32[]{:S(2)}) collective-permute-start(bf16[192,576]{1,0:T(8,128)(2,1)S(1)} %collective-permute-done.26.refs_5_), channel_id=1, source_target_pairs={{0,2},{1,3},{4,0},{5,1},{8,4},{9,5},{12,8},{13,9},{14,12},{15,13},... | collective-permute-start | bytes 663560 | tf_op jit(solution)/shard_map/ppermute | solution.py:71
  70.3 8.4 %collective-permute-start.32 = (bf16[192,576]{1,0:T(8,128)(2,1)S(1)}, bf16[192,576]{1,0:T(8,128)(2,1)S(1)}, u32[]{:S(2)}, u32[]{:S(2)}) collective-permute-start(bf16[192,576]{1,0:T(8,128)(2,1)S(1)} %collective-permute-done.31.refs_6_), channel_id=1, source_target_pairs={{0,4},{1,5},{4,8},{5,9},{8,12},{9,13},{12,14},{13,15},{14,10},{15,... | collective-permute-start | bytes 663560 | tf_op jit(solution)/shard_map/ppermute | solution.py:68
  72.4 9.0 %collective-permute-start.19 = (bf16[192,576]{1,0:T(8,128)(2,1)S(1)}, bf16[192,576]{1,0:T(8,128)(2,1)S(1)}, u32[]{:S(2)}, u32[]{:S(2)}) collective-permute-start(bf16[192,576]{1,0:T(8,128)(2,1)S(1)} %get-tuple-element.34.refs_0_.mo_ref), channel_id=1, source_target_pairs={{0,1},{1,0},{2,3},{3,2},{4,5},{5,4},{6,7},{7,6},{8,9},{9,8},{10,11... | collective-permute-start | bytes 663560 | tf_op jit(solution)/shard_map/ppermute | solution.py:74
  77.2 13.1 %collective-permute-start.24 = (bf16[96,576]{1,0:T(8,128)(2,1)S(1)}, bf16[96,576]{1,0:T(8,128)(2,1)S(1)}, u32[]{:S(2)}, u32[]{:S(2)}) collective-permute-start(bf16[96,576]{1,0:T(8,128)(2,1)S(1)} %slice.102), channel_id=1, source_target_pairs={{0,4},{1,5},{4,8},{5,9},{8,12},{9,13},{12,14},{13,15},{14,10},{15,... | collective-permute-start | bytes 331784 | tf_op jit(solution)/shard_map/ppermute | solution.py:68
  78.7 11.5 %collective-permute-start.28 = (bf16[96,576]{1,0:T(8,128)(2,1)S(1)}, bf16[96,576]{1,0:T(8,128)(2,1)S(1)}, u32[]{:S(2)}, u32[]{:S(2)}) collective-permute-start(bf16[96,576]{1,0:T(8,128)(2,1)S(1)} %slice.103), channel_id=1, source_target_pairs={{0,2},{1,3},{4,0},{5,1},{8,4},{9,5},{12,8},{13,9},{14,12},{15,13},... | collective-permute-start | bytes 331784 | tf_op jit(solution)/shard_map/ppermute | solution.py:71
  79.8 10.5 %collective-permute-start.33 = (bf16[96,576]{1,0:T(8,128)(2,1)S(1)}, bf16[96,576]{1,0:T(8,128)(2,1)S(1)}, u32[]{:S(2)}, u32[]{:S(2)}) collective-permute-start(bf16[96,576]{1,0:T(8,128)(2,1)S(1)} %slice.104), channel_id=1, source_target_pairs={{0,4},{1,5},{4,8},{5,9},{8,12},{9,13},{12,14},{13,15},{14,10},{15,... | collective-permute-start | bytes 331784 | tf_op jit(solution)/shard_map/ppermute | solution.py:68
  81.4 8.9 %collective-permute-start.37 = (bf16[96,576]{1,0:T(8,128)(2,1)S(1)}, bf16[96,576]{1,0:T(8,128)(2,1)S(1)}, u32[]{:S(2)}, u32[]{:S(2)}) collective-permute-start(bf16[96,576]{1,0:T(8,128)(2,1)S(1)} %slice.105), channel_id=1, source_target_pairs={{0,2},{1,3},{4,0},{5,1},{8,4},{9,5},{12,8},{13,9},{14,12},{15,13},... | collective-permute-start | bytes 331784 | tf_op jit(solution)/shard_map/ppermute | solution.py:71
  97.8 8.4 %collective-permute-start.39 = (bf16[192,576]{1,0:T(8,128)(2,1)S(1)}, bf16[192,576]{1,0:T(8,128)(2,1)S(1)}, u32[]{:S(2)}, u32[]{:S(2)}) collective-permute-start(bf16[192,576]{1,0:T(8,128)(2,1)S(1)} %get-tuple-element.48), channel_id=1, source_target_pairs={{0,16},{16,0},{1,17},{17,1},{2,18},{18,2},{3,19},{19,3},{4,20},{20... | collective-permute-start | bytes 663560 | tf_op jit(solution)/shard_map/ppermute | solution.py:85
  114.4 18.3 %collective-permute-start.45 = (bf16[192,576]{1,0:T(8,128)(2,1)S(1)}, bf16[192,576]{1,0:T(8,128)(2,1)S(1)}, u32[]{:S(2)}, u32[]{:S(2)}) collective-permute-start(bf16[192,576]{1,0:T(8,128)(2,1)S(1)} %convolution_convert_fusion.1), channel_id=1, source_target_pairs={{0,16},{16,0},{1,17},{17,1},{2,18},{18,2},{3,19},{19,3},{4,20},{20... | collective-permute-start | bytes 663560 | tf_op jit(solution)/shard_map/ppermute | solution.py:85
  119.5 8.6 %collective-permute-start.51 = (bf16[176,576]{1,0:T(8,128)(2,1)S(1)}, bf16[176,576]{1,0:T(8,128)(2,1)S(1)}, u32[]{:S(2)}, u32[]{:S(2)}) collective-permute-start(bf16[176,576]{1,0:T(8,128)(2,1)S(1)} %pad_maximum_fusion.1), channel_id=1, source_target_pairs={{0,2},{1,3},{4,0},{5,1},{8,4},{9,5},{12,8},{13,9},{14,12},{15,13},... | collective-permute-start | bytes 608264 | tf_op jit(solution)/shard_map/ppermute | solution.py:71
  126.8 13.2 %collective-permute-start.44 = (bf16[192,768]{1,0:T(8,128)(2,1)S(1)}, bf16[192,768]{1,0:T(8,128)(2,1)S(1)}, u32[]{:S(2)}, u32[]{:S(2)}) collective-permute-start(bf16[192,768]{1,0:T(8,128)(2,1)S(1)} %convolution_convert_fusion), channel_id=1, source_target_pairs={{0,16},{16,0},{1,17},{17,1},{2,18},{18,2},{3,19},{19,3},{4,20},{20... | collective-permute-start | bytes 884744 | tf_op jit(solution)/shard_map/ppermute | solution.py:85
  (35 other events, 203.9 us)

commit v3 on v2

--- a/solution.py
+++ b/solution.py
@@ -31,7 +31,7 @@
     return -(-k // 16) * 16
 
 
-def call(body, outs, scalars, arrays, alias=None):
+def call(body, outs, scalars, arrays, us, alias=None):
     smem = pl.BlockSpec(memory_space=pltpu.SMEM)
     vmem = pl.BlockSpec(memory_space=pltpu.VMEM)
     return pl.pallas_call(
@@ -40,8 +40,17 @@
         in_specs=[smem] * len(scalars) + [vmem] * len(arrays),
         out_specs=[vmem] * len(outs),
         input_output_aliases=alias or {},
+        cost_estimate=pl.CostEstimate(
+            flops=int(us * 2e8),
+            transcendentals=0,
+            bytes_accessed=sum(a.size * a.dtype.itemsize for a in arrays),
+        ),
         compiler_params=pltpu.CompilerParams(vmem_limit_bytes=48 * 1024 * 1024),
     )(*scalars, *arrays)
+
+
+def tie(xs):
+    return lax.optimization_barrier(xs)
 
 
 class Ring:
@@ -73,20 +82,57 @@
     def other_core(self, x):
         return lax.ppermute(x, "batch", self.core)
 
-    def gather(self, x, cut):
-        f = b = x
-        for _ in range(1, self.n // 2):
-            f, b = self.right(f), self.left(b)
-            yield f, b
-        yield self.right(f[:cut]), self.left(b[cut:])
-
 
 def swap(x):
     return lax.ppermute(x, "tower", [(0, 1), (1, 0)])
 
 
-def project(n, rpi, rpt, half, slot_ref, img_ref, txt_ref, *refs):
-    chunks, (wi_ref, wt_ref, pi_ref, pt_ref, sq_ref) = refs[:-5], refs[-5:]
+def prepare(nb, ri, rt, rpi, rpt, core_ref, img_ref, txt_ref, ki_ref, gi_ref, kt_ref, gt_ref, *wide):
+    first = core_ref[0] == 0
+    rows = img_ref.shape[0]
+    for feat, r, rp, keep, give in (
+        (img_ref, ri, rpi, ki_ref, gi_ref),
+        (txt_ref, rt, rpt, kt_ref, gt_ref),
+    ):
+        t = feat[...].T if r == rp else feat[...].astype(F32).T
+
+        def block(b):
+            x = t[b * r : (b + 1) * r]
+            if rp > r:
+                x = jnp.concatenate([x, jnp.zeros((rp - r, rows), x.dtype)])
+            return x.astype(BF16)
+
+        for q in range(nb // 2):
+            a, b = block(2 * q), block(2 * q + 1)
+            keep[q] = jnp.where(first, a, b)
+            give[q] = jnp.where(first, b, a)
+    for feat, r, rp, out in ((txt_ref, rt, rpt, wide[0]), (img_ref, ri, rpi, wide[-1])):
+        if rp > r:
+            out[...] = jnp.zeros_like(out)
+            for b in range(nb):
+                out[:, b * rp : b * rp + r] = feat[:, b * r : (b + 1) * r]
+
+
+def feature_products(nb, ri, rt, final, s_ref, do_ref, dg_ref, wi_ref, wt_ref, *refs):
+    image = s_ref[0] == 0
+    do, dg = do_ref[...], dg_ref[...]
+    dps = jnp.where(image, do, dg), jnp.where(image, dg, do)
+    h = nb // 2
+    base = (s_ref[0] if final else 1 - s_ref[0]) * h
+    got, outs = refs[:-2], refs[-2:]
+    for i, (dp, w_ref, r) in enumerate(((dps[0], wi_ref, ri), (dps[1], wt_ref, rt))):
+        rp = w_ref.shape[1]
+        if r == rp:
+            x = nt(dp, w_ref[pl.ds(base, h)].reshape(h * r, dp.shape[1]))
+        else:
+            x = jnp.concatenate([nt(dp, w_ref[base + b])[:, :r] for b in range(h)], axis=1)
+        if final:
+            x = x + got[i][...].astype(F32)
+        outs[i][...] = x.astype(BF16)
+
+
+def project(n, rpi, rpt, rt, half, slot_ref, img_ref, txt_ref, *refs):
+    chunks, (wi_ref, wt_ref, pi_ref, pt_ref, sq_ref, count_ref) = refs[:-6], refs[-6:]
     it = iter(chunks)
     h = n // 2
     for sibling in range(2):
@@ -99,6 +145,9 @@
                 c = next(it)
                 wi_ref[b] = c[:rpi]
                 wt_ref[b] = c[rpi:]
+    count_ref[...] = jnp.broadcast_to(
+        sum(wt_ref[b, :, :128].astype(F32)[rt : rt + 1] for b in range(2 * n)), (8, 128)
+    )
     pi = nn(img_ref[...], wi_ref[...].reshape(2 * n * rpi, half))
     pt = nn(txt_ref[...], wt_ref[...].reshape(2 * n * rpt, half))
     pi_ref[...] = pi
@@ -124,15 +173,16 @@
     norm_ref[...] = jnp.where(image, ni, nt_)
 
 
-def pairs(chunks, first, *refs):
+def pairs(chunks, sides, first, *refs):
     half = refs[0].shape[1]
-    mine, refs = refs[:4], refs[4:]
+    m = len(sides)
+    mine, refs = refs[: 2 * m], refs[2 * m :]
     fs, refs = refs[: 2 * chunks], refs[2 * chunks :]
     fo = jnp.concatenate([f[...] for f in fs[:chunks]]) if chunks > 1 else fs[0][...]
     fx = jnp.concatenate([f[...] for f in fs[chunks:]]) if chunks > 1 else fs[1][...]
-    ins, outs = (None, refs) if first else (refs[:2], refs[2:])
-    for side in range(2):
-        mo, mx = mine[2 * side], mine[2 * side + 1]
+    ins, outs = ((), refs) if first else (refs[:m], refs[m:])
+    for i, side in enumerate(sides):
+        mo, mx = mine[2 * i], mine[2 * i + 1]
         s = sharpness * (nt(mo[...], fo) + nt(mx[...], fx)) + shift
         if first and side == 0:
             r = lax.broadcasted_iota(jnp.int32, s.shape, 0)
@@ -145,13 +195,16 @@
         for at, f in ((0, fo), (half, fx)):
             part = nn(qb, f)
             cols = slice(at, at + half)
-            outs[side][:, cols] = part if first else ins[side][:, cols] + part
-
-
-def back_norm(s_ref, c_ref, acc_ref, got_ref, mo_ref, mx_ref, norm_ref, do_ref, dx_ref):
-    valid, coef = s_ref[1], c_ref[0]
+            outs[i][:, cols] = (part if first else ins[i][:, cols] + part).astype(outs[i].dtype)
+
+
+def back_norm(
+    s_ref, count_ref, acc_ref, got_ref, last_ref, mo_ref, mx_ref, norm_ref, do_ref, dx_ref
+):
+    valid = s_ref[1]
+    coef = sharpness * multiplier / count_ref[0:1, 0:1]
     rows, half = mo_ref.shape
-    du = (acc_ref[...] + got_ref[...]) * coef
+    du = (acc_ref[...] + got_ref[...] + last_ref[...].astype(F32)) * coef
     duo, dux = du[:, :half], du[:, half:]
     mo, mx = mo_ref[...].astype(F32), mx_ref[...].astype(F32)
     along = jnp.sum(mo * duo, axis=1, keepdims=True) + jnp.sum(mx * dux, axis=1, keepdims=True)
@@ -195,14 +248,29 @@
     count_rows = jnp.broadcast_to(valid_rows.astype(BF16)[:, None], (rpt - rt, half))
     pad = jnp.zeros((rpi - ri, half), BF16)
     w = jnp.concatenate([img_proj] + [pad] * (rpi > ri) + [txt_proj, count_rows])
+    prep = call(
+        functools.partial(prepare, nb, ri, rt, rpi, rpt),
+        [((n, rpi, rows), BF16)] * 2
+        + [((n, rpt, rows), BF16)] * 2
+        + [((rows, nb * rpt), BF16)]
+        + [((rows, nb * rpi), BF16)] * (rpi > ri),
+        [core.astype(jnp.int32).reshape(1)],
+        [img_feat, txt_feat],
+        1,
+    )
     at = {0: w}
     sib = {0: ring.other_core(w)}
-    for k, (f, b) in enumerate(ring.gather(w, rpi), 1):
-        if k < h:
-            at[n - k], at[k] = f, b
-            sib[n - k], sib[k] = ring.other_core(f), ring.other_core(b)
-        else:
-            at[h], sib[h] = (f, b), (ring.other_core(f), ring.other_core(b))
+    f = b = w
+    for k in range(1, h):
+        f, b = ring.right(f), ring.left(b)
+        if k == 1:
+            f, b, *prep = tie((f, b, *prep))
+        at[n - k], at[k] = f, b
+        sib[n - k], sib[k] = ring.other_core(f), ring.other_core(b)
+    img_keep, img_give, txt_keep, txt_give, txt_wide = prep[:5]
+    img_wide = prep[5] if rpi > ri else img_feat
+    f, b = ring.right(f[:rpi]), ring.left(b[rpi:])
+    at[h], sib[h] = (f, b), (ring.other_core(f), ring.other_core(b))
 
     def flat(chunks):
         out = []
@@ -210,100 +278,124 @@
             out += list(chunks[d]) if d == h else [chunks[d]]
         return out
 
-    def spread(feat, r, rp):
-        if rp == r:
-            return feat
-        f = feat.reshape(rows, nb, r)
-        return jnp.pad(f, ((0, 0), (0, 0), (0, rp - r))).reshape(rows, nb * rp)
-
     slots = jnp.stack([2 * ring.chips + core, 2 * ring.chips + 1 - core]).astype(jnp.int32)
-    wi, wt, p_img, p_txt, sq = call(
-        functools.partial(project, n, rpi, rpt, half),
+    wi, wt, p_img, p_txt, sq, count = call(
+        functools.partial(project, n, rpi, rpt, rt, half),
         [
             ((nb, rpi, half), BF16),
             ((nb, rpt, half), BF16),
             ((rows, half), F32),
             ((rows, half), F32),
             ((8, rows), F32),
+            ((8, 128), F32),
         ],
         [slots],
-        [spread(img_feat, ri, rpi), spread(txt_feat, rt, rpt)] + flat(at) + flat(sib),
+        [img_wide, txt_wide] + flat(at) + flat(sib),
+        4,
     )
     mine_o, other_o, norm = call(
         normalize,
         [((rows, half), BF16), ((rows, half), BF16), ((rows, 1), F32)],
         [flags],
         [p_img, p_txt, sq, swap(sq)],
+        1,
     )
 
     other_x = swap(mine_o)
-    mine_x = swap(other_o)
+    other_x, late = tie((other_x, other_o))
+    mine_x = swap(late)
     mine = [mine_o, mine_x, ring.other_core(mine_o), ring.other_core(mine_x)]
-    acc_type = [((rows, 2 * half), F32)] * 2
-    acc = call(functools.partial(pairs, 1, True), acc_type, [], mine + [other_o, other_x])
+
+    def add(acc, sides, arrays, first=False, out=F32):
+        chunks = len(arrays) // 2
+        own = [a for side in sides for a in mine[2 * side : 2 * side + 2]]
+        given = own + arrays
+        return call(
+            functools.partial(pairs, chunks, sides, first),
+            [((rows, 2 * half), out)] * len(sides),
+            [],
+            given + list(acc),
+            1.1 * len(sides),
+            {len(given) + i: i for i in range(len(acc))},
+        )
+
+    acc = ()
+    fa = ba = other_o
+    fc = bc = other_x
+    chunks = [[other_o, other_x]]
     cut = rows // 2
-    for so, sx in zip(ring.gather(other_o, cut), ring.gather(other_x, cut)):
-        acc = call(
-            functools.partial(pairs, 2, False),
-            acc_type,
-            [],
-            mine + list(so) + list(sx) + list(acc),
-            {8: 0, 9: 1},
-        )
-    count = jnp.sum(wt[:, rt, 0].astype(F32))
-    coef = (sharpness * multiplier / count).reshape(1)
+    for k in range(1, h + 1):
+        if k == h:
+            fa, ba, fc, bc = fa[:cut], ba[cut:], fc[:cut], bc[cut:]
+        if k > 2 or k == h:
+            j = k - 3
+            if j >= 0:
+                acc = add(acc, (0, 1), chunks[j], first=j == 0)
+                fa, ba, *acc = tie((fa, ba, *acc))
+        fa, ba = ring.right(fa), ring.left(ba)
+        if k < h:
+            fc, bc, fa, ba = tie((fc, bc, fa, ba))
+        if k == h:
+            acc = add(acc, (0, 1), chunks[h - 2], first=h == 2)
+            fc, bc, *acc = tie((fc, bc, *acc))
+        fc, bc = ring.right(fc), ring.left(bc)
+        chunks.append([fa, ba, fc, bc])
+    waiting = chunks[h - 1][:2] + chunks[h][:2] + chunks[h - 1][2:] + chunks[h][2:]
+    got = ring.other_core(acc[1])
+    (last,) = add((), (1,), waiting, first=True, out=BF16)
+    last, *waiting = tie((last, *waiting))
+    (mine_acc,) = add(acc[:1], (0,), waiting)
     dp_o, dp_x = call(
         back_norm,
         [((rows, half), BF16)] * 2,
-        [flags, coef],
-        [acc[0], ring.other_core(acc[1]), mine_o, mine_x, norm],
+        [flags],
+        [count, mine_acc, got, ring.other_core(last), mine_o, mine_x, norm],
+        1,
     )
     dp_got = swap(dp_x)
     dps = [dp_o, dp_got, ring.other_core(dp_o), ring.other_core(dp_got)]
 
-    def columns(feat, r, rp):
-        t = feat.T.reshape(n, 2, r, rows)
-        t = jnp.pad(t, ((0, 0), (0, 0), (0, rp - r), (0, 0)))
-        keep = lax.dynamic_index_in_dim(t, core, 1, keepdims=False)
-        give = lax.dynamic_index_in_dim(t, 1 - core, 1, keepdims=False)
-        return [keep, ring.other_core(give)]
-
-    feats = columns(img_feat, ri, rpi) + columns(txt_feat, rt, rpt)
+    feats = [img_keep, ring.other_core(img_give), txt_keep, ring.other_core(txt_give)]
 
     def product(first, outs, ds):
-        return call(functools.partial(products, n, first), outs, [flags, ring.chips], ds + feats)
+        body = functools.partial(products, n, first)
+        return call(body, outs, [flags, ring.chips], ds + feats, 1 if first else 2)
 
     f, b = product(True, [((rpi, half), BF16), ((rpt, half), BF16)], dps)
-    dp_o, dp_got, f, b = lax.optimization_barrier((dp_o, dp_got, f, b))
+    dp_o, dp_got, f, b = tie((dp_o, dp_got, f, b))
+    def grads(final, got):
+        return call(
+            functools.partial(feature_products, nb, ri, rt, final),
+            [((rows, nb * ri // 2), BF16), ((rows, nb * rt // 2), BF16)],
+            [flags],
+            [dp_o, dp_got, wi, wt] + got,
+            2,
+        )
+
     (g,) = product(False, [((n, rpi + rpt, half), F32)], [dp_o, dp_got] + dps[2:])
     f, b = ring.right(f), ring.left(b)
+    gives, got = grads(False, []), []
     for k in range(h - 1, 0, -1):
         pf, pb = g[k], g[n - k]
         if k == h - 1:
+            f, b, *gives = tie((f, b, *gives))
             f = jnp.concatenate([pf[:rpi] + f.astype(F32), pf[rpi:]])
             b = jnp.concatenate([pb[:rpi], pb[rpi:] + b.astype(F32)])
         else:
             f, b = pf + f.astype(F32), pb + b.astype(F32)
-        f, b = ring.right(f.astype(BF16)), ring.left(b.astype(BF16))
-    total = g[0] + f.astype(F32) + b.astype(F32)
-
-    is_image = tower == 0
-    dp_img = jnp.where(is_image, dp_o, dp_got)
-    dp_txt = jnp.where(is_image, dp_got, dp_o)
-
-    def halves(wm, r):
-        wm = wm[:, :r].reshape(nb * r, half)
-        m = nb * r // 2
-        keep = lax.dynamic_slice_in_dim(wm, tower * m, m, 0)
-        give = lax.dynamic_slice_in_dim(wm, (1 - tower) * m, m, 0)
-        return keep, give
-
-    (ki, gi), (kt, gt) = halves(wi, ri), halves(wt, rt)
-    img_got = swap(nt(dp_img, gi).astype(BF16)).astype(F32)
-    txt_got = swap(nt(dp_txt, gt).astype(BF16)).astype(F32)
-    img_grad = nt(dp_img, ki) + img_got
-    txt_grad = nt(dp_txt, kt) + txt_got
-    return (img_grad.astype(BF16), txt_grad.astype(BF16), total[:ri], total[rpi : rpi + rt])
+        f, b = f.astype(BF16), b.astype(BF16)
+        if k < h - 1 and gives:
+            got.insert(0, swap(gives.pop()))
+            f, b, got[0] = tie((f, b, got[0]))
+        f, b = ring.right(f), ring.left(b)
+    img_grad, txt_grad = grads(True, [swap(x) for x in gives] + got)
+    f, b, img_grad, txt_grad = tie((f, b, img_grad, txt_grad))
+
+    def total(lo, hi):
+        return g[0, lo:hi] + f[lo:hi].astype(F32) + b[lo:hi].astype(F32)
+
+
+    return (img_grad, txt_grad, total(0, ri), total(rpi, rpi + rt))
 
 
 def solution(mesh):

time: 146 us -> 140 us (0.959)
  local copies, waits for them, and re-layouts: 15.6 us -> 6.58 us
  waiting for transfers between devices: 55.5 us -> 64.2 us
  starting transfers between devices: 46.6 us -> 42.3 us
  matrix products: 3.2 us -> 0 us
  Pallas kernels: 19 us -> 21.8 us
    ppermute x6, waiting for transfers between devices: 5.77 us -> 16.2 us  [swap(): return lax.ppermute(x, 'tower', [(0, 1), (1, 0)])]
    ppermute x16, starting transfers between devices: 25.1 us -> 15.3 us  [right(): return lax.ppermute(x, 'batch', self.fwd)]
    ppermute x16, starting transfers between devices: 10.2 us -> 18.5 us  [left(): return lax.ppermute(x, 'batch', self.bwd)]
    ppermute x16, waiting for transfers between devices: 36.6 us -> 32.7 us  [right(): return lax.ppermute(x, 'batch', self.fwd)]
    dot_general x4 -> x0, matrix products: 3.2 us -> none  [dot(): return lax.dot_general(a, b, (dims, ((), ())), preferred_element_type=F32)]
    slice x9 -> x6, local copies, waits for them, and re-layouts: 2.97 us -> 0.07 us  [the longest x4 0.05 us: shards(): fa, ba, fc, bc = (fa[:cut], ba[cut:], fc[:cut], bc[cut:])]
    reshape x2 -> x0, local copies, waits for them, and re-layouts: 2.87 us -> none  [the longest x1 1.56 us: columns(): t = feat.T.reshape(n, 2, r, rows)]
    pallas_call x10 -> x13, Pallas kernels: 19 us -> 21.8 us  [call(): pl.pallas_call(body, out_shape=[jax.ShapeDtypeStruct(s, t) for s, t in ou...]
  transfers between devices with their start and end apart: 54 -> 55, of which waited for: 20 -> 35; matrix products, arithmetic and copies ran while one was open for 13% -> 0% of each run, Pallas kernels for 6% -> 11%
where the time goes in v3:
time: 140 us
  waiting for transfers between devices  64.2 us (46%)
  starting transfers between devices  42.3 us (30%)
  Pallas kernels  21.8 us (16%)
  local copies, waits for them, and re-layouts  6.58 us (5%)
  other arithmetic  3.14 us (2%)
  between operations  1.63 us (1%)
    ppermute x16, waiting for transfers between devices, right(): return lax.ppermute(x, 'batch', self.fwd)  32.7 us
    pallas_call x13, Pallas kernels, call(): pl.pallas_call(body, out_shape=[jax.ShapeDtypeStruct(s, t) for s, t in ou...  21.8 us
    ppermute x16, starting transfers between devices, left(): return lax.ppermute(x, 'batch', self.bwd)  18.5 us
    ppermute x6, waiting for transfers between devices, swap(): return lax.ppermute(x, 'tower', [(0, 1), (1, 0)])  16.2 us
    ppermute x16, starting transfers between devices, right(): return lax.ppermute(x, 'batch', self.fwd)  15.3 us
    ppermute x16, waiting for transfers between devices, left(): return lax.ppermute(x, 'batch', self.bwd)  12.5 us
    unnamed x18, local copies, waits for them, and re-layouts  6.41 us
    ppermute x6, starting transfers between devices, swap(): return lax.ppermute(x, 'tower', [(0, 1), (1, 0)])  6.23 us
  transfers between devices with their start and end apart: 55, of which 35 were waited for; matrix products, arithmetic and copies ran while one was open for 0% of the time, Pallas kernels for 11%

profile of v3, /device:TPU:0, one launch (start us, length us, event | category | flops | bytes accessed | tf_op | source)
XLA Modules:
  0.0 139.6 jit_solution(13872989008954184940)
XLA Ops:
  2.4 3.1 %collective-permute-start = (bf16[176,576]{1,0:T(8,128)(2,1)S(1)}, bf16[176,576]{1,0:T(8,128)(2,1)S(1)}, u32[]{:S(2)}, u32[]{:S(2)}) collective-permute-start(bf16[176,576]{1,0:T(8,128)(2,1)S(1)} %maximum_maximum_fusion.refs_0_), channel_id=1, source_target_pairs={{0,4},{1,5},{4,8},{5,9},{8,12},{9,13},{12,14},{13,15},{14,10},{15,... | collective-permute-start | bytes 608264 | tf_op jit(solution)/shard_map/ppermute | solution.py:77
  14.5 4.0 %collective-permute-done.4.refs_7_ = bf16[176,576]{1,0:T(8,128)(2,1)S(1)} collective-permute-done((bf16[176,576]{1,0:T(8,128)(2,1)S(1)}, bf16[176,576]{1,0:T(8,128)(2,1)S(1)}, u32[]{:S(2)}, u32[]{:S(2)}) %collective-permute-start.4) | collective-permute-done | bytes 202784 | tf_op jit(solution)/shard_map/ppermute | solution.py:77
  21.1 3.4 %collective-permute-done.5.refs_6_ = bf16[176,576]{1,0:T(8,128)(2,1)S(1)} collective-permute-done((bf16[176,576]{1,0:T(8,128)(2,1)S(1)}, bf16[176,576]{1,0:T(8,128)(2,1)S(1)}, u32[]{:S(2)}, u32[]{:S(2)}) %collective-permute-start.5) | collective-permute-done | bytes 202784 | tf_op jit(solution)/shard_map/ppermute | solution.py:77
  28.7 4.0 %collective-permute-done.7.refs_5_ = bf16[80,576]{1,0:T(8,128)(2,1)S(1)} collective-permute-done((bf16[80,576]{1,0:T(8,128)(2,1)S(1)}, bf16[80,576]{1,0:T(8,128)(2,1)S(1)}, u32[]{:S(2)}, u32[]{:S(2)}) %collective-permute-start.7) | collective-permute-done | bytes 92192 | tf_op jit(solution)/shard_map/ppermute | solution.py:80
  35.3 3.5 %shard_map.85 = (bf16[16,96,576]{2,1,0:T(8,128)(2,1)}, bf16[16,80,576]{2,1,0:T(8,128)(2,1)}, f32[192,576]{1,0:T(8,128)S(1)}, f32[192,576]{1,0:T(8,128)S(1)}, f32[8,192]{1,0:T(8,128)S(1)}, /*index=5*/f32[8,128]{1,0:T(8,128)S(1)}) custom-call(s32[2,8]{1,0:T(2,128)S(1)} %pad_add_fusion.slot_ref, bf16[192,1536]{1,0:T(8,128)(2,1)S(1)} %copy-done.3, ...), custom_call_target="tpu_custom_call" | custom-call | flops 800000000 | bytes 4325376 | tf_op jit(solution)/shard_map/pallas_call | solution.py:37
  40.5 2.0 %collective-permute-done.17.got_ref = f32[8,192]{1,0:T(8,128)S(1)} collective-permute-done((f32[8,192]{1,0:T(8,128)S(1)}, f32[8,192]{1,0:T(8,128)S(1)}, u32[]{:S(2)}, u32[]{:S(2)}) %collective-permute-start.17) | collective-permute-done | bytes 6176 | tf_op jit(solution)/shard_map/ppermute | solution.py:87
  47.0 3.5 %collective-permute-done.18.refs_5_ = bf16[192,576]{1,0:T(8,128)(2,1)S(1)} collective-permute-done((bf16[192,576]{1,0:T(8,128)(2,1)S(1)}, bf16[192,576]{1,0:T(8,128)(2,1)S(1)}, u32[]{:S(2)}, u32[]{:S(2)}) %collective-permute-start.18) | collective-permute-done | bytes 221216 | tf_op jit(solution)/shard_map/ppermute | solution.py:87
  57.0 4.2 %collective-permute-done.24.refs_6_ = bf16[192,576]{1,0:T(8,128)(2,1)S(1)} collective-permute-done((bf16[192,576]{1,0:T(8,128)(2,1)S(1)}, bf16[192,576]{1,0:T(8,128)(2,1)S(1)}, u32[]{:S(2)}, u32[]{:S(2)}) %collective-permute-start.24) | collective-permute-done | bytes 221216 | tf_op jit(solution)/shard_map/ppermute | solution.py:77
  61.8 2.1 %collective-permute-done.26.refs_4_ = bf16[192,576]{1,0:T(8,128)(2,1)S(1)} collective-permute-done((bf16[192,576]{1,0:T(8,128)(2,1)S(1)}, bf16[192,576]{1,0:T(8,128)(2,1)S(1)}, u32[]{:S(2)}, u32[]{:S(2)}) %collective-permute-start.26) | collective-permute-done | bytes 221216 | tf_op jit(solution)/shard_map/ppermute | solution.py:77
  70.1 2.6 %collective-permute-done.28.refs_6_ = bf16[192,576]{1,0:T(8,128)(2,1)S(1)} collective-permute-done((bf16[192,576]{1,0:T(8,128)(2,1)S(1)}, bf16[192,576]{1,0:T(8,128)(2,1)S(1)}, u32[]{:S(2)}, u32[]{:S(2)}) %collective-permute-start.28) | collective-permute-done | bytes 221216 | tf_op jit(solution)/shard_map/ppermute | solution.py:77
  73.3 2.1 %collective-permute-done.30.refs_2_ = bf16[192,576]{1,0:T(8,128)(2,1)S(1)} collective-permute-done((bf16[192,576]{1,0:T(8,128)(2,1)S(1)}, bf16[192,576]{1,0:T(8,128)(2,1)S(1)}, u32[]{:S(2)}, u32[]{:S(2)}) %collective-permute-start.30) | collective-permute-done | bytes 221216 | tf_op jit(solution)/shard_map/ppermute | solution.py:77
  78.0 2.2 %shard_map.88 = (f32[192,1152]{1,0:T(8,128)S(1)}, f32[192,1152]{1,0:T(8,128)S(1)}) custom-call(bf16[192,576]{1,0:T(8,128)(2,1)S(1)} %get-tuple-element.104.refs_0_.mo_ref, bf16[192,576]{1,0:T(8,128)(2,1)S(1)} %collective-permute-done.19.refs_1_.mx_ref, ...), custom_call_target="tpu_custom_call", output_to_operand_aliasing={{0}: (8, {}), {1}: (9, {})} | custom-call | flops 440000000 | bytes 3538944 | tf_op jit(solution)/shard_map/pallas_call | solution.py:37
  80.2 2.2 %shard_map.89 = (f32[192,1152]{1,0:T(8,128)S(1)}, f32[192,1152]{1,0:T(8,128)S(1)}) custom-call(bf16[192,576]{1,0:T(8,128)(2,1)S(1)} %get-tuple-element.104.refs_0_.mo_ref, bf16[192,576]{1,0:T(8,128)(2,1)S(1)} %collective-permute-done.19.refs_1_.mx_ref, ...), custom_call_target="tpu_custom_call", output_to_operand_aliasing={{0}: (8, {}), {1}: (9, {})} | custom-call | flops 440000000 | bytes 3538944 | tf_op jit(solution)/shard_map/pallas_call | solution.py:37
  83.3 1.7 %collective-permute-start.33 = (bf16[96,576]{1,0:T(8,128)(2,1)S(1)}, bf16[96,576]{1,0:T(8,128)(2,1)S(1)}, u32[]{:S(2)}, u32[]{:S(2)}) collective-permute-start(bf16[96,576]{1,0:T(8,128)(2,1)S(1)} %slice.83), channel_id=1, source_target_pairs={{0,2},{1,3},{4,0},{5,1},{8,4},{9,5},{12,8},{13,9},{14,12},{15,13},... | collective-permute-start | bytes 331784 | tf_op jit(solution)/shard_map/ppermute | solution.py:80
  85.3 1.7 %collective-permute-start.37 = (bf16[96,576]{1,0:T(8,128)(2,1)S(1)}, bf16[96,576]{1,0:T(8,128)(2,1)S(1)}, u32[]{:S(2)}, u32[]{:S(2)}) collective-permute-start(bf16[96,576]{1,0:T(8,128)(2,1)S(1)} %slice.107), channel_id=1, source_target_pairs={{0,2},{1,3},{4,0},{5,1},{8,4},{9,5},{12,8},{13,9},{14,12},{15,13},... | collective-permute-start | bytes 331784 | tf_op jit(solution)/shard_map/ppermute | solution.py:80
  87.0 2.1 %collective-permute-done.32.refs_4_ = bf16[96,576]{1,0:T(8,128)(2,1)S(1)} collective-permute-done((bf16[96,576]{1,0:T(8,128)(2,1)S(1)}, bf16[96,576]{1,0:T(8,128)(2,1)S(1)}, u32[]{:S(2)}, u32[]{:S(2)}) %collective-permute-start.32) | collective-permute-done | bytes 110624 | tf_op jit(solution)/shard_map/ppermute | solution.py:77
  89.4 1.8 %collective-permute-done.36.refs_8_ = bf16[96,576]{1,0:T(8,128)(2,1)S(1)} collective-permute-done((bf16[96,576]{1,0:T(8,128)(2,1)S(1)}, bf16[96,576]{1,0:T(8,128)(2,1)S(1)}, u32[]{:S(2)}, u32[]{:S(2)}) %collective-permute-start.36) | collective-permute-done | bytes 110624 | tf_op jit(solution)/shard_map/ppermute | solution.py:77
  96.9 6.9 %collective-permute-done.40.dg_ref = bf16[192,576]{1,0:T(8,128)(2,1)S(1)} collective-permute-done((bf16[192,576]{1,0:T(8,128)(2,1)S(1)}, bf16[192,576]{1,0:T(8,128)(2,1)S(1)}, u32[]{:S(2)}, u32[]{:S(2)}) %collective-permute-start.40) | collective-permute-done | bytes 221216 | tf_op jit(solution)/shard_map/ppermute | solution.py:87
  108.3 1.8 %shard_map.94 = f32[8,176,576]{2,1,0:T(8,128)S(1)} custom-call(s32[2]{0:T(128)S(1)} %pad_add_fusion.1.s_ref, s32[8]{0:T(128)S(1)} %compare_select_fusion.5.chip_ref, bf16[192,576]{1,0:T(8,128)(2,1)S(1)} %get-tuple-element.156.do_ref, bf16[192,576]{1,0:T(8,128)(2,1)S(1)} %collective-permute-done.40.dg_ref, ...), custom_call_target="tpu_custom_call" | custom-call | flops 400000000 | bytes 1966080 | tf_op jit(solution)/shard_map/pallas_call | solution.py:37
  112.2 1.6 %shard_map.95 = (bf16[192,768]{1,0:T(8,128)(2,1)S(1)}, bf16[192,576]{1,0:T(8,128)(2,1)S(1)}) custom-call(s32[2]{0:T(128)S(1)} %pad_add_fusion.1.s_ref, bf16[192,576]{1,0:T(8,128)(2,1)S(1)} %get-tuple-element.156.do_ref, bf16[192,576]{1,0:T(8,128)(2,1)S(1)} %collective-permute-done.40.dg_ref, bf16[16,96,576]{2,1,0:T(8,128)(2,1)S(1)} %copy-done, ...), custom_call_target="tpu_custom_call" | custom-call | flops 400000000 | bytes 3686400 | tf_op jit(solution)/shard_map/pallas_call | solution.py:37
  116.6 4.4 %collective-permute-done.47 = bf16[176,576]{1,0:T(8,128)(2,1)S(1)} collective-permute-done((bf16[176,576]{1,0:T(8,128)(2,1)S(1)}, bf16[176,576]{1,0:T(8,128)(2,1)S(1)}, u32[]{:S(2)}, u32[]{:S(2)}) %collective-permute-start.47) | collective-permute-done | bytes 202784 | tf_op jit(solution)/shard_map/ppermute | solution.py:77
  125.5 3.4 %collective-permute-done.50 = bf16[176,576]{1,0:T(8,128)(2,1)S(1)} collective-permute-done((bf16[176,576]{1,0:T(8,128)(2,1)S(1)}, bf16[176,576]{1,0:T(8,128)(2,1)S(1)}, u32[]{:S(2)}, u32[]{:S(2)}) %collective-permute-start.50) | collective-permute-done | bytes 202784 | tf_op jit(solution)/shard_map/ppermute | solution.py:77
  129.5 2.1 %collective-permute-done.52.refs_0_ = bf16[192,768]{1,0:T(8,128)(2,1)S(1)} collective-permute-done((bf16[192,768]{1,0:T(8,128)(2,1)S(1)}, bf16[192,768]{1,0:T(8,128)(2,1)S(1)}, u32[]{:S(2)}, u32[]{:S(2)}) %collective-permute-start.52) | collective-permute-done | bytes 294944 | tf_op jit(solution)/shard_map/ppermute | solution.py:87
  133.7 2.3 %shard_map.96 = (bf16[192,768]{1,0:T(8,128)(2,1)}, bf16[192,576]{1,0:T(8,128)(2,1)}) custom-call(s32[2]{0:T(128)S(1)} %pad_add_fusion.1.s_ref, bf16[192,576]{1,0:T(8,128)(2,1)S(1)} %get-tuple-element.156.do_ref, bf16[192,576]{1,0:T(8,128)(2,1)S(1)} %collective-permute-done.40.dg_ref, bf16[16,96,576]{2,1,0:T(8,128)(2,1)S(1)} %copy-done, ...), custom_call_target="tpu_custom_call" | custom-call | flops 400000000 | bytes 4202496 | tf_op jit(solution)/shard_map/pallas_call | solution.py:37
  (141 shorter events, 69.2 us)
Async XLA Ops:
  2.4 8.5 %collective-permute-start = (bf16[176,576]{1,0:T(8,128)(2,1)S(1)}, bf16[176,576]{1,0:T(8,128)(2,1)S(1)}, u32[]{:S(2)}, u32[]{:S(2)}) collective-permute-start(bf16[176,576]{1,0:T(8,128)(2,1)S(1)} %maximum_maximum_fusion.refs_0_), channel_id=1, source_target_pairs={{0,4},{1,5},{4,8},{5,9},{8,12},{9,13},{12,14},{13,15},{14,10},{15,... | collective-permute-start | bytes 608264 | tf_op jit(solution)/shard_map/ppermute | solution.py:77
  5.5 7.0 %collective-permute-start.1 = (bf16[176,576]{1,0:T(8,128)(2,1)S(1)}, bf16[176,576]{1,0:T(8,128)(2,1)S(1)}, u32[]{:S(2)}, u32[]{:S(2)}) collective-permute-start(bf16[176,576]{1,0:T(8,128)(2,1)S(1)} %maximum_maximum_fusion.refs_0_), channel_id=1, source_target_pairs={{0,2},{1,3},{4,0},{5,1},{8,4},{9,5},{12,8},{13,9},{14,12},{15,13},... | collective-permute-start | bytes 608264 | tf_op jit(solution)/shard_map/ppermute | solution.py:80
  20.6 7.2 %collective-permute-start.16 = (bf16[176,576]{1,0:T(8,128)(2,1)S(1)}, bf16[176,576]{1,0:T(8,128)(2,1)S(1)}, u32[]{:S(2)}, u32[]{:S(2)}) collective-permute-start(bf16[176,576]{1,0:T(8,128)(2,1)S(1)} %collective-permute-done.refs_8_), channel_id=1, source_target_pairs={{0,1},{1,0},{2,3},{3,2},{4,5},{5,4},{6,7},{7,6},{8,9},{9,8},{10,11... | collective-permute-start | bytes 608264 | tf_op jit(solution)/shard_map/ppermute | solution.py:83
  21.1 7.1 %collective-permute-start.9 = (bf16[176,576]{1,0:T(8,128)(2,1)S(1)}, bf16[176,576]{1,0:T(8,128)(2,1)S(1)}, u32[]{:S(2)}, u32[]{:S(2)}) collective-permute-start(bf16[176,576]{1,0:T(8,128)(2,1)S(1)} %collective-permute-done.1.refs_1_), channel_id=1, source_target_pairs={{0,1},{1,0},{2,3},{3,2},{4,5},{5,4},{6,7},{7,6},{8,9},{9,8},{10,11... | collective-permute-start | bytes 608264 | tf_op jit(solution)/shard_map/ppermute | solution.py:83
  26.1 7.2 %collective-permute-start.15 = (bf16[176,576]{1,0:T(8,128)(2,1)S(1)}, bf16[176,576]{1,0:T(8,128)(2,1)S(1)}, u32[]{:S(2)}, u32[]{:S(2)}) collective-permute-start(bf16[176,576]{1,0:T(8,128)(2,1)S(1)} %collective-permute-done.4.refs_7_), channel_id=1, source_target_pairs={{0,1},{1,0},{2,3},{3,2},{4,5},{5,4},{6,7},{7,6},{8,9},{9,8},{10,11... | collective-permute-start | bytes 608264 | tf_op jit(solution)/shard_map/ppermute | solution.py:83
  43.4 7.1 %collective-permute-start.18 = (bf16[192,576]{1,0:T(8,128)(2,1)S(1)}, bf16[192,576]{1,0:T(8,128)(2,1)S(1)}, u32[]{:S(2)}, u32[]{:S(2)}) collective-permute-start(bf16[192,576]{1,0:T(8,128)(2,1)S(1)} %get-tuple-element.104.refs_0_.mo_ref), channel_id=1, source_target_pairs={{0,16},{16,0},{1,17},{17,1},{2,18},{18,2},{3,19},{19,3},{4,20},{20... | collective-permute-start | bytes 663560 | tf_op jit(solution)/shard_map/ppermute | solution.py:87
  45.0 7.1 %collective-permute-start.22 = (bf16[192,576]{1,0:T(8,128)(2,1)S(1)}, bf16[192,576]{1,0:T(8,128)(2,1)S(1)}, u32[]{:S(2)}, u32[]{:S(2)}) collective-permute-start(bf16[192,576]{1,0:T(8,128)(2,1)S(1)} %get-tuple-element.106.refs_4_), channel_id=1, source_target_pairs={{0,4},{1,5},{4,8},{5,9},{8,12},{9,13},{12,14},{13,15},{14,10},{15,... | collective-permute-start | bytes 663560 | tf_op jit(solution)/shard_map/ppermute | solution.py:77
  53.0 8.2 %collective-permute-start.24 = (bf16[192,576]{1,0:T(8,128)(2,1)S(1)}, bf16[192,576]{1,0:T(8,128)(2,1)S(1)}, u32[]{:S(2)}, u32[]{:S(2)}) collective-permute-start(bf16[192,576]{1,0:T(8,128)(2,1)S(1)} %collective-permute-done.18.refs_5_), channel_id=1, source_target_pairs={{0,4},{1,5},{4,8},{5,9},{8,12},{9,13},{12,14},{13,15},{14,10},{15,... | collective-permute-start | bytes 663560 | tf_op jit(solution)/shard_map/ppermute | solution.py:77
  53.6 8.2 %collective-permute-start.25 = (bf16[192,576]{1,0:T(8,128)(2,1)S(1)}, bf16[192,576]{1,0:T(8,128)(2,1)S(1)}, u32[]{:S(2)}, u32[]{:S(2)}) collective-permute-start(bf16[192,576]{1,0:T(8,128)(2,1)S(1)} %collective-permute-done.18.refs_5_), channel_id=1, source_target_pairs={{0,2},{1,3},{4,0},{5,1},{8,4},{9,5},{12,8},{13,9},{14,12},{15,13},... | collective-permute-start | bytes 663560 | tf_op jit(solution)/shard_map/ppermute | solution.py:80
  55.0 8.8 %collective-permute-start.26 = (bf16[192,576]{1,0:T(8,128)(2,1)S(1)}, bf16[192,576]{1,0:T(8,128)(2,1)S(1)}, u32[]{:S(2)}, u32[]{:S(2)}) collective-permute-start(bf16[192,576]{1,0:T(8,128)(2,1)S(1)} %collective-permute-done.22.refs_4_), channel_id=1, source_target_pairs={{0,4},{1,5},{4,8},{5,9},{8,12},{9,13},{12,14},{13,15},{14,10},{15,... | collective-permute-start | bytes 663560 | tf_op jit(solution)/shard_map/ppermute | solution.py:77
  55.6 8.8 %collective-permute-start.27 = (bf16[192,576]{1,0:T(8,128)(2,1)S(1)}, bf16[192,576]{1,0:T(8,128)(2,1)S(1)}, u32[]{:S(2)}, u32[]{:S(2)}) collective-permute-start(bf16[192,576]{1,0:T(8,128)(2,1)S(1)} %collective-permute-done.23.refs_5_), channel_id=1, source_target_pairs={{0,2},{1,3},{4,0},{5,1},{8,4},{9,5},{12,8},{13,9},{14,12},{15,13},... | collective-permute-start | bytes 663560 | tf_op jit(solution)/shard_map/ppermute | solution.py:80
  57.0 9.4 %collective-permute-start.20 = (bf16[192,576]{1,0:T(8,128)(2,1)S(1)}, bf16[192,576]{1,0:T(8,128)(2,1)S(1)}, u32[]{:S(2)}, u32[]{:S(2)}) collective-permute-start(bf16[192,576]{1,0:T(8,128)(2,1)S(1)} %get-tuple-element.104.refs_0_.mo_ref), channel_id=1, source_target_pairs={{0,1},{1,0},{2,3},{3,2},{4,5},{5,4},{6,7},{7,6},{8,9},{9,8},{10,11... | collective-permute-start | bytes 663560 | tf_op jit(solution)/shard_map/ppermute | solution.py:83
  64.4 8.4 %collective-permute-start.28 = (bf16[192,576]{1,0:T(8,128)(2,1)S(1)}, bf16[192,576]{1,0:T(8,128)(2,1)S(1)}, u32[]{:S(2)}, u32[]{:S(2)}) collective-permute-start(bf16[192,576]{1,0:T(8,128)(2,1)S(1)} %collective-permute-done.24.refs_6_), channel_id=1, source_target_pairs={{0,4},{1,5},{4,8},{5,9},{8,12},{9,13},{12,14},{13,15},{14,10},{15,... | collective-permute-start | bytes 663560 | tf_op jit(solution)/shard_map/ppermute | solution.py:77
  65.0 8.3 %collective-permute-start.29 = (bf16[192,576]{1,0:T(8,128)(2,1)S(1)}, bf16[192,576]{1,0:T(8,128)(2,1)S(1)}, u32[]{:S(2)}, u32[]{:S(2)}) collective-permute-start(bf16[192,576]{1,0:T(8,128)(2,1)S(1)} %collective-permute-done.25.refs_7_), channel_id=1, source_target_pairs={{0,2},{1,3},{4,0},{5,1},{8,4},{9,5},{12,8},{13,9},{14,12},{15,13},... | collective-permute-start | bytes 663560 | tf_op jit(solution)/shard_map/ppermute | solution.py:80
  68.0 7.4 %collective-permute-start.30 = (bf16[192,576]{1,0:T(8,128)(2,1)S(1)}, bf16[192,576]{1,0:T(8,128)(2,1)S(1)}, u32[]{:S(2)}, u32[]{:S(2)}) collective-permute-start(bf16[192,576]{1,0:T(8,128)(2,1)S(1)} %collective-permute-done.26.refs_4_), channel_id=1, source_target_pairs={{0,4},{1,5},{4,8},{5,9},{8,12},{9,13},{12,14},{13,15},{14,10},{15,... | collective-permute-start | bytes 663560 | tf_op jit(solution)/shard_map/ppermute | solution.py:77
  68.7 7.3 %collective-permute-start.31 = (bf16[192,576]{1,0:T(8,128)(2,1)S(1)}, bf16[192,576]{1,0:T(8,128)(2,1)S(1)}, u32[]{:S(2)}, u32[]{:S(2)}) collective-permute-start(bf16[192,576]{1,0:T(8,128)(2,1)S(1)} %collective-permute-done.27.refs_5_), channel_id=1, source_target_pairs={{0,2},{1,3},{4,0},{5,1},{8,4},{9,5},{12,8},{13,9},{14,12},{15,13},... | collective-permute-start | bytes 663560 | tf_op jit(solution)/shard_map/ppermute | solution.py:80
  82.8 11.7 %collective-permute-start.38 = (f32[192,1152]{1,0:T(8,128)S(1)}, f32[192,1152]{1,0:T(8,128)S(1)}, u32[]{:S(2)}, u32[]{:S(2)}) collective-permute-start(f32[192,1152]{1,0:T(8,128)S(1)} %get-tuple-element.145), channel_id=1, source_target_pairs={{0,1},{1,0},{2,3},{3,2},{4,5},{5,4},{6,7},{7,6},{8,9},{9,8},{10,11... | collective-permute-start | bytes 2654216 | tf_op jit(solution)/shard_map/ppermute | solution.py:83
  95.7 8.1 %collective-permute-start.40 = (bf16[192,576]{1,0:T(8,128)(2,1)S(1)}, bf16[192,576]{1,0:T(8,128)(2,1)S(1)}, u32[]{:S(2)}, u32[]{:S(2)}) collective-permute-start(bf16[192,576]{1,0:T(8,128)(2,1)S(1)} %get-tuple-element.149), channel_id=1, source_target_pairs={{0,16},{16,0},{1,17},{17,1},{2,18},{18,2},{3,19},{19,3},{4,20},{20... | collective-permute-start | bytes 663560 | tf_op jit(solution)/shard_map/ppermute | solution.py:87
  96.3 7.6 %collective-permute-start.43 = (bf16[8,96,192]{2,1,0:T(8,128)(2,1)S(1)}, bf16[8,96,192]{2,1,0:T(8,128)(2,1)S(1)}, u32[]{:S(2)}, u32[]{:S(2)}) collective-permute-start(bf16[8,96,192]{2,1,0:T(8,128)(2,1)S(1)} %copy-done.6), channel_id=1, source_target_pairs={{0,1},{1,0},{2,3},{3,2},{4,5},{5,4},{6,7},{7,6},{8,9},{9,8},{10,11... | collective-permute-start | bytes 884744 | tf_op jit(solution)/shard_map/ppermute | solution.py:83
  96.3 7.5 %collective-permute-start.44 = (bf16[8,80,192]{2,1,0:T(8,128)(2,1)S(1)}, bf16[8,80,192]{2,1,0:T(8,128)(2,1)S(1)}, u32[]{:S(2)}, u32[]{:S(2)}) collective-permute-start(bf16[8,80,192]{2,1,0:T(8,128)(2,1)S(1)} %copy-done.8), channel_id=1, source_target_pairs={{0,1},{1,0},{2,3},{3,2},{4,5},{5,4},{6,7},{7,6},{8,9},{9,8},{10,11... | collective-permute-start | bytes 737288 | tf_op jit(solution)/shard_map/ppermute | solution.py:83
  96.8 7.1 %collective-permute-start.41 = (bf16[192,576]{1,0:T(8,128)(2,1)S(1)}, bf16[192,576]{1,0:T(8,128)(2,1)S(1)}, u32[]{:S(2)}, u32[]{:S(2)}) collective-permute-start(bf16[192,576]{1,0:T(8,128)(2,1)S(1)} %get-tuple-element.156.do_ref), channel_id=1, source_target_pairs={{0,1},{1,0},{2,3},{3,2},{4,5},{5,4},{6,7},{7,6},{8,9},{9,8},{10,11... | collective-permute-start | bytes 663560 | tf_op jit(solution)/shard_map/ppermute | solution.py:83
  106.2 7.6 %collective-permute-start.45 = (bf16[96,576]{1,0:T(8,128)(2,1)S(1)}, bf16[96,576]{1,0:T(8,128)(2,1)S(1)}, u32[]{:S(2)}, u32[]{:S(2)}) collective-permute-start(bf16[96,576]{1,0:T(8,128)(2,1)S(1)} %get-tuple-element.158), channel_id=1, source_target_pairs={{0,4},{1,5},{4,8},{5,9},{8,12},{9,13},{12,14},{13,15},{14,10},{15,... | collective-permute-start | bytes 331784 | tf_op jit(solution)/shard_map/ppermute | solution.py:77
  106.8 7.0 %collective-permute-start.46 = (bf16[80,576]{1,0:T(8,128)(2,1)S(1)}, bf16[80,576]{1,0:T(8,128)(2,1)S(1)}, u32[]{:S(2)}, u32[]{:S(2)}) collective-permute-start(bf16[80,576]{1,0:T(8,128)(2,1)S(1)} %get-tuple-element.159), channel_id=1, source_target_pairs={{0,2},{1,3},{4,0},{5,1},{8,4},{9,5},{12,8},{13,9},{14,12},{15,13},... | collective-permute-start | bytes 276488 | tf_op jit(solution)/shard_map/ppermute | solution.py:80
  113.9 7.0 %collective-permute-start.47 = (bf16[176,576]{1,0:T(8,128)(2,1)S(1)}, bf16[176,576]{1,0:T(8,128)(2,1)S(1)}, u32[]{:S(2)}, u32[]{:S(2)}) collective-permute-start(bf16[176,576]{1,0:T(8,128)(2,1)S(1)} %pad_maximum_fusion), channel_id=1, source_target_pairs={{0,4},{1,5},{4,8},{5,9},{8,12},{9,13},{12,14},{13,15},{14,10},{15,... | collective-permute-start | bytes 608264 | tf_op jit(solution)/shard_map/ppermute | solution.py:77
  (40 other events, 181.9 us)

commit v4 on v3

--- a/solution.py
+++ b/solution.py
@@ -113,22 +113,29 @@
                 out[:, b * rp : b * rp + r] = feat[:, b * r : (b + 1) * r]
 
 
-def feature_products(nb, ri, rt, final, s_ref, do_ref, dg_ref, wi_ref, wt_ref, *refs):
+def feature_products(nb, ri, rt, s_ref, do_ref, dg_ref, wi_ref, wt_ref, keep_ref, give_ref):
     image = s_ref[0] == 0
     do, dg = do_ref[...], dg_ref[...]
     dps = jnp.where(image, do, dg), jnp.where(image, dg, do)
     h = nb // 2
-    base = (s_ref[0] if final else 1 - s_ref[0]) * h
-    got, outs = refs[:-2], refs[-2:]
-    for i, (dp, w_ref, r) in enumerate(((dps[0], wi_ref, ri), (dps[1], wt_ref, rt))):
-        rp = w_ref.shape[1]
-        if r == rp:
-            x = nt(dp, w_ref[pl.ds(base, h)].reshape(h * r, dp.shape[1]))
-        else:
-            x = jnp.concatenate([nt(dp, w_ref[base + b])[:, :r] for b in range(h)], axis=1)
-        if final:
-            x = x + got[i][...].astype(F32)
-        outs[i][...] = x.astype(BF16)
+    for out, tower in ((give_ref, 1 - s_ref[0]), (keep_ref, s_ref[0])):
+        at = 0
+        for dp, w_ref, r in ((dps[0], wi_ref, ri), (dps[1], wt_ref, rt)):
+            if r == w_ref.shape[1]:
+                x = nt(dp, w_ref[pl.ds(tower * h, h)].reshape(h * r, dp.shape[1]))
+            else:
+                x = [nt(dp, w_ref[tower * h + b])[:, :r] for b in range(h)]
+                x = jnp.concatenate(x, axis=1)
+            out[:, at : at + h * r] = x.astype(out.dtype)
+            at += h * r
+
+
+def finish(keep_ref, got_ref, img_ref, txt_ref):
+    at = 0
+    for out in (img_ref, txt_ref):
+        cols = slice(at, at + out.shape[1])
+        out[...] = (keep_ref[:, cols] + got_ref[:, cols].astype(F32)).astype(BF16)
+        at += out.shape[1]
 
 
 def project(n, rpi, rpt, rt, half, slot_ref, img_ref, txt_ref, *refs):
@@ -221,16 +228,18 @@
     txt, txt_s = jnp.where(image, dg, do), jnp.where(image, sg, so)
     rpi = ai.shape[1]
     h = n // 2
-    for d in [h] if first else [d for d in range(n) if d != h]:
+    early = [h, h - 1, n - h + 1]
+    for d in early if first else [d for d in range(n) if d not in early]:
         q = chip_ref[d]
         gi = nn(ai[q], img) + nn(bi[q], img_s)
         gt = nn(at[q], txt) + nn(bt[q], txt_s)
-        if first:
+        if d == h:
             outs[0][...] = gi.astype(BF16)
             outs[1][...] = gt.astype(BF16)
         else:
-            outs[0][d, :rpi] = gi
-            outs[0][d, rpi:] = gt
+            out = outs[1 + early.index(d)] if first else outs[0].at[d]
+            out[:rpi] = gi
+            out[rpi:] = gt
 
 
 def shards(img_feat, txt_feat, img_proj, txt_proj, valid_rows):
@@ -361,41 +370,46 @@
         body = functools.partial(products, n, first)
         return call(body, outs, [flags, ring.chips], ds + feats, 1 if first else 2)
 
-    f, b = product(True, [((rpi, half), BF16), ((rpt, half), BF16)], dps)
+    chunk = ((rpi + rpt, half), F32)
+    f, b, gf, gb = product(True, [((rpi, half), BF16), ((rpt, half), BF16), chunk, chunk], dps)
     dp_o, dp_got, f, b = tie((dp_o, dp_got, f, b))
-    def grads(final, got):
-        return call(
-            functools.partial(feature_products, nb, ri, rt, final),
-            [((rows, nb * ri // 2), BF16), ((rows, nb * rt // 2), BF16)],
-            [flags],
-            [dp_o, dp_got, wi, wt] + got,
-            2,
-        )
-
-    (g,) = product(False, [((n, rpi + rpt, half), F32)], [dp_o, dp_got] + dps[2:])
+    keep, give = call(
+        functools.partial(feature_products, nb, ri, rt),
+        [((rows, nb * (ri + rt) // 2), F32), ((rows, nb * (ri + rt) // 2), BF16)],
+        [flags],
+        [dp_o, dp_got, wi, wt],
+        3,
+    )
+
     f, b = ring.right(f), ring.left(b)
-    gives, got = grads(False, []), []
+    f, *late = tie((f, *dps))
+    (g,) = product(False, [((n, rpi + rpt, half), F32)], late)
     for k in range(h - 1, 0, -1):
-        pf, pb = g[k], g[n - k]
+        pf, pb = (gf, gb) if k == h - 1 else (g[k], g[n - k])
         if k == h - 1:
-            f, b, *gives = tie((f, b, *gives))
             f = jnp.concatenate([pf[:rpi] + f.astype(F32), pf[rpi:]])
             b = jnp.concatenate([pb[:rpi], pb[rpi:] + b.astype(F32)])
         else:
             f, b = pf + f.astype(F32), pb + b.astype(F32)
         f, b = f.astype(BF16), b.astype(BF16)
-        if k < h - 1 and gives:
-            got.insert(0, swap(gives.pop()))
-            f, b, got[0] = tie((f, b, got[0]))
+        if k == h - 2:
+            f, b, keep, give = tie((f, b, keep, give))
         f, b = ring.right(f), ring.left(b)
-    img_grad, txt_grad = grads(True, [swap(x) for x in gives] + got)
+    got = swap(give)
+    img_grad, txt_grad = call(
+        finish,
+        [((rows, nb * r // 2), BF16) for r in (ri, rt)],
+        [],
+        [keep, got],
+        10,
+    )
     f, b, img_grad, txt_grad = tie((f, b, img_grad, txt_grad))
 
     def total(lo, hi):
         return g[0, lo:hi] + f[lo:hi].astype(F32) + b[lo:hi].astype(F32)
 
-
-    return (img_grad, txt_grad, total(0, ri), total(rpi, rpi + rt))
+    img_total, txt_total = total(0, ri), total(rpi, rpi + rt)
+    return img_grad, txt_grad, img_total, txt_total
 
 
 def solution(mesh):

time: 140 us -> 135 us (0.964)
  local copies, waits for them, and re-layouts: 6.58 us -> 4.83 us
  waiting for transfers between devices: 64.2 us -> 62.7 us
    ppermute x16, waiting for transfers between devices: 32.7 us -> 29.6 us  [right(): return lax.ppermute(x, 'batch', self.fwd)]
    ppermute x16, waiting for transfers between devices: 12.5 us -> 15.1 us  [left(): return lax.ppermute(x, 'batch', self.bwd)]
    unnamed x18, local copies, waits for them, and re-layouts: 6.41 us -> 4.65 us
    ppermute x6 -> x5, waiting for transfers between devices: 16.2 us -> 15.2 us  [swap(): return lax.ppermute(x, 'tower', [(0, 1), (1, 0)])]
    ppermute x6 -> x5, starting transfers between devices: 6.23 us -> 5.78 us  [swap(): return lax.ppermute(x, 'tower', [(0, 1), (1, 0)])]
  transfers between devices with their start and end apart: 55 -> 54, of which waited for: 35 -> 35; matrix products, arithmetic and copies ran while one was open for 0% -> 0% of each run, Pallas kernels for 11% -> 11%
where the time goes in v4:
time: 135 us
  waiting for transfers between devices  62.7 us (46%)
  starting transfers between devices  41.9 us (31%)
  Pallas kernels  21.2 us (16%)
  local copies, waits for them, and re-layouts  4.83 us (4%)
  other arithmetic  2.94 us (2%)
  between operations  1.6 us (1%)
    ppermute x16, waiting for transfers between devices, right(): return lax.ppermute(x, 'batch', self.fwd)  29.6 us
    pallas_call x13, Pallas kernels, call(): pl.pallas_call(body, out_shape=[jax.ShapeDtypeStruct(s, t) for s, t in ou...  21.2 us
    ppermute x16, starting transfers between devices, left(): return lax.ppermute(x, 'batch', self.bwd)  19.5 us
    ppermute x5, waiting for transfers between devices, swap(): return lax.ppermute(x, 'tower', [(0, 1), (1, 0)])  15.2 us
    ppermute x16, waiting for transfers between devices, left(): return lax.ppermute(x, 'batch', self.bwd)  15.1 us
    ppermute x16, starting transfers between devices, right(): return lax.ppermute(x, 'batch', self.fwd)  14.3 us
    ppermute x5, starting transfers between devices, swap(): return lax.ppermute(x, 'tower', [(0, 1), (1, 0)])  5.78 us
    unnamed x18, local copies, waits for them, and re-layouts  4.65 us
  transfers between devices with their start and end apart: 54, of which 35 were waited for; matrix products, arithmetic and copies ran while one was open for 0% of the time, Pallas kernels for 11%

profile of v4, /device:TPU:0, one launch (start us, length us, event | category | flops | bytes accessed | tf_op | source)
XLA Modules:
  0.0 135.1 jit_solution(15657687595523063593)
XLA Ops:
  2.4 3.1 %collective-permute-start = (bf16[176,576]{1,0:T(8,128)(2,1)S(1)}, bf16[176,576]{1,0:T(8,128)(2,1)S(1)}, u32[]{:S(2)}, u32[]{:S(2)}) collective-permute-start(bf16[176,576]{1,0:T(8,128)(2,1)S(1)} %maximum_maximum_fusion.refs_0_), channel_id=1, source_target_pairs={{0,4},{1,5},{4,8},{5,9},{8,12},{9,13},{12,14},{13,15},{14,10},{15,... | collective-permute-start | bytes 608264 | tf_op jit(solution)/shard_map/ppermute | solution.py:77
  14.5 4.0 %collective-permute-done.4.refs_7_ = bf16[176,576]{1,0:T(8,128)(2,1)S(1)} collective-permute-done((bf16[176,576]{1,0:T(8,128)(2,1)S(1)}, bf16[176,576]{1,0:T(8,128)(2,1)S(1)}, u32[]{:S(2)}, u32[]{:S(2)}) %collective-permute-start.4) | collective-permute-done | bytes 202784 | tf_op jit(solution)/shard_map/ppermute | solution.py:77
  21.1 3.4 %collective-permute-done.5.refs_6_ = bf16[176,576]{1,0:T(8,128)(2,1)S(1)} collective-permute-done((bf16[176,576]{1,0:T(8,128)(2,1)S(1)}, bf16[176,576]{1,0:T(8,128)(2,1)S(1)}, u32[]{:S(2)}, u32[]{:S(2)}) %collective-permute-start.5) | collective-permute-done | bytes 202784 | tf_op jit(solution)/shard_map/ppermute | solution.py:77
  28.7 4.0 %collective-permute-done.7.refs_5_ = bf16[80,576]{1,0:T(8,128)(2,1)S(1)} collective-permute-done((bf16[80,576]{1,0:T(8,128)(2,1)S(1)}, bf16[80,576]{1,0:T(8,128)(2,1)S(1)}, u32[]{:S(2)}, u32[]{:S(2)}) %collective-permute-start.7) | collective-permute-done | bytes 92192 | tf_op jit(solution)/shard_map/ppermute | solution.py:80
  35.3 3.5 %shard_map.85 = (bf16[16,96,576]{2,1,0:T(8,128)(2,1)}, bf16[16,80,576]{2,1,0:T(8,128)(2,1)}, f32[192,576]{1,0:T(8,128)S(1)}, f32[192,576]{1,0:T(8,128)S(1)}, f32[8,192]{1,0:T(8,128)S(1)}, /*index=5*/f32[8,128]{1,0:T(8,128)S(1)}) custom-call(s32[2,8]{1,0:T(2,128)S(1)} %pad_add_fusion.slot_ref, bf16[192,1536]{1,0:T(8,128)(2,1)S(1)} %copy-done.1, ...), custom_call_target="tpu_custom_call" | custom-call | flops 800000000 | bytes 4325376 | tf_op jit(solution)/shard_map/pallas_call | solution.py:37
  40.5 2.0 %collective-permute-done.17.got_ref = f32[8,192]{1,0:T(8,128)S(1)} collective-permute-done((f32[8,192]{1,0:T(8,128)S(1)}, f32[8,192]{1,0:T(8,128)S(1)}, u32[]{:S(2)}, u32[]{:S(2)}) %collective-permute-start.17) | collective-permute-done | bytes 6176 | tf_op jit(solution)/shard_map/ppermute | solution.py:87
  47.0 3.5 %collective-permute-done.18.refs_5_ = bf16[192,576]{1,0:T(8,128)(2,1)S(1)} collective-permute-done((bf16[192,576]{1,0:T(8,128)(2,1)S(1)}, bf16[192,576]{1,0:T(8,128)(2,1)S(1)}, u32[]{:S(2)}, u32[]{:S(2)}) %collective-permute-start.18) | collective-permute-done | bytes 221216 | tf_op jit(solution)/shard_map/ppermute | solution.py:87
  57.0 4.2 %collective-permute-done.24.refs_6_ = bf16[192,576]{1,0:T(8,128)(2,1)S(1)} collective-permute-done((bf16[192,576]{1,0:T(8,128)(2,1)S(1)}, bf16[192,576]{1,0:T(8,128)(2,1)S(1)}, u32[]{:S(2)}, u32[]{:S(2)}) %collective-permute-start.24) | collective-permute-done | bytes 221216 | tf_op jit(solution)/shard_map/ppermute | solution.py:77
  61.8 2.1 %collective-permute-done.26.refs_4_ = bf16[192,576]{1,0:T(8,128)(2,1)S(1)} collective-permute-done((bf16[192,576]{1,0:T(8,128)(2,1)S(1)}, bf16[192,576]{1,0:T(8,128)(2,1)S(1)}, u32[]{:S(2)}, u32[]{:S(2)}) %collective-permute-start.26) | collective-permute-done | bytes 221216 | tf_op jit(solution)/shard_map/ppermute | solution.py:77
  70.1 2.6 %collective-permute-done.28.refs_6_ = bf16[192,576]{1,0:T(8,128)(2,1)S(1)} collective-permute-done((bf16[192,576]{1,0:T(8,128)(2,1)S(1)}, bf16[192,576]{1,0:T(8,128)(2,1)S(1)}, u32[]{:S(2)}, u32[]{:S(2)}) %collective-permute-start.28) | collective-permute-done | bytes 221216 | tf_op jit(solution)/shard_map/ppermute | solution.py:77
  73.3 2.1 %collective-permute-done.30.refs_2_ = bf16[192,576]{1,0:T(8,128)(2,1)S(1)} collective-permute-done((bf16[192,576]{1,0:T(8,128)(2,1)S(1)}, bf16[192,576]{1,0:T(8,128)(2,1)S(1)}, u32[]{:S(2)}, u32[]{:S(2)}) %collective-permute-start.30) | collective-permute-done | bytes 221216 | tf_op jit(solution)/shard_map/ppermute | solution.py:77
  78.0 2.2 %shard_map.88 = (f32[192,1152]{1,0:T(8,128)S(1)}, f32[192,1152]{1,0:T(8,128)S(1)}) custom-call(bf16[192,576]{1,0:T(8,128)(2,1)S(1)} %get-tuple-element.105.refs_0_.mo_ref, bf16[192,576]{1,0:T(8,128)(2,1)S(1)} %collective-permute-done.19.refs_1_.mx_ref, ...), custom_call_target="tpu_custom_call", output_to_operand_aliasing={{0}: (8, {}), {1}: (9, {})} | custom-call | flops 440000000 | bytes 3538944 | tf_op jit(solution)/shard_map/pallas_call | solution.py:37
  80.2 2.2 %shard_map.89 = (f32[192,1152]{1,0:T(8,128)S(1)}, f32[192,1152]{1,0:T(8,128)S(1)}) custom-call(bf16[192,576]{1,0:T(8,128)(2,1)S(1)} %get-tuple-element.105.refs_0_.mo_ref, bf16[192,576]{1,0:T(8,128)(2,1)S(1)} %collective-permute-done.19.refs_1_.mx_ref, ...), custom_call_target="tpu_custom_call", output_to_operand_aliasing={{0}: (8, {}), {1}: (9, {})} | custom-call | flops 440000000 | bytes 3538944 | tf_op jit(solution)/shard_map/pallas_call | solution.py:37
  85.3 1.7 %collective-permute-start.37 = (bf16[96,576]{1,0:T(8,128)(2,1)S(1)}, bf16[96,576]{1,0:T(8,128)(2,1)S(1)}, u32[]{:S(2)}, u32[]{:S(2)}) collective-permute-start(bf16[96,576]{1,0:T(8,128)(2,1)S(1)} %slice.85), channel_id=1, source_target_pairs={{0,2},{1,3},{4,0},{5,1},{8,4},{9,5},{12,8},{13,9},{14,12},{15,13},... | collective-permute-start | bytes 331784 | tf_op jit(solution)/shard_map/ppermute | solution.py:80
  86.9 2.1 %collective-permute-done.32.refs_4_ = bf16[96,576]{1,0:T(8,128)(2,1)S(1)} collective-permute-done((bf16[96,576]{1,0:T(8,128)(2,1)S(1)}, bf16[96,576]{1,0:T(8,128)(2,1)S(1)}, u32[]{:S(2)}, u32[]{:S(2)}) %collective-permute-start.32) | collective-permute-done | bytes 110624 | tf_op jit(solution)/shard_map/ppermute | solution.py:77
  89.4 1.8 %collective-permute-done.36.refs_8_ = bf16[96,576]{1,0:T(8,128)(2,1)S(1)} collective-permute-done((bf16[96,576]{1,0:T(8,128)(2,1)S(1)}, bf16[96,576]{1,0:T(8,128)(2,1)S(1)}, u32[]{:S(2)}, u32[]{:S(2)}) %collective-permute-start.36) | collective-permute-done | bytes 110624 | tf_op jit(solution)/shard_map/ppermute | solution.py:77
  96.9 7.0 %collective-permute-done.40.dg_ref = bf16[192,576]{1,0:T(8,128)(2,1)S(1)} collective-permute-done((bf16[192,576]{1,0:T(8,128)(2,1)S(1)}, bf16[192,576]{1,0:T(8,128)(2,1)S(1)}, u32[]{:S(2)}, u32[]{:S(2)}) %collective-permute-start.40) | collective-permute-done | bytes 221216 | tf_op jit(solution)/shard_map/ppermute | solution.py:87
  106.6 1.7 %collective-permute-start.47 = (bf16[80,576]{1,0:T(8,128)(2,1)S(1)}, bf16[80,576]{1,0:T(8,128)(2,1)S(1)}, u32[]{:S(2)}, u32[]{:S(2)}) collective-permute-start(bf16[80,576]{1,0:T(8,128)(2,1)S(1)} %get-tuple-element.165), channel_id=1, source_target_pairs={{0,2},{1,3},{4,0},{5,1},{8,4},{9,5},{12,8},{13,9},{14,12},{15,13},... | collective-permute-start | bytes 276488 | tf_op jit(solution)/shard_map/ppermute | solution.py:80
  108.7 2.9 %collective-permute-done.47 = bf16[80,576]{1,0:T(8,128)(2,1)S(1)} collective-permute-done((bf16[80,576]{1,0:T(8,128)(2,1)S(1)}, bf16[80,576]{1,0:T(8,128)(2,1)S(1)}, u32[]{:S(2)}, u32[]{:S(2)}) %collective-permute-start.47) | collective-permute-done | bytes 92192 | tf_op jit(solution)/shard_map/ppermute | solution.py:80
  111.6 1.7 %collective-permute-start.48 = (bf16[176,576]{1,0:T(8,128)(2,1)S(1)}, bf16[176,576]{1,0:T(8,128)(2,1)S(1)}, u32[]{:S(2)}, u32[]{:S(2)}) collective-permute-start(bf16[176,576]{1,0:T(8,128)(2,1)S(1)} %pad_maximum_fusion.1), channel_id=1, source_target_pairs={{0,2},{1,3},{4,0},{5,1},{8,4},{9,5},{12,8},{13,9},{14,12},{15,13},... | collective-permute-start | bytes 608264 | tf_op jit(solution)/shard_map/ppermute | solution.py:80
  113.9 2.5 %shard_map.95 = (f32[192,1344]{1,0:T(8,128)S(1)}, bf16[192,1344]{1,0:T(8,128)(2,1)S(1)}) custom-call(s32[2]{0:T(128)S(1)} %pad_add_fusion.1.s_ref, bf16[192,576]{1,0:T(8,128)(2,1)S(1)} %get-tuple-element.166.do_ref, bf16[192,576]{1,0:T(8,128)(2,1)S(1)} %collective-permute-done.40.dg_ref, bf16[16,96,576]{2,1,0:T(8,128)(2,1)S(1)} %copy-done.2, ...), custom_call_target="tpu_custom_call" | custom-call | flops 600000000 | bytes 3686400 | tf_op jit(solution)/shard_map/pallas_call | solution.py:37
  122.6 4.4 %collective-permute-done.49 = bf16[176,576]{1,0:T(8,128)(2,1)S(1)} collective-permute-done((bf16[176,576]{1,0:T(8,128)(2,1)S(1)}, bf16[176,576]{1,0:T(8,128)(2,1)S(1)}, u32[]{:S(2)}, u32[]{:S(2)}) %collective-permute-start.49) | collective-permute-done | bytes 202784 | tf_op jit(solution)/shard_map/ppermute | solution.py:77
  127.7 2.0 %collective-permute-start.52 = (bf16[176,576]{1,0:T(8,128)(2,1)S(1)}, bf16[176,576]{1,0:T(8,128)(2,1)S(1)}, u32[]{:S(2)}, u32[]{:S(2)}) collective-permute-start(bf16[176,576]{1,0:T(8,128)(2,1)S(1)} %get-tuple-element.182), channel_id=1, source_target_pairs={{0,2},{1,3},{4,0},{5,1},{8,4},{9,5},{12,8},{13,9},{14,12},{15,13},... | collective-permute-start | bytes 608264 | tf_op jit(solution)/shard_map/ppermute | solution.py:80
  129.7 2.7 %collective-permute-done.53.got_ref = bf16[192,1344]{1,0:T(8,128)(2,1)S(1)} collective-permute-done((bf16[192,1344]{1,0:T(8,128)(2,1)S(1)}, bf16[192,1344]{1,0:T(8,128)(2,1)S(1)}, u32[]{:S(2)}, u32[]{:S(2)}) %collective-permute-start.53) | collective-permute-done | bytes 516128 | tf_op jit(solution)/shard_map/ppermute | solution.py:87
  (138 shorter events, 64.3 us)
Async XLA Ops:
  2.4 8.5 %collective-permute-start = (bf16[176,576]{1,0:T(8,128)(2,1)S(1)}, bf16[176,576]{1,0:T(8,128)(2,1)S(1)}, u32[]{:S(2)}, u32[]{:S(2)}) collective-permute-start(bf16[176,576]{1,0:T(8,128)(2,1)S(1)} %maximum_maximum_fusion.refs_0_), channel_id=1, source_target_pairs={{0,4},{1,5},{4,8},{5,9},{8,12},{9,13},{12,14},{13,15},{14,10},{15,... | collective-permute-start | bytes 608264 | tf_op jit(solution)/shard_map/ppermute | solution.py:77
  5.5 7.0 %collective-permute-start.1 = (bf16[176,576]{1,0:T(8,128)(2,1)S(1)}, bf16[176,576]{1,0:T(8,128)(2,1)S(1)}, u32[]{:S(2)}, u32[]{:S(2)}) collective-permute-start(bf16[176,576]{1,0:T(8,128)(2,1)S(1)} %maximum_maximum_fusion.refs_0_), channel_id=1, source_target_pairs={{0,2},{1,3},{4,0},{5,1},{8,4},{9,5},{12,8},{13,9},{14,12},{15,13},... | collective-permute-start | bytes 608264 | tf_op jit(solution)/shard_map/ppermute | solution.py:80
  20.6 7.2 %collective-permute-start.16 = (bf16[176,576]{1,0:T(8,128)(2,1)S(1)}, bf16[176,576]{1,0:T(8,128)(2,1)S(1)}, u32[]{:S(2)}, u32[]{:S(2)}) collective-permute-start(bf16[176,576]{1,0:T(8,128)(2,1)S(1)} %collective-permute-done.refs_8_), channel_id=1, source_target_pairs={{0,1},{1,0},{2,3},{3,2},{4,5},{5,4},{6,7},{7,6},{8,9},{9,8},{10,11... | collective-permute-start | bytes 608264 | tf_op jit(solution)/shard_map/ppermute | solution.py:83
  21.1 7.1 %collective-permute-start.9 = (bf16[176,576]{1,0:T(8,128)(2,1)S(1)}, bf16[176,576]{1,0:T(8,128)(2,1)S(1)}, u32[]{:S(2)}, u32[]{:S(2)}) collective-permute-start(bf16[176,576]{1,0:T(8,128)(2,1)S(1)} %collective-permute-done.1.refs_1_), channel_id=1, source_target_pairs={{0,1},{1,0},{2,3},{3,2},{4,5},{5,4},{6,7},{7,6},{8,9},{9,8},{10,11... | collective-permute-start | bytes 608264 | tf_op jit(solution)/shard_map/ppermute | solution.py:83
  26.1 7.2 %collective-permute-start.15 = (bf16[176,576]{1,0:T(8,128)(2,1)S(1)}, bf16[176,576]{1,0:T(8,128)(2,1)S(1)}, u32[]{:S(2)}, u32[]{:S(2)}) collective-permute-start(bf16[176,576]{1,0:T(8,128)(2,1)S(1)} %collective-permute-done.4.refs_7_), channel_id=1, source_target_pairs={{0,1},{1,0},{2,3},{3,2},{4,5},{5,4},{6,7},{7,6},{8,9},{9,8},{10,11... | collective-permute-start | bytes 608264 | tf_op jit(solution)/shard_map/ppermute | solution.py:83
  26.1 6.7 %collective-permute-start.6 = (bf16[96,576]{1,0:T(8,128)(2,1)S(1)}, bf16[96,576]{1,0:T(8,128)(2,1)S(1)}, u32[]{:S(2)}, u32[]{:S(2)}) collective-permute-start(bf16[96,576]{1,0:T(8,128)(2,1)S(1)} %slice.82), channel_id=1, source_target_pairs={{0,4},{1,5},{4,8},{5,9},{8,12},{9,13},{12,14},{13,15},{14,10},{15,... | collective-permute-start | bytes 331784 | tf_op jit(solution)/shard_map/ppermute | solution.py:77
  43.4 7.1 %collective-permute-start.18 = (bf16[192,576]{1,0:T(8,128)(2,1)S(1)}, bf16[192,576]{1,0:T(8,128)(2,1)S(1)}, u32[]{:S(2)}, u32[]{:S(2)}) collective-permute-start(bf16[192,576]{1,0:T(8,128)(2,1)S(1)} %get-tuple-element.105.refs_0_.mo_ref), channel_id=1, source_target_pairs={{0,16},{16,0},{1,17},{17,1},{2,18},{18,2},{3,19},{19,3},{4,20},{20... | collective-permute-start | bytes 663560 | tf_op jit(solution)/shard_map/ppermute | solution.py:87
  45.0 7.1 %collective-permute-start.22 = (bf16[192,576]{1,0:T(8,128)(2,1)S(1)}, bf16[192,576]{1,0:T(8,128)(2,1)S(1)}, u32[]{:S(2)}, u32[]{:S(2)}) collective-permute-start(bf16[192,576]{1,0:T(8,128)(2,1)S(1)} %get-tuple-element.107.refs_4_), channel_id=1, source_target_pairs={{0,4},{1,5},{4,8},{5,9},{8,12},{9,13},{12,14},{13,15},{14,10},{15,... | collective-permute-start | bytes 663560 | tf_op jit(solution)/shard_map/ppermute | solution.py:77
  53.0 8.2 %collective-permute-start.24 = (bf16[192,576]{1,0:T(8,128)(2,1)S(1)}, bf16[192,576]{1,0:T(8,128)(2,1)S(1)}, u32[]{:S(2)}, u32[]{:S(2)}) collective-permute-start(bf16[192,576]{1,0:T(8,128)(2,1)S(1)} %collective-permute-done.18.refs_5_), channel_id=1, source_target_pairs={{0,4},{1,5},{4,8},{5,9},{8,12},{9,13},{12,14},{13,15},{14,10},{15,... | collective-permute-start | bytes 663560 | tf_op jit(solution)/shard_map/ppermute | solution.py:77
  53.6 8.2 %collective-permute-start.25 = (bf16[192,576]{1,0:T(8,128)(2,1)S(1)}, bf16[192,576]{1,0:T(8,128)(2,1)S(1)}, u32[]{:S(2)}, u32[]{:S(2)}) collective-permute-start(bf16[192,576]{1,0:T(8,128)(2,1)S(1)} %collective-permute-done.18.refs_5_), channel_id=1, source_target_pairs={{0,2},{1,3},{4,0},{5,1},{8,4},{9,5},{12,8},{13,9},{14,12},{15,13},... | collective-permute-start | bytes 663560 | tf_op jit(solution)/shard_map/ppermute | solution.py:80
  55.0 8.8 %collective-permute-start.26 = (bf16[192,576]{1,0:T(8,128)(2,1)S(1)}, bf16[192,576]{1,0:T(8,128)(2,1)S(1)}, u32[]{:S(2)}, u32[]{:S(2)}) collective-permute-start(bf16[192,576]{1,0:T(8,128)(2,1)S(1)} %collective-permute-done.22.refs_4_), channel_id=1, source_target_pairs={{0,4},{1,5},{4,8},{5,9},{8,12},{9,13},{12,14},{13,15},{14,10},{15,... | collective-permute-start | bytes 663560 | tf_op jit(solution)/shard_map/ppermute | solution.py:77
  55.6 8.8 %collective-permute-start.27 = (bf16[192,576]{1,0:T(8,128)(2,1)S(1)}, bf16[192,576]{1,0:T(8,128)(2,1)S(1)}, u32[]{:S(2)}, u32[]{:S(2)}) collective-permute-start(bf16[192,576]{1,0:T(8,128)(2,1)S(1)} %collective-permute-done.23.refs_5_), channel_id=1, source_target_pairs={{0,2},{1,3},{4,0},{5,1},{8,4},{9,5},{12,8},{13,9},{14,12},{15,13},... | collective-permute-start | bytes 663560 | tf_op jit(solution)/shard_map/ppermute | solution.py:80
  57.0 9.4 %collective-permute-start.20 = (bf16[192,576]{1,0:T(8,128)(2,1)S(1)}, bf16[192,576]{1,0:T(8,128)(2,1)S(1)}, u32[]{:S(2)}, u32[]{:S(2)}) collective-permute-start(bf16[192,576]{1,0:T(8,128)(2,1)S(1)} %get-tuple-element.105.refs_0_.mo_ref), channel_id=1, source_target_pairs={{0,1},{1,0},{2,3},{3,2},{4,5},{5,4},{6,7},{7,6},{8,9},{9,8},{10,11... | collective-permute-start | bytes 663560 | tf_op jit(solution)/shard_map/ppermute | solution.py:83
  64.4 8.4 %collective-permute-start.28 = (bf16[192,576]{1,0:T(8,128)(2,1)S(1)}, bf16[192,576]{1,0:T(8,128)(2,1)S(1)}, u32[]{:S(2)}, u32[]{:S(2)}) collective-permute-start(bf16[192,576]{1,0:T(8,128)(2,1)S(1)} %collective-permute-done.24.refs_6_), channel_id=1, source_target_pairs={{0,4},{1,5},{4,8},{5,9},{8,12},{9,13},{12,14},{13,15},{14,10},{15,... | collective-permute-start | bytes 663560 | tf_op jit(solution)/shard_map/ppermute | solution.py:77
  65.0 8.3 %collective-permute-start.29 = (bf16[192,576]{1,0:T(8,128)(2,1)S(1)}, bf16[192,576]{1,0:T(8,128)(2,1)S(1)}, u32[]{:S(2)}, u32[]{:S(2)}) collective-permute-start(bf16[192,576]{1,0:T(8,128)(2,1)S(1)} %collective-permute-done.25.refs_7_), channel_id=1, source_target_pairs={{0,2},{1,3},{4,0},{5,1},{8,4},{9,5},{12,8},{13,9},{14,12},{15,13},... | collective-permute-start | bytes 663560 | tf_op jit(solution)/shard_map/ppermute | solution.py:80
  68.0 7.4 %collective-permute-start.30 = (bf16[192,576]{1,0:T(8,128)(2,1)S(1)}, bf16[192,576]{1,0:T(8,128)(2,1)S(1)}, u32[]{:S(2)}, u32[]{:S(2)}) collective-permute-start(bf16[192,576]{1,0:T(8,128)(2,1)S(1)} %collective-permute-done.26.refs_4_), channel_id=1, source_target_pairs={{0,4},{1,5},{4,8},{5,9},{8,12},{9,13},{12,14},{13,15},{14,10},{15,... | collective-permute-start | bytes 663560 | tf_op jit(solution)/shard_map/ppermute | solution.py:77
  68.7 7.3 %collective-permute-start.31 = (bf16[192,576]{1,0:T(8,128)(2,1)S(1)}, bf16[192,576]{1,0:T(8,128)(2,1)S(1)}, u32[]{:S(2)}, u32[]{:S(2)}) collective-permute-start(bf16[192,576]{1,0:T(8,128)(2,1)S(1)} %collective-permute-done.27.refs_5_), channel_id=1, source_target_pairs={{0,2},{1,3},{4,0},{5,1},{8,4},{9,5},{12,8},{13,9},{14,12},{15,13},... | collective-permute-start | bytes 663560 | tf_op jit(solution)/shard_map/ppermute | solution.py:80
  82.8 11.7 %collective-permute-start.38 = (f32[192,1152]{1,0:T(8,128)S(1)}, f32[192,1152]{1,0:T(8,128)S(1)}, u32[]{:S(2)}, u32[]{:S(2)}) collective-permute-start(f32[192,1152]{1,0:T(8,128)S(1)} %get-tuple-element.146), channel_id=1, source_target_pairs={{0,1},{1,0},{2,3},{3,2},{4,5},{5,4},{6,7},{7,6},{8,9},{9,8},{10,11... | collective-permute-start | bytes 2654216 | tf_op jit(solution)/shard_map/ppermute | solution.py:83
  95.8 8.1 %collective-permute-start.40 = (bf16[192,576]{1,0:T(8,128)(2,1)S(1)}, bf16[192,576]{1,0:T(8,128)(2,1)S(1)}, u32[]{:S(2)}, u32[]{:S(2)}) collective-permute-start(bf16[192,576]{1,0:T(8,128)(2,1)S(1)} %get-tuple-element.150), channel_id=1, source_target_pairs={{0,16},{16,0},{1,17},{17,1},{2,18},{18,2},{3,19},{19,3},{4,20},{20... | collective-permute-start | bytes 663560 | tf_op jit(solution)/shard_map/ppermute | solution.py:87
  96.3 7.6 %collective-permute-start.43 = (bf16[8,96,192]{2,1,0:T(8,128)(2,1)S(1)}, bf16[8,96,192]{2,1,0:T(8,128)(2,1)S(1)}, u32[]{:S(2)}, u32[]{:S(2)}) collective-permute-start(bf16[8,96,192]{2,1,0:T(8,128)(2,1)S(1)} %copy-done.6), channel_id=1, source_target_pairs={{0,1},{1,0},{2,3},{3,2},{4,5},{5,4},{6,7},{7,6},{8,9},{9,8},{10,11... | collective-permute-start | bytes 884744 | tf_op jit(solution)/shard_map/ppermute | solution.py:83
  96.3 7.6 %collective-permute-start.44 = (bf16[8,80,192]{2,1,0:T(8,128)(2,1)S(1)}, bf16[8,80,192]{2,1,0:T(8,128)(2,1)S(1)}, u32[]{:S(2)}, u32[]{:S(2)}) collective-permute-start(bf16[8,80,192]{2,1,0:T(8,128)(2,1)S(1)} %copy-done.8), channel_id=1, source_target_pairs={{0,1},{1,0},{2,3},{3,2},{4,5},{5,4},{6,7},{7,6},{8,9},{9,8},{10,11... | collective-permute-start | bytes 737288 | tf_op jit(solution)/shard_map/ppermute | solution.py:83
  96.8 7.1 %collective-permute-start.41 = (bf16[192,576]{1,0:T(8,128)(2,1)S(1)}, bf16[192,576]{1,0:T(8,128)(2,1)S(1)}, u32[]{:S(2)}, u32[]{:S(2)}) collective-permute-start(bf16[192,576]{1,0:T(8,128)(2,1)S(1)} %get-tuple-element.166.do_ref), channel_id=1, source_target_pairs={{0,1},{1,0},{2,3},{3,2},{4,5},{5,4},{6,7},{7,6},{8,9},{9,8},{10,11... | collective-permute-start | bytes 663560 | tf_op jit(solution)/shard_map/ppermute | solution.py:83
  111.6 6.8 %collective-permute-start.48 = (bf16[176,576]{1,0:T(8,128)(2,1)S(1)}, bf16[176,576]{1,0:T(8,128)(2,1)S(1)}, u32[]{:S(2)}, u32[]{:S(2)}) collective-permute-start(bf16[176,576]{1,0:T(8,128)(2,1)S(1)} %pad_maximum_fusion.1), channel_id=1, source_target_pairs={{0,2},{1,3},{4,0},{5,1},{8,4},{9,5},{12,8},{13,9},{14,12},{15,13},... | collective-permute-start | bytes 608264 | tf_op jit(solution)/shard_map/ppermute | solution.py:80
  120.0 12.3 %collective-permute-start.53 = (bf16[192,1344]{1,0:T(8,128)(2,1)S(1)}, bf16[192,1344]{1,0:T(8,128)(2,1)S(1)}, u32[]{:S(2)}, u32[]{:S(2)}) collective-permute-start(bf16[192,1344]{1,0:T(8,128)(2,1)S(1)} %get-tuple-element.175), channel_id=1, source_target_pairs={{0,16},{16,0},{1,17},{17,1},{2,18},{18,2},{3,19},{19,3},{4,20},{20... | collective-permute-start | bytes 1548296 | tf_op jit(solution)/shard_map/ppermute | solution.py:87
  (39 other events, 207.7 us)

commit v5 on v4

--- a/solution.py
+++ b/solution.py
@@ -336,16 +336,13 @@
     for k in range(1, h + 1):
         if k == h:
             fa, ba, fc, bc = fa[:cut], ba[cut:], fc[:cut], bc[cut:]
-        if k > 2 or k == h:
-            j = k - 3
-            if j >= 0:
-                acc = add(acc, (0, 1), chunks[j], first=j == 0)
-                fa, ba, *acc = tie((fa, ba, *acc))
+        if 2 < k < h:
+            acc = add(acc, (0, 1), chunks[k - 3], first=k == 3)
+            fa, ba, *acc = tie((fa, ba, *acc))
         fa, ba = ring.right(fa), ring.left(ba)
-        if k < h:
-            fc, bc, fa, ba = tie((fc, bc, fa, ba))
-        if k == h:
-            acc = add(acc, (0, 1), chunks[h - 2], first=h == 2)
+        fc, bc, fa, ba = tie((fc, bc, fa, ba))
+        if k > max(1, h - 2):
+            acc = add(acc, (0, 1), chunks[k - 2], first=k == 2)
             fc, bc, *acc = tie((fc, bc, *acc))
         fc, bc = ring.right(fc), ring.left(bc)
         chunks.append([fa, ba, fc, bc])

time: 135 us -> 134 us (level)
    ppermute x16, waiting for transfers between devices: 29.6 us -> 28 us  [right(): return lax.ppermute(x, 'batch', self.fwd)]
where the time goes in v5:
time: 134 us
  waiting for transfers between devices  61.6 us (46%)
  starting transfers between devices  41.9 us (31%)
  Pallas kernels  21.2 us (16%)
  local copies, waits for them, and re-layouts  4.83 us (4%)
  other arithmetic  2.94 us (2%)
  between operations  1.58 us (1%)
    ppermute x16, waiting for transfers between devices, right(): return lax.ppermute(x, 'batch', self.fwd)  28 us
    pallas_call x13, Pallas kernels, call(): pl.pallas_call(body, out_shape=[jax.ShapeDtypeStruct(s, t) for s, t in ou...  21.2 us
    ppermute x16, starting transfers between devices, left(): return lax.ppermute(x, 'batch', self.bwd)  18.9 us
    ppermute x16, waiting for transfers between devices, left(): return lax.ppermute(x, 'batch', self.bwd)  15.7 us
    ppermute x16, starting transfers between devices, right(): return lax.ppermute(x, 'batch', self.fwd)  15 us
    ppermute x5, waiting for transfers between devices, swap(): return lax.ppermute(x, 'tower', [(0, 1), (1, 0)])  15 us
    ppermute x5, starting transfers between devices, swap(): return lax.ppermute(x, 'tower', [(0, 1), (1, 0)])  5.78 us
    unnamed x18, local copies, waits for them, and re-layouts  4.65 us
  transfers between devices with their start and end apart: 54, of which 35 were waited for; matrix products, arithmetic and copies ran while one was open for 0% of the time, Pallas kernels for 11%

profile of v5, /device:TPU:0, one launch (start us, length us, event | category | flops | bytes accessed | tf_op | source)
XLA Modules:
  0.0 134.0 jit_solution(10194546612810591298)
XLA Ops:
  2.4 3.1 %collective-permute-start = (bf16[176,576]{1,0:T(8,128)(2,1)S(1)}, bf16[176,576]{1,0:T(8,128)(2,1)S(1)}, u32[]{:S(2)}, u32[]{:S(2)}) collective-permute-start(bf16[176,576]{1,0:T(8,128)(2,1)S(1)} %maximum_maximum_fusion.refs_0_), channel_id=1, source_target_pairs={{0,4},{1,5},{4,8},{5,9},{8,12},{9,13},{12,14},{13,15},{14,10},{15,... | collective-permute-start | bytes 608264 | tf_op jit(solution)/shard_map/ppermute | solution.py:77
  14.5 4.0 %collective-permute-done.4.refs_7_ = bf16[176,576]{1,0:T(8,128)(2,1)S(1)} collective-permute-done((bf16[176,576]{1,0:T(8,128)(2,1)S(1)}, bf16[176,576]{1,0:T(8,128)(2,1)S(1)}, u32[]{:S(2)}, u32[]{:S(2)}) %collective-permute-start.4) | collective-permute-done | bytes 202784 | tf_op jit(solution)/shard_map/ppermute | solution.py:77
  21.1 3.4 %collective-permute-done.5.refs_6_ = bf16[176,576]{1,0:T(8,128)(2,1)S(1)} collective-permute-done((bf16[176,576]{1,0:T(8,128)(2,1)S(1)}, bf16[176,576]{1,0:T(8,128)(2,1)S(1)}, u32[]{:S(2)}, u32[]{:S(2)}) %collective-permute-start.5) | collective-permute-done | bytes 202784 | tf_op jit(solution)/shard_map/ppermute | solution.py:77
  26.1 1.6 %collective-permute-start.6 = (bf16[96,576]{1,0:T(8,128)(2,1)S(1)}, bf16[96,576]{1,0:T(8,128)(2,1)S(1)}, u32[]{:S(2)}, u32[]{:S(2)}) collective-permute-start(bf16[96,576]{1,0:T(8,128)(2,1)S(1)} %slice.82), channel_id=1, source_target_pairs={{0,4},{1,5},{4,8},{5,9},{8,12},{9,13},{12,14},{13,15},{14,10},{15,... | collective-permute-start | bytes 331784 | tf_op jit(solution)/shard_map/ppermute | solution.py:77
  28.7 4.0 %collective-permute-done.7.refs_5_ = bf16[80,576]{1,0:T(8,128)(2,1)S(1)} collective-permute-done((bf16[80,576]{1,0:T(8,128)(2,1)S(1)}, bf16[80,576]{1,0:T(8,128)(2,1)S(1)}, u32[]{:S(2)}, u32[]{:S(2)}) %collective-permute-start.7) | collective-permute-done | bytes 92192 | tf_op jit(solution)/shard_map/ppermute | solution.py:80
  35.3 3.5 %shard_map.85 = (bf16[16,96,576]{2,1,0:T(8,128)(2,1)}, bf16[16,80,576]{2,1,0:T(8,128)(2,1)}, f32[192,576]{1,0:T(8,128)S(1)}, f32[192,576]{1,0:T(8,128)S(1)}, f32[8,192]{1,0:T(8,128)S(1)}, /*index=5*/f32[8,128]{1,0:T(8,128)S(1)}) custom-call(s32[2,8]{1,0:T(2,128)S(1)} %pad_add_fusion.slot_ref, bf16[192,1536]{1,0:T(8,128)(2,1)S(1)} %copy-done.1, ...), custom_call_target="tpu_custom_call" | custom-call | flops 800000000 | bytes 4325376 | tf_op jit(solution)/shard_map/pallas_call | solution.py:37
  40.5 2.0 %collective-permute-done.17.got_ref = f32[8,192]{1,0:T(8,128)S(1)} collective-permute-done((f32[8,192]{1,0:T(8,128)S(1)}, f32[8,192]{1,0:T(8,128)S(1)}, u32[]{:S(2)}, u32[]{:S(2)}) %collective-permute-start.17) | collective-permute-done | bytes 6176 | tf_op jit(solution)/shard_map/ppermute | solution.py:87
  43.4 1.6 %collective-permute-start.18 = (bf16[192,576]{1,0:T(8,128)(2,1)S(1)}, bf16[192,576]{1,0:T(8,128)(2,1)S(1)}, u32[]{:S(2)}, u32[]{:S(2)}) collective-permute-start(bf16[192,576]{1,0:T(8,128)(2,1)S(1)} %get-tuple-element.109.refs_0_.mo_ref), channel_id=1, source_target_pairs={{0,16},{16,0},{1,17},{17,1},{2,18},{18,2},{3,19},{19,3},{4,20},{20... | collective-permute-start | bytes 663560 | tf_op jit(solution)/shard_map/ppermute | solution.py:87
  47.0 3.5 %collective-permute-done.18.refs_5_ = bf16[192,576]{1,0:T(8,128)(2,1)S(1)} collective-permute-done((bf16[192,576]{1,0:T(8,128)(2,1)S(1)}, bf16[192,576]{1,0:T(8,128)(2,1)S(1)}, u32[]{:S(2)}, u32[]{:S(2)}) %collective-permute-start.18) | collective-permute-done | bytes 221216 | tf_op jit(solution)/shard_map/ppermute | solution.py:87
  57.0 4.2 %collective-permute-done.24.refs_6_ = bf16[192,576]{1,0:T(8,128)(2,1)S(1)} collective-permute-done((bf16[192,576]{1,0:T(8,128)(2,1)S(1)}, bf16[192,576]{1,0:T(8,128)(2,1)S(1)}, u32[]{:S(2)}, u32[]{:S(2)}) %collective-permute-start.24) | collective-permute-done | bytes 221216 | tf_op jit(solution)/shard_map/ppermute | solution.py:77
  61.8 2.1 %collective-permute-done.26.refs_4_ = bf16[192,576]{1,0:T(8,128)(2,1)S(1)} collective-permute-done((bf16[192,576]{1,0:T(8,128)(2,1)S(1)}, bf16[192,576]{1,0:T(8,128)(2,1)S(1)}, u32[]{:S(2)}, u32[]{:S(2)}) %collective-permute-start.26) | collective-permute-done | bytes 221216 | tf_op jit(solution)/shard_map/ppermute | solution.py:77
  66.4 1.6 %shard_map.87 = (f32[192,1152]{1,0:T(8,128)S(1)}, f32[192,1152]{1,0:T(8,128)S(1)}) custom-call(bf16[192,576]{1,0:T(8,128)(2,1)S(1)} %get-tuple-element.109.refs_0_.mo_ref, bf16[192,576]{1,0:T(8,128)(2,1)S(1)} %collective-permute-done.19.refs_1_.mx_ref, bf16[192,576]{1,0:T(8,128)(2,1)S(1)} %collective-permute-done.20.refs_2_.refs_0_, ...), custom_call_target="tpu_custom_call" | custom-call | flops 440000000 | bytes 1327104 | tf_op jit(solution)/shard_map/pallas_call | solution.py:37
  70.1 2.1 %shard_map.88 = (f32[192,1152]{1,0:T(8,128)S(1)}, f32[192,1152]{1,0:T(8,128)S(1)}) custom-call(bf16[192,576]{1,0:T(8,128)(2,1)S(1)} %get-tuple-element.109.refs_0_.mo_ref, bf16[192,576]{1,0:T(8,128)(2,1)S(1)} %collective-permute-done.19.refs_1_.mx_ref, ...), custom_call_target="tpu_custom_call", output_to_operand_aliasing={{0}: (8, {}), {1}: (9, {})} | custom-call | flops 440000000 | bytes 3538944 | tf_op jit(solution)/shard_map/pallas_call | solution.py:37
  73.3 2.1 %collective-permute-done.30.refs_2_ = bf16[192,576]{1,0:T(8,128)(2,1)S(1)} collective-permute-done((bf16[192,576]{1,0:T(8,128)(2,1)S(1)}, bf16[192,576]{1,0:T(8,128)(2,1)S(1)}, u32[]{:S(2)}, u32[]{:S(2)}) %collective-permute-start.30) | collective-permute-done | bytes 221216 | tf_op jit(solution)/shard_map/ppermute | solution.py:77
  80.1 2.1 %shard_map.89 = (f32[192,1152]{1,0:T(8,128)S(1)}, f32[192,1152]{1,0:T(8,128)S(1)}) custom-call(bf16[192,576]{1,0:T(8,128)(2,1)S(1)} %get-tuple-element.109.refs_0_.mo_ref, bf16[192,576]{1,0:T(8,128)(2,1)S(1)} %collective-permute-done.19.refs_1_.mx_ref, ...), custom_call_target="tpu_custom_call", output_to_operand_aliasing={{0}: (8, {}), {1}: (9, {})} | custom-call | flops 440000000 | bytes 3538944 | tf_op jit(solution)/shard_map/pallas_call | solution.py:37
  86.1 3.7 %collective-permute-done.36.refs_8_ = bf16[96,576]{1,0:T(8,128)(2,1)S(1)} collective-permute-done((bf16[96,576]{1,0:T(8,128)(2,1)S(1)}, bf16[96,576]{1,0:T(8,128)(2,1)S(1)}, u32[]{:S(2)}, u32[]{:S(2)}) %collective-permute-start.36) | collective-permute-done | bytes 110624 | tf_op jit(solution)/shard_map/ppermute | solution.py:77
  95.6 7.0 %collective-permute-done.40.dg_ref = bf16[192,576]{1,0:T(8,128)(2,1)S(1)} collective-permute-done((bf16[192,576]{1,0:T(8,128)(2,1)S(1)}, bf16[192,576]{1,0:T(8,128)(2,1)S(1)}, u32[]{:S(2)}, u32[]{:S(2)}) %collective-permute-start.40) | collective-permute-done | bytes 221216 | tf_op jit(solution)/shard_map/ppermute | solution.py:87
  105.3 1.6 %collective-permute-start.47 = (bf16[80,576]{1,0:T(8,128)(2,1)S(1)}, bf16[80,576]{1,0:T(8,128)(2,1)S(1)}, u32[]{:S(2)}, u32[]{:S(2)}) collective-permute-start(bf16[80,576]{1,0:T(8,128)(2,1)S(1)} %get-tuple-element.173), channel_id=1, source_target_pairs={{0,2},{1,3},{4,0},{5,1},{8,4},{9,5},{12,8},{13,9},{14,12},{15,13},... | collective-permute-start | bytes 276488 | tf_op jit(solution)/shard_map/ppermute | solution.py:80
  107.4 2.9 %collective-permute-done.47 = bf16[80,576]{1,0:T(8,128)(2,1)S(1)} collective-permute-done((bf16[80,576]{1,0:T(8,128)(2,1)S(1)}, bf16[80,576]{1,0:T(8,128)(2,1)S(1)}, u32[]{:S(2)}, u32[]{:S(2)}) %collective-permute-start.47) | collective-permute-done | bytes 92192 | tf_op jit(solution)/shard_map/ppermute | solution.py:80
  110.3 1.6 %collective-permute-start.48 = (bf16[176,576]{1,0:T(8,128)(2,1)S(1)}, bf16[176,576]{1,0:T(8,128)(2,1)S(1)}, u32[]{:S(2)}, u32[]{:S(2)}) collective-permute-start(bf16[176,576]{1,0:T(8,128)(2,1)S(1)} %pad_maximum_fusion.1), channel_id=1, source_target_pairs={{0,2},{1,3},{4,0},{5,1},{8,4},{9,5},{12,8},{13,9},{14,12},{15,13},... | collective-permute-start | bytes 608264 | tf_op jit(solution)/shard_map/ppermute | solution.py:80
  112.6 2.5 %shard_map.95 = (f32[192,1344]{1,0:T(8,128)S(1)}, bf16[192,1344]{1,0:T(8,128)(2,1)S(1)}) custom-call(s32[2]{0:T(128)S(1)} %pad_add_fusion.1.s_ref, bf16[192,576]{1,0:T(8,128)(2,1)S(1)} %get-tuple-element.174.do_ref, bf16[192,576]{1,0:T(8,128)(2,1)S(1)} %collective-permute-done.40.dg_ref, bf16[16,96,576]{2,1,0:T(8,128)(2,1)S(1)} %copy-done.2, ...), custom_call_target="tpu_custom_call" | custom-call | flops 600000000 | bytes 3686400 | tf_op jit(solution)/shard_map/pallas_call | solution.py:37
  121.2 4.3 %collective-permute-done.49 = bf16[176,576]{1,0:T(8,128)(2,1)S(1)} collective-permute-done((bf16[176,576]{1,0:T(8,128)(2,1)S(1)}, bf16[176,576]{1,0:T(8,128)(2,1)S(1)}, u32[]{:S(2)}, u32[]{:S(2)}) %collective-permute-start.49) | collective-permute-done | bytes 202784 | tf_op jit(solution)/shard_map/ppermute | solution.py:77
  126.5 2.0 %collective-permute-start.52 = (bf16[176,576]{1,0:T(8,128)(2,1)S(1)}, bf16[176,576]{1,0:T(8,128)(2,1)S(1)}, u32[]{:S(2)}, u32[]{:S(2)}) collective-permute-start(bf16[176,576]{1,0:T(8,128)(2,1)S(1)} %get-tuple-element.190), channel_id=1, source_target_pairs={{0,2},{1,3},{4,0},{5,1},{8,4},{9,5},{12,8},{13,9},{14,12},{15,13},... | collective-permute-start | bytes 608264 | tf_op jit(solution)/shard_map/ppermute | solution.py:80
  128.5 2.5 %collective-permute-done.53.got_ref = bf16[192,1344]{1,0:T(8,128)(2,1)S(1)} collective-permute-done((bf16[192,1344]{1,0:T(8,128)(2,1)S(1)}, bf16[192,1344]{1,0:T(8,128)(2,1)S(1)}, u32[]{:S(2)}, u32[]{:S(2)}) %collective-permute-start.53) | collective-permute-done | bytes 516128 | tf_op jit(solution)/shard_map/ppermute | solution.py:87
  (138 shorter events, 63.3 us)
Async XLA Ops:
  2.4 8.5 %collective-permute-start = (bf16[176,576]{1,0:T(8,128)(2,1)S(1)}, bf16[176,576]{1,0:T(8,128)(2,1)S(1)}, u32[]{:S(2)}, u32[]{:S(2)}) collective-permute-start(bf16[176,576]{1,0:T(8,128)(2,1)S(1)} %maximum_maximum_fusion.refs_0_), channel_id=1, source_target_pairs={{0,4},{1,5},{4,8},{5,9},{8,12},{9,13},{12,14},{13,15},{14,10},{15,... | collective-permute-start | bytes 608264 | tf_op jit(solution)/shard_map/ppermute | solution.py:77
  5.5 7.0 %collective-permute-start.1 = (bf16[176,576]{1,0:T(8,128)(2,1)S(1)}, bf16[176,576]{1,0:T(8,128)(2,1)S(1)}, u32[]{:S(2)}, u32[]{:S(2)}) collective-permute-start(bf16[176,576]{1,0:T(8,128)(2,1)S(1)} %maximum_maximum_fusion.refs_0_), channel_id=1, source_target_pairs={{0,2},{1,3},{4,0},{5,1},{8,4},{9,5},{12,8},{13,9},{14,12},{15,13},... | collective-permute-start | bytes 608264 | tf_op jit(solution)/shard_map/ppermute | solution.py:80
  20.6 7.2 %collective-permute-start.16 = (bf16[176,576]{1,0:T(8,128)(2,1)S(1)}, bf16[176,576]{1,0:T(8,128)(2,1)S(1)}, u32[]{:S(2)}, u32[]{:S(2)}) collective-permute-start(bf16[176,576]{1,0:T(8,128)(2,1)S(1)} %collective-permute-done.refs_8_), channel_id=1, source_target_pairs={{0,1},{1,0},{2,3},{3,2},{4,5},{5,4},{6,7},{7,6},{8,9},{9,8},{10,11... | collective-permute-start | bytes 608264 | tf_op jit(solution)/shard_map/ppermute | solution.py:83
  21.1 7.1 %collective-permute-start.9 = (bf16[176,576]{1,0:T(8,128)(2,1)S(1)}, bf16[176,576]{1,0:T(8,128)(2,1)S(1)}, u32[]{:S(2)}, u32[]{:S(2)}) collective-permute-start(bf16[176,576]{1,0:T(8,128)(2,1)S(1)} %collective-permute-done.1.refs_1_), channel_id=1, source_target_pairs={{0,1},{1,0},{2,3},{3,2},{4,5},{5,4},{6,7},{7,6},{8,9},{9,8},{10,11... | collective-permute-start | bytes 608264 | tf_op jit(solution)/shard_map/ppermute | solution.py:83
  26.1 7.2 %collective-permute-start.15 = (bf16[176,576]{1,0:T(8,128)(2,1)S(1)}, bf16[176,576]{1,0:T(8,128)(2,1)S(1)}, u32[]{:S(2)}, u32[]{:S(2)}) collective-permute-start(bf16[176,576]{1,0:T(8,128)(2,1)S(1)} %collective-permute-done.4.refs_7_), channel_id=1, source_target_pairs={{0,1},{1,0},{2,3},{3,2},{4,5},{5,4},{6,7},{7,6},{8,9},{9,8},{10,11... | collective-permute-start | bytes 608264 | tf_op jit(solution)/shard_map/ppermute | solution.py:83
  26.1 6.7 %collective-permute-start.6 = (bf16[96,576]{1,0:T(8,128)(2,1)S(1)}, bf16[96,576]{1,0:T(8,128)(2,1)S(1)}, u32[]{:S(2)}, u32[]{:S(2)}) collective-permute-start(bf16[96,576]{1,0:T(8,128)(2,1)S(1)} %slice.82), channel_id=1, source_target_pairs={{0,4},{1,5},{4,8},{5,9},{8,12},{9,13},{12,14},{13,15},{14,10},{15,... | collective-permute-start | bytes 331784 | tf_op jit(solution)/shard_map/ppermute | solution.py:77
  43.4 7.1 %collective-permute-start.18 = (bf16[192,576]{1,0:T(8,128)(2,1)S(1)}, bf16[192,576]{1,0:T(8,128)(2,1)S(1)}, u32[]{:S(2)}, u32[]{:S(2)}) collective-permute-start(bf16[192,576]{1,0:T(8,128)(2,1)S(1)} %get-tuple-element.109.refs_0_.mo_ref), channel_id=1, source_target_pairs={{0,16},{16,0},{1,17},{17,1},{2,18},{18,2},{3,19},{19,3},{4,20},{20... | collective-permute-start | bytes 663560 | tf_op jit(solution)/shard_map/ppermute | solution.py:87
  45.0 7.1 %collective-permute-start.22 = (bf16[192,576]{1,0:T(8,128)(2,1)S(1)}, bf16[192,576]{1,0:T(8,128)(2,1)S(1)}, u32[]{:S(2)}, u32[]{:S(2)}) collective-permute-start(bf16[192,576]{1,0:T(8,128)(2,1)S(1)} %get-tuple-element.111.refs_4_), channel_id=1, source_target_pairs={{0,4},{1,5},{4,8},{5,9},{8,12},{9,13},{12,14},{13,15},{14,10},{15,... | collective-permute-start | bytes 663560 | tf_op jit(solution)/shard_map/ppermute | solution.py:77
  53.0 8.2 %collective-permute-start.24 = (bf16[192,576]{1,0:T(8,128)(2,1)S(1)}, bf16[192,576]{1,0:T(8,128)(2,1)S(1)}, u32[]{:S(2)}, u32[]{:S(2)}) collective-permute-start(bf16[192,576]{1,0:T(8,128)(2,1)S(1)} %collective-permute-done.18.refs_5_), channel_id=1, source_target_pairs={{0,4},{1,5},{4,8},{5,9},{8,12},{9,13},{12,14},{13,15},{14,10},{15,... | collective-permute-start | bytes 663560 | tf_op jit(solution)/shard_map/ppermute | solution.py:77
  53.6 8.2 %collective-permute-start.25 = (bf16[192,576]{1,0:T(8,128)(2,1)S(1)}, bf16[192,576]{1,0:T(8,128)(2,1)S(1)}, u32[]{:S(2)}, u32[]{:S(2)}) collective-permute-start(bf16[192,576]{1,0:T(8,128)(2,1)S(1)} %collective-permute-done.18.refs_5_), channel_id=1, source_target_pairs={{0,2},{1,3},{4,0},{5,1},{8,4},{9,5},{12,8},{13,9},{14,12},{15,13},... | collective-permute-start | bytes 663560 | tf_op jit(solution)/shard_map/ppermute | solution.py:80
  55.0 8.8 %collective-permute-start.26 = (bf16[192,576]{1,0:T(8,128)(2,1)S(1)}, bf16[192,576]{1,0:T(8,128)(2,1)S(1)}, u32[]{:S(2)}, u32[]{:S(2)}) collective-permute-start(bf16[192,576]{1,0:T(8,128)(2,1)S(1)} %collective-permute-done.22.refs_4_), channel_id=1, source_target_pairs={{0,4},{1,5},{4,8},{5,9},{8,12},{9,13},{12,14},{13,15},{14,10},{15,... | collective-permute-start | bytes 663560 | tf_op jit(solution)/shard_map/ppermute | solution.py:77
  55.6 8.8 %collective-permute-start.27 = (bf16[192,576]{1,0:T(8,128)(2,1)S(1)}, bf16[192,576]{1,0:T(8,128)(2,1)S(1)}, u32[]{:S(2)}, u32[]{:S(2)}) collective-permute-start(bf16[192,576]{1,0:T(8,128)(2,1)S(1)} %collective-permute-done.23.refs_5_), channel_id=1, source_target_pairs={{0,2},{1,3},{4,0},{5,1},{8,4},{9,5},{12,8},{13,9},{14,12},{15,13},... | collective-permute-start | bytes 663560 | tf_op jit(solution)/shard_map/ppermute | solution.py:80
  57.0 9.4 %collective-permute-start.20 = (bf16[192,576]{1,0:T(8,128)(2,1)S(1)}, bf16[192,576]{1,0:T(8,128)(2,1)S(1)}, u32[]{:S(2)}, u32[]{:S(2)}) collective-permute-start(bf16[192,576]{1,0:T(8,128)(2,1)S(1)} %get-tuple-element.109.refs_0_.mo_ref), channel_id=1, source_target_pairs={{0,1},{1,0},{2,3},{3,2},{4,5},{5,4},{6,7},{7,6},{8,9},{9,8},{10,11... | collective-permute-start | bytes 663560 | tf_op jit(solution)/shard_map/ppermute | solution.py:83
  64.4 8.4 %collective-permute-start.28 = (bf16[192,576]{1,0:T(8,128)(2,1)S(1)}, bf16[192,576]{1,0:T(8,128)(2,1)S(1)}, u32[]{:S(2)}, u32[]{:S(2)}) collective-permute-start(bf16[192,576]{1,0:T(8,128)(2,1)S(1)} %collective-permute-done.24.refs_6_), channel_id=1, source_target_pairs={{0,4},{1,5},{4,8},{5,9},{8,12},{9,13},{12,14},{13,15},{14,10},{15,... | collective-permute-start | bytes 663560 | tf_op jit(solution)/shard_map/ppermute | solution.py:77
  65.0 8.3 %collective-permute-start.29 = (bf16[192,576]{1,0:T(8,128)(2,1)S(1)}, bf16[192,576]{1,0:T(8,128)(2,1)S(1)}, u32[]{:S(2)}, u32[]{:S(2)}) collective-permute-start(bf16[192,576]{1,0:T(8,128)(2,1)S(1)} %collective-permute-done.25.refs_7_), channel_id=1, source_target_pairs={{0,2},{1,3},{4,0},{5,1},{8,4},{9,5},{12,8},{13,9},{14,12},{15,13},... | collective-permute-start | bytes 663560 | tf_op jit(solution)/shard_map/ppermute | solution.py:80
  68.0 7.4 %collective-permute-start.30 = (bf16[192,576]{1,0:T(8,128)(2,1)S(1)}, bf16[192,576]{1,0:T(8,128)(2,1)S(1)}, u32[]{:S(2)}, u32[]{:S(2)}) collective-permute-start(bf16[192,576]{1,0:T(8,128)(2,1)S(1)} %collective-permute-done.26.refs_4_), channel_id=1, source_target_pairs={{0,4},{1,5},{4,8},{5,9},{8,12},{9,13},{12,14},{13,15},{14,10},{15,... | collective-permute-start | bytes 663560 | tf_op jit(solution)/shard_map/ppermute | solution.py:77
  68.7 7.3 %collective-permute-start.31 = (bf16[192,576]{1,0:T(8,128)(2,1)S(1)}, bf16[192,576]{1,0:T(8,128)(2,1)S(1)}, u32[]{:S(2)}, u32[]{:S(2)}) collective-permute-start(bf16[192,576]{1,0:T(8,128)(2,1)S(1)} %collective-permute-done.27.refs_5_), channel_id=1, source_target_pairs={{0,2},{1,3},{4,0},{5,1},{8,4},{9,5},{12,8},{13,9},{14,12},{15,13},... | collective-permute-start | bytes 663560 | tf_op jit(solution)/shard_map/ppermute | solution.py:80
  84.1 9.1 %collective-permute-start.38 = (f32[192,1152]{1,0:T(8,128)S(1)}, f32[192,1152]{1,0:T(8,128)S(1)}, u32[]{:S(2)}, u32[]{:S(2)}) collective-permute-start(f32[192,1152]{1,0:T(8,128)S(1)} %get-tuple-element.154), channel_id=1, source_target_pairs={{0,1},{1,0},{2,3},{3,2},{4,5},{5,4},{6,7},{7,6},{8,9},{9,8},{10,11... | collective-permute-start | bytes 2654216 | tf_op jit(solution)/shard_map/ppermute | solution.py:83
  94.5 8.1 %collective-permute-start.40 = (bf16[192,576]{1,0:T(8,128)(2,1)S(1)}, bf16[192,576]{1,0:T(8,128)(2,1)S(1)}, u32[]{:S(2)}, u32[]{:S(2)}) collective-permute-start(bf16[192,576]{1,0:T(8,128)(2,1)S(1)} %get-tuple-element.158), channel_id=1, source_target_pairs={{0,16},{16,0},{1,17},{17,1},{2,18},{18,2},{3,19},{19,3},{4,20},{20... | collective-permute-start | bytes 663560 | tf_op jit(solution)/shard_map/ppermute | solution.py:87
  95.0 7.6 %collective-permute-start.43 = (bf16[8,96,192]{2,1,0:T(8,128)(2,1)S(1)}, bf16[8,96,192]{2,1,0:T(8,128)(2,1)S(1)}, u32[]{:S(2)}, u32[]{:S(2)}) collective-permute-start(bf16[8,96,192]{2,1,0:T(8,128)(2,1)S(1)} %copy-done.6), channel_id=1, source_target_pairs={{0,1},{1,0},{2,3},{3,2},{4,5},{5,4},{6,7},{7,6},{8,9},{9,8},{10,11... | collective-permute-start | bytes 884744 | tf_op jit(solution)/shard_map/ppermute | solution.py:83
  95.0 7.6 %collective-permute-start.44 = (bf16[8,80,192]{2,1,0:T(8,128)(2,1)S(1)}, bf16[8,80,192]{2,1,0:T(8,128)(2,1)S(1)}, u32[]{:S(2)}, u32[]{:S(2)}) collective-permute-start(bf16[8,80,192]{2,1,0:T(8,128)(2,1)S(1)} %copy-done.8), channel_id=1, source_target_pairs={{0,1},{1,0},{2,3},{3,2},{4,5},{5,4},{6,7},{7,6},{8,9},{9,8},{10,11... | collective-permute-start | bytes 737288 | tf_op jit(solution)/shard_map/ppermute | solution.py:83
  95.5 7.1 %collective-permute-start.41 = (bf16[192,576]{1,0:T(8,128)(2,1)S(1)}, bf16[192,576]{1,0:T(8,128)(2,1)S(1)}, u32[]{:S(2)}, u32[]{:S(2)}) collective-permute-start(bf16[192,576]{1,0:T(8,128)(2,1)S(1)} %get-tuple-element.174.do_ref), channel_id=1, source_target_pairs={{0,1},{1,0},{2,3},{3,2},{4,5},{5,4},{6,7},{7,6},{8,9},{9,8},{10,11... | collective-permute-start | bytes 663560 | tf_op jit(solution)/shard_map/ppermute | solution.py:83
  110.3 6.8 %collective-permute-start.48 = (bf16[176,576]{1,0:T(8,128)(2,1)S(1)}, bf16[176,576]{1,0:T(8,128)(2,1)S(1)}, u32[]{:S(2)}, u32[]{:S(2)}) collective-permute-start(bf16[176,576]{1,0:T(8,128)(2,1)S(1)} %pad_maximum_fusion.1), channel_id=1, source_target_pairs={{0,2},{1,3},{4,0},{5,1},{8,4},{9,5},{12,8},{13,9},{14,12},{15,13},... | collective-permute-start | bytes 608264 | tf_op jit(solution)/shard_map/ppermute | solution.py:80
  118.6 12.3 %collective-permute-start.53 = (bf16[192,1344]{1,0:T(8,128)(2,1)S(1)}, bf16[192,1344]{1,0:T(8,128)(2,1)S(1)}, u32[]{:S(2)}, u32[]{:S(2)}) collective-permute-start(bf16[192,1344]{1,0:T(8,128)(2,1)S(1)} %get-tuple-element.183), channel_id=1, source_target_pairs={{0,16},{16,0},{1,17},{17,1},{2,18},{18,2},{3,19},{19,3},{4,20},{20... | collective-permute-start | bytes 1548296 | tf_op jit(solution)/shard_map/ppermute | solution.py:87
  (39 other events, 205.2 us)

commit v6 on v5

--- a/solution.py
+++ b/solution.py
@@ -107,10 +107,12 @@
             keep[q] = jnp.where(first, a, b)
             give[q] = jnp.where(first, b, a)
     for feat, r, rp, out in ((txt_ref, rt, rpt, wide[0]), (img_ref, ri, rpi, wide[-1])):
-        if rp > r:
-            out[...] = jnp.zeros_like(out)
-            for b in range(nb):
-                out[:, b * rp : b * rp + r] = feat[:, b * r : (b + 1) * r]
+        if rp == r:
+            out[...] = feat[...]
+            continue
+        out[...] = jnp.zeros_like(out)
+        for b in range(nb):
+            out[:, b * rp : b * rp + r] = feat[:, b * r : (b + 1) * r]
 
 
 def feature_products(nb, ri, rt, s_ref, do_ref, dg_ref, wi_ref, wt_ref, keep_ref, give_ref):
@@ -136,6 +138,12 @@
         cols = slice(at, at + out.shape[1])
         out[...] = (keep_ref[:, cols] + got_ref[:, cols].astype(F32)).astype(BF16)
         at += out.shape[1]
+
+
+def sums(rpi, g_ref, f_ref, b_ref, img_ref, txt_ref):
+    x = g_ref[...] + f_ref[...].astype(F32) + b_ref[...].astype(F32)
+    img_ref[...] = x[: img_ref.shape[0]]
+    txt_ref[...] = x[rpi : rpi + txt_ref.shape[0]]
 
 
 def project(n, rpi, rpt, rt, half, slot_ref, img_ref, txt_ref, *refs):
@@ -262,7 +270,7 @@
         [((n, rpi, rows), BF16)] * 2
         + [((n, rpt, rows), BF16)] * 2
         + [((rows, nb * rpt), BF16)]
-        + [((rows, nb * rpi), BF16)] * (rpi > ri),
+        + [((rows, nb * rpi), BF16)],
         [core.astype(jnp.int32).reshape(1)],
         [img_feat, txt_feat],
         1,
@@ -276,8 +284,7 @@
             f, b, *prep = tie((f, b, *prep))
         at[n - k], at[k] = f, b
         sib[n - k], sib[k] = ring.other_core(f), ring.other_core(b)
-    img_keep, img_give, txt_keep, txt_give, txt_wide = prep[:5]
-    img_wide = prep[5] if rpi > ri else img_feat
+    img_keep, img_give, txt_keep, txt_give, txt_wide, img_wide = prep
     f, b = ring.right(f[:rpi]), ring.left(b[rpi:])
     at[h], sib[h] = (f, b), (ring.other_core(f), ring.other_core(b))
 
@@ -401,11 +408,13 @@
         10,
     )
     f, b, img_grad, txt_grad = tie((f, b, img_grad, txt_grad))
-
-    def total(lo, hi):
-        return g[0, lo:hi] + f[lo:hi].astype(F32) + b[lo:hi].astype(F32)
-
-    img_total, txt_total = total(0, ri), total(rpi, rpi + rt)
+    img_total, txt_total = call(
+        functools.partial(sums, rpi),
+        [((ri, half), F32), ((rt, half), F32)],
+        [],
+        [g[0], f, b],
+        1,
+    )
     return img_grad, txt_grad, img_total, txt_total
 
 

time: 134 us -> 134 us (level)
  other arithmetic: 2.94 us -> 1.51 us
    ppermute x5, waiting for transfers between devices: 15 us -> 17.2 us  [swap(): return lax.ppermute(x, 'tower', [(0, 1), (1, 0)])]
    add x2 -> x0, other arithmetic: 1.44 us -> none  [total(): return g[0, lo:hi] + f[lo:hi].astype(F32) + b[lo:hi].astype(F32)]
    ppermute x16, waiting for transfers between devices: 28 us -> 26.6 us  [right(): return lax.ppermute(x, 'batch', self.fwd)]
    pallas_call x13 -> x14, Pallas kernels: 21.2 us -> 22.3 us  [call(): pl.pallas_call(body, out_shape=[jax.ShapeDtypeStruct(s, t) for s, t in ou...]
    unnamed x18 -> x16, local copies, waits for them, and re-layouts: 4.65 us -> 3.59 us
  transfers between devices with their start and end apart: 54 -> 54, of which waited for: 35 -> 33; matrix products, arithmetic and copies ran while one was open for 0% -> 0% of each run, Pallas kernels for 11% -> 11%
where the time goes in v6:
time: 134 us; the launch traced here: 133 us
  waiting for transfers between devices  62.4 us (47%)
  starting transfers between devices  41.8 us (31%)
  Pallas kernels  22.3 us (17%)
  local copies, waits for them, and re-layouts  3.8 us (3%)
  between operations  1.58 us (1%)
  other arithmetic  1.51 us (1%)
    ppermute x16, waiting for transfers between devices, right(): return lax.ppermute(x, 'batch', self.fwd)  26.6 us
    pallas_call x14, Pallas kernels, call(): pl.pallas_call(body, out_shape=[jax.ShapeDtypeStruct(s, t) for s, t in ou...  22.3 us
    ppermute x16, starting transfers between devices, left(): return lax.ppermute(x, 'batch', self.bwd)  18.9 us
    ppermute x5, waiting for transfers between devices, swap(): return lax.ppermute(x, 'tower', [(0, 1), (1, 0)])  17.2 us
    ppermute x16, waiting for transfers between devices, left(): return lax.ppermute(x, 'batch', self.bwd)  15.8 us
    ppermute x16, starting transfers between devices, right(): return lax.ppermute(x, 'batch', self.fwd)  15 us
    ppermute x5, starting transfers between devices, swap(): return lax.ppermute(x, 'tower', [(0, 1), (1, 0)])  5.7 us
    unnamed x16, local copies, waits for them, and re-layouts  3.59 us
  transfers between devices with their start and end apart: 54, of which 33 were waited for; matrix products, arithmetic and copies ran while one was open for 0% of the time, Pallas kernels for 11%

profile of v6, /device:TPU:0, one launch (start us, length us, event | category | flops | bytes accessed | tf_op | source)
XLA Modules:
  0.0 133.4 jit_solution(15491501145764260585)
XLA Ops:
  2.4 3.1 %collective-permute-start = (bf16[176,576]{1,0:T(8,128)(2,1)S(1)}, bf16[176,576]{1,0:T(8,128)(2,1)S(1)}, u32[]{:S(2)}, u32[]{:S(2)}) collective-permute-start(bf16[176,576]{1,0:T(8,128)(2,1)S(1)} %maximum_maximum_fusion.refs_0_), channel_id=1, source_target_pairs={{0,4},{1,5},{4,8},{5,9},{8,12},{9,13},{12,14},{13,15},{14,10},{15,... | collective-permute-start | bytes 608264 | tf_op jit(solution)/shard_map/ppermute | solution.py:77
  14.5 4.0 %collective-permute-done.4.refs_7_ = bf16[176,576]{1,0:T(8,128)(2,1)S(1)} collective-permute-done((bf16[176,576]{1,0:T(8,128)(2,1)S(1)}, bf16[176,576]{1,0:T(8,128)(2,1)S(1)}, u32[]{:S(2)}, u32[]{:S(2)}) %collective-permute-start.4) | collective-permute-done | bytes 202784 | tf_op jit(solution)/shard_map/ppermute | solution.py:77
  21.1 3.4 %collective-permute-done.5.refs_6_ = bf16[176,576]{1,0:T(8,128)(2,1)S(1)} collective-permute-done((bf16[176,576]{1,0:T(8,128)(2,1)S(1)}, bf16[176,576]{1,0:T(8,128)(2,1)S(1)}, u32[]{:S(2)}, u32[]{:S(2)}) %collective-permute-start.5) | collective-permute-done | bytes 202784 | tf_op jit(solution)/shard_map/ppermute | solution.py:77
  26.1 1.6 %collective-permute-start.6 = (bf16[96,576]{1,0:T(8,128)(2,1)S(1)}, bf16[96,576]{1,0:T(8,128)(2,1)S(1)}, u32[]{:S(2)}, u32[]{:S(2)}) collective-permute-start(bf16[96,576]{1,0:T(8,128)(2,1)S(1)} %slice.62), channel_id=1, source_target_pairs={{0,4},{1,5},{4,8},{5,9},{8,12},{9,13},{12,14},{13,15},{14,10},{15,... | collective-permute-start | bytes 331784 | tf_op jit(solution)/shard_map/ppermute | solution.py:77
  28.7 4.0 %collective-permute-done.7.refs_5_ = bf16[80,576]{1,0:T(8,128)(2,1)S(1)} collective-permute-done((bf16[80,576]{1,0:T(8,128)(2,1)S(1)}, bf16[80,576]{1,0:T(8,128)(2,1)S(1)}, u32[]{:S(2)}, u32[]{:S(2)}) %collective-permute-start.7) | collective-permute-done | bytes 92192 | tf_op jit(solution)/shard_map/ppermute | solution.py:80
  34.3 3.9 %shard_map.85 = (bf16[16,96,576]{2,1,0:T(8,128)(2,1)}, bf16[16,80,576]{2,1,0:T(8,128)(2,1)}, f32[192,576]{1,0:T(8,128)S(1)}, f32[192,576]{1,0:T(8,128)S(1)}, f32[8,192]{1,0:T(8,128)S(1)}, /*index=5*/f32[8,128]{1,0:T(8,128)S(1)}) custom-call(s32[2,8]{1,0:T(2,128)S(1)} %pad_add_fusion.slot_ref, bf16[192,1536]{1,0:T(8,128)(2,1)S(1)} %get-tuple-element.107.img_ref, ...), custom_call_target="tpu_custom_call" | custom-call | flops 800000000 | bytes 4325376 | tf_op jit(solution)/shard_map/pallas_call | solution.py:37
  39.7 2.1 %collective-permute-done.17.got_ref = f32[8,192]{1,0:T(8,128)S(1)} collective-permute-done((f32[8,192]{1,0:T(8,128)S(1)}, f32[8,192]{1,0:T(8,128)S(1)}, u32[]{:S(2)}, u32[]{:S(2)}) %collective-permute-start.17) | collective-permute-done | bytes 6176 | tf_op jit(solution)/shard_map/ppermute | solution.py:87
  42.7 1.6 %collective-permute-start.18 = (bf16[192,576]{1,0:T(8,128)(2,1)S(1)}, bf16[192,576]{1,0:T(8,128)(2,1)S(1)}, u32[]{:S(2)}, u32[]{:S(2)}) collective-permute-start(bf16[192,576]{1,0:T(8,128)(2,1)S(1)} %get-tuple-element.115.refs_0_.mo_ref), channel_id=1, source_target_pairs={{0,16},{16,0},{1,17},{17,1},{2,18},{18,2},{3,19},{19,3},{4,20},{20... | collective-permute-start | bytes 663560 | tf_op jit(solution)/shard_map/ppermute | solution.py:87
  46.3 3.5 %collective-permute-done.18.refs_5_ = bf16[192,576]{1,0:T(8,128)(2,1)S(1)} collective-permute-done((bf16[192,576]{1,0:T(8,128)(2,1)S(1)}, bf16[192,576]{1,0:T(8,128)(2,1)S(1)}, u32[]{:S(2)}, u32[]{:S(2)}) %collective-permute-start.18) | collective-permute-done | bytes 221216 | tf_op jit(solution)/shard_map/ppermute | solution.py:87
  56.3 4.2 %collective-permute-done.24.refs_6_ = bf16[192,576]{1,0:T(8,128)(2,1)S(1)} collective-permute-done((bf16[192,576]{1,0:T(8,128)(2,1)S(1)}, bf16[192,576]{1,0:T(8,128)(2,1)S(1)}, u32[]{:S(2)}, u32[]{:S(2)}) %collective-permute-start.24) | collective-permute-done | bytes 221216 | tf_op jit(solution)/shard_map/ppermute | solution.py:77
  61.0 2.1 %collective-permute-done.26.refs_4_ = bf16[192,576]{1,0:T(8,128)(2,1)S(1)} collective-permute-done((bf16[192,576]{1,0:T(8,128)(2,1)S(1)}, bf16[192,576]{1,0:T(8,128)(2,1)S(1)}, u32[]{:S(2)}, u32[]{:S(2)}) %collective-permute-start.26) | collective-permute-done | bytes 221216 | tf_op jit(solution)/shard_map/ppermute | solution.py:77
  65.7 1.6 %shard_map.87 = (f32[192,1152]{1,0:T(8,128)S(1)}, f32[192,1152]{1,0:T(8,128)S(1)}) custom-call(bf16[192,576]{1,0:T(8,128)(2,1)S(1)} %get-tuple-element.115.refs_0_.mo_ref, bf16[192,576]{1,0:T(8,128)(2,1)S(1)} %collective-permute-done.19.refs_1_.mx_ref, bf16[192,576]{1,0:T(8,128)(2,1)S(1)} %collective-permute-done.20.refs_2_.refs_0_, ...), custom_call_target="tpu_custom_call" | custom-call | flops 440000000 | bytes 1327104 | tf_op jit(solution)/shard_map/pallas_call | solution.py:37
  69.4 2.1 %shard_map.88 = (f32[192,1152]{1,0:T(8,128)S(1)}, f32[192,1152]{1,0:T(8,128)S(1)}) custom-call(bf16[192,576]{1,0:T(8,128)(2,1)S(1)} %get-tuple-element.115.refs_0_.mo_ref, bf16[192,576]{1,0:T(8,128)(2,1)S(1)} %collective-permute-done.19.refs_1_.mx_ref, ...), custom_call_target="tpu_custom_call", output_to_operand_aliasing={{0}: (8, {}), {1}: (9, {})} | custom-call | flops 440000000 | bytes 3538944 | tf_op jit(solution)/shard_map/pallas_call | solution.py:37
  72.6 2.1 %collective-permute-done.30.refs_2_ = bf16[192,576]{1,0:T(8,128)(2,1)S(1)} collective-permute-done((bf16[192,576]{1,0:T(8,128)(2,1)S(1)}, bf16[192,576]{1,0:T(8,128)(2,1)S(1)}, u32[]{:S(2)}, u32[]{:S(2)}) %collective-permute-start.30) | collective-permute-done | bytes 221216 | tf_op jit(solution)/shard_map/ppermute | solution.py:77
  79.4 2.1 %shard_map.89 = (f32[192,1152]{1,0:T(8,128)S(1)}, f32[192,1152]{1,0:T(8,128)S(1)}) custom-call(bf16[192,576]{1,0:T(8,128)(2,1)S(1)} %get-tuple-element.115.refs_0_.mo_ref, bf16[192,576]{1,0:T(8,128)(2,1)S(1)} %collective-permute-done.19.refs_1_.mx_ref, ...), custom_call_target="tpu_custom_call", output_to_operand_aliasing={{0}: (8, {}), {1}: (9, {})} | custom-call | flops 440000000 | bytes 3538944 | tf_op jit(solution)/shard_map/pallas_call | solution.py:37
  85.4 3.7 %collective-permute-done.36.refs_8_ = bf16[96,576]{1,0:T(8,128)(2,1)S(1)} collective-permute-done((bf16[96,576]{1,0:T(8,128)(2,1)S(1)}, bf16[96,576]{1,0:T(8,128)(2,1)S(1)}, u32[]{:S(2)}, u32[]{:S(2)}) %collective-permute-start.36) | collective-permute-done | bytes 110624 | tf_op jit(solution)/shard_map/ppermute | solution.py:77
  94.9 7.0 %collective-permute-done.40.dg_ref = bf16[192,576]{1,0:T(8,128)(2,1)S(1)} collective-permute-done((bf16[192,576]{1,0:T(8,128)(2,1)S(1)}, bf16[192,576]{1,0:T(8,128)(2,1)S(1)}, u32[]{:S(2)}, u32[]{:S(2)}) %collective-permute-start.40) | collective-permute-done | bytes 221216 | tf_op jit(solution)/shard_map/ppermute | solution.py:87
  104.6 1.6 %collective-permute-start.47 = (bf16[80,576]{1,0:T(8,128)(2,1)S(1)}, bf16[80,576]{1,0:T(8,128)(2,1)S(1)}, u32[]{:S(2)}, u32[]{:S(2)}) collective-permute-start(bf16[80,576]{1,0:T(8,128)(2,1)S(1)} %get-tuple-element.179), channel_id=1, source_target_pairs={{0,2},{1,3},{4,0},{5,1},{8,4},{9,5},{12,8},{13,9},{14,12},{15,13},... | collective-permute-start | bytes 276488 | tf_op jit(solution)/shard_map/ppermute | solution.py:80
  106.7 2.9 %collective-permute-done.47 = bf16[80,576]{1,0:T(8,128)(2,1)S(1)} collective-permute-done((bf16[80,576]{1,0:T(8,128)(2,1)S(1)}, bf16[80,576]{1,0:T(8,128)(2,1)S(1)}, u32[]{:S(2)}, u32[]{:S(2)}) %collective-permute-start.47) | collective-permute-done | bytes 92192 | tf_op jit(solution)/shard_map/ppermute | solution.py:80
  109.6 1.6 %collective-permute-start.48 = (bf16[176,576]{1,0:T(8,128)(2,1)S(1)}, bf16[176,576]{1,0:T(8,128)(2,1)S(1)}, u32[]{:S(2)}, u32[]{:S(2)}) collective-permute-start(bf16[176,576]{1,0:T(8,128)(2,1)S(1)} %pad_maximum_fusion.1), channel_id=1, source_target_pairs={{0,2},{1,3},{4,0},{5,1},{8,4},{9,5},{12,8},{13,9},{14,12},{15,13},... | collective-permute-start | bytes 608264 | tf_op jit(solution)/shard_map/ppermute | solution.py:80
  111.9 2.5 %shard_map.95 = (f32[192,1344]{1,0:T(8,128)S(1)}, bf16[192,1344]{1,0:T(8,128)(2,1)S(1)}) custom-call(s32[2]{0:T(128)S(1)} %pad_add_fusion.1.s_ref, bf16[192,576]{1,0:T(8,128)(2,1)S(1)} %get-tuple-element.180.do_ref, bf16[192,576]{1,0:T(8,128)(2,1)S(1)} %collective-permute-done.40.dg_ref, bf16[16,96,576]{2,1,0:T(8,128)(2,1)S(1)} %copy-done, ...), custom_call_target="tpu_custom_call" | custom-call | flops 600000000 | bytes 3686400 | tf_op jit(solution)/shard_map/pallas_call | solution.py:37
  120.5 3.5 %collective-permute-done.49 = bf16[176,576]{1,0:T(8,128)(2,1)S(1)} collective-permute-done((bf16[176,576]{1,0:T(8,128)(2,1)S(1)}, bf16[176,576]{1,0:T(8,128)(2,1)S(1)}, u32[]{:S(2)}, u32[]{:S(2)}) %collective-permute-start.49) | collective-permute-done | bytes 202784 | tf_op jit(solution)/shard_map/ppermute | solution.py:77
  125.0 2.0 %collective-permute-start.52 = (bf16[176,576]{1,0:T(8,128)(2,1)S(1)}, bf16[176,576]{1,0:T(8,128)(2,1)S(1)}, u32[]{:S(2)}, u32[]{:S(2)}) collective-permute-start(bf16[176,576]{1,0:T(8,128)(2,1)S(1)} %get-tuple-element.198), channel_id=1, source_target_pairs={{0,2},{1,3},{4,0},{5,1},{8,4},{9,5},{12,8},{13,9},{14,12},{15,13},... | collective-permute-start | bytes 608264 | tf_op jit(solution)/shard_map/ppermute | solution.py:80
  127.1 4.6 %collective-permute-done.53.got_ref = bf16[192,1344]{1,0:T(8,128)(2,1)S(1)} collective-permute-done((bf16[192,1344]{1,0:T(8,128)(2,1)S(1)}, bf16[192,1344]{1,0:T(8,128)(2,1)S(1)}, u32[]{:S(2)}, u32[]{:S(2)}) %collective-permute-start.53) | collective-permute-done | bytes 516128 | tf_op jit(solution)/shard_map/ppermute | solution.py:87
  (136 shorter events, 61.1 us)
Async XLA Ops:
  2.4 8.5 %collective-permute-start = (bf16[176,576]{1,0:T(8,128)(2,1)S(1)}, bf16[176,576]{1,0:T(8,128)(2,1)S(1)}, u32[]{:S(2)}, u32[]{:S(2)}) collective-permute-start(bf16[176,576]{1,0:T(8,128)(2,1)S(1)} %maximum_maximum_fusion.refs_0_), channel_id=1, source_target_pairs={{0,4},{1,5},{4,8},{5,9},{8,12},{9,13},{12,14},{13,15},{14,10},{15,... | collective-permute-start | bytes 608264 | tf_op jit(solution)/shard_map/ppermute | solution.py:77
  5.5 7.0 %collective-permute-start.1 = (bf16[176,576]{1,0:T(8,128)(2,1)S(1)}, bf16[176,576]{1,0:T(8,128)(2,1)S(1)}, u32[]{:S(2)}, u32[]{:S(2)}) collective-permute-start(bf16[176,576]{1,0:T(8,128)(2,1)S(1)} %maximum_maximum_fusion.refs_0_), channel_id=1, source_target_pairs={{0,2},{1,3},{4,0},{5,1},{8,4},{9,5},{12,8},{13,9},{14,12},{15,13},... | collective-permute-start | bytes 608264 | tf_op jit(solution)/shard_map/ppermute | solution.py:80
  20.6 7.2 %collective-permute-start.16 = (bf16[176,576]{1,0:T(8,128)(2,1)S(1)}, bf16[176,576]{1,0:T(8,128)(2,1)}, u32[]{:S(2)}, u32[]{:S(2)}) collective-permute-start(bf16[176,576]{1,0:T(8,128)(2,1)S(1)} %collective-permute-done.refs_8_), channel_id=1, source_target_pairs={{0,1},{1,0},{2,3},{3,2},{4,5},{5,4},{6,7},{7,6},{8,9},{9,8},{10,11... | collective-permute-start | bytes 608264 | tf_op jit(solution)/shard_map/ppermute | solution.py:83
  21.1 7.1 %collective-permute-start.9 = (bf16[176,576]{1,0:T(8,128)(2,1)S(1)}, bf16[176,576]{1,0:T(8,128)(2,1)}, u32[]{:S(2)}, u32[]{:S(2)}) collective-permute-start(bf16[176,576]{1,0:T(8,128)(2,1)S(1)} %collective-permute-done.1.refs_1_), channel_id=1, source_target_pairs={{0,1},{1,0},{2,3},{3,2},{4,5},{5,4},{6,7},{7,6},{8,9},{9,8},{10,11... | collective-permute-start | bytes 608264 | tf_op jit(solution)/shard_map/ppermute | solution.py:83
  26.1 7.2 %collective-permute-start.15 = (bf16[176,576]{1,0:T(8,128)(2,1)S(1)}, bf16[176,576]{1,0:T(8,128)(2,1)S(1)}, u32[]{:S(2)}, u32[]{:S(2)}) collective-permute-start(bf16[176,576]{1,0:T(8,128)(2,1)S(1)} %collective-permute-done.4.refs_7_), channel_id=1, source_target_pairs={{0,1},{1,0},{2,3},{3,2},{4,5},{5,4},{6,7},{7,6},{8,9},{9,8},{10,11... | collective-permute-start | bytes 608264 | tf_op jit(solution)/shard_map/ppermute | solution.py:83
  42.7 7.1 %collective-permute-start.18 = (bf16[192,576]{1,0:T(8,128)(2,1)S(1)}, bf16[192,576]{1,0:T(8,128)(2,1)S(1)}, u32[]{:S(2)}, u32[]{:S(2)}) collective-permute-start(bf16[192,576]{1,0:T(8,128)(2,1)S(1)} %get-tuple-element.115.refs_0_.mo_ref), channel_id=1, source_target_pairs={{0,16},{16,0},{1,17},{17,1},{2,18},{18,2},{3,19},{19,3},{4,20},{20... | collective-permute-start | bytes 663560 | tf_op jit(solution)/shard_map/ppermute | solution.py:87
  44.3 7.1 %collective-permute-start.22 = (bf16[192,576]{1,0:T(8,128)(2,1)S(1)}, bf16[192,576]{1,0:T(8,128)(2,1)S(1)}, u32[]{:S(2)}, u32[]{:S(2)}) collective-permute-start(bf16[192,576]{1,0:T(8,128)(2,1)S(1)} %get-tuple-element.117.refs_4_), channel_id=1, source_target_pairs={{0,4},{1,5},{4,8},{5,9},{8,12},{9,13},{12,14},{13,15},{14,10},{15,... | collective-permute-start | bytes 663560 | tf_op jit(solution)/shard_map/ppermute | solution.py:77
  52.2 8.2 %collective-permute-start.24 = (bf16[192,576]{1,0:T(8,128)(2,1)S(1)}, bf16[192,576]{1,0:T(8,128)(2,1)S(1)}, u32[]{:S(2)}, u32[]{:S(2)}) collective-permute-start(bf16[192,576]{1,0:T(8,128)(2,1)S(1)} %collective-permute-done.18.refs_5_), channel_id=1, source_target_pairs={{0,4},{1,5},{4,8},{5,9},{8,12},{9,13},{12,14},{13,15},{14,10},{15,... | collective-permute-start | bytes 663560 | tf_op jit(solution)/shard_map/ppermute | solution.py:77
  52.8 8.2 %collective-permute-start.25 = (bf16[192,576]{1,0:T(8,128)(2,1)S(1)}, bf16[192,576]{1,0:T(8,128)(2,1)S(1)}, u32[]{:S(2)}, u32[]{:S(2)}) collective-permute-start(bf16[192,576]{1,0:T(8,128)(2,1)S(1)} %collective-permute-done.18.refs_5_), channel_id=1, source_target_pairs={{0,2},{1,3},{4,0},{5,1},{8,4},{9,5},{12,8},{13,9},{14,12},{15,13},... | collective-permute-start | bytes 663560 | tf_op jit(solution)/shard_map/ppermute | solution.py:80
  54.3 8.8 %collective-permute-start.26 = (bf16[192,576]{1,0:T(8,128)(2,1)S(1)}, bf16[192,576]{1,0:T(8,128)(2,1)S(1)}, u32[]{:S(2)}, u32[]{:S(2)}) collective-permute-start(bf16[192,576]{1,0:T(8,128)(2,1)S(1)} %collective-permute-done.22.refs_4_), channel_id=1, source_target_pairs={{0,4},{1,5},{4,8},{5,9},{8,12},{9,13},{12,14},{13,15},{14,10},{15,... | collective-permute-start | bytes 663560 | tf_op jit(solution)/shard_map/ppermute | solution.py:77
  54.9 8.8 %collective-permute-start.27 = (bf16[192,576]{1,0:T(8,128)(2,1)S(1)}, bf16[192,576]{1,0:T(8,128)(2,1)S(1)}, u32[]{:S(2)}, u32[]{:S(2)}) collective-permute-start(bf16[192,576]{1,0:T(8,128)(2,1)S(1)} %collective-permute-done.23.refs_5_), channel_id=1, source_target_pairs={{0,2},{1,3},{4,0},{5,1},{8,4},{9,5},{12,8},{13,9},{14,12},{15,13},... | collective-permute-start | bytes 663560 | tf_op jit(solution)/shard_map/ppermute | solution.py:80
  56.3 9.4 %collective-permute-start.20 = (bf16[192,576]{1,0:T(8,128)(2,1)S(1)}, bf16[192,576]{1,0:T(8,128)(2,1)S(1)}, u32[]{:S(2)}, u32[]{:S(2)}) collective-permute-start(bf16[192,576]{1,0:T(8,128)(2,1)S(1)} %get-tuple-element.115.refs_0_.mo_ref), channel_id=1, source_target_pairs={{0,1},{1,0},{2,3},{3,2},{4,5},{5,4},{6,7},{7,6},{8,9},{9,8},{10,11... | collective-permute-start | bytes 663560 | tf_op jit(solution)/shard_map/ppermute | solution.py:83
  63.7 8.4 %collective-permute-start.28 = (bf16[192,576]{1,0:T(8,128)(2,1)S(1)}, bf16[192,576]{1,0:T(8,128)(2,1)S(1)}, u32[]{:S(2)}, u32[]{:S(2)}) collective-permute-start(bf16[192,576]{1,0:T(8,128)(2,1)S(1)} %collective-permute-done.24.refs_6_), channel_id=1, source_target_pairs={{0,4},{1,5},{4,8},{5,9},{8,12},{9,13},{12,14},{13,15},{14,10},{15,... | collective-permute-start | bytes 663560 | tf_op jit(solution)/shard_map/ppermute | solution.py:77
  64.3 8.3 %collective-permute-start.29 = (bf16[192,576]{1,0:T(8,128)(2,1)S(1)}, bf16[192,576]{1,0:T(8,128)(2,1)S(1)}, u32[]{:S(2)}, u32[]{:S(2)}) collective-permute-start(bf16[192,576]{1,0:T(8,128)(2,1)S(1)} %collective-permute-done.25.refs_7_), channel_id=1, source_target_pairs={{0,2},{1,3},{4,0},{5,1},{8,4},{9,5},{12,8},{13,9},{14,12},{15,13},... | collective-permute-start | bytes 663560 | tf_op jit(solution)/shard_map/ppermute | solution.py:80
  67.3 7.4 %collective-permute-start.30 = (bf16[192,576]{1,0:T(8,128)(2,1)S(1)}, bf16[192,576]{1,0:T(8,128)(2,1)S(1)}, u32[]{:S(2)}, u32[]{:S(2)}) collective-permute-start(bf16[192,576]{1,0:T(8,128)(2,1)S(1)} %collective-permute-done.26.refs_4_), channel_id=1, source_target_pairs={{0,4},{1,5},{4,8},{5,9},{8,12},{9,13},{12,14},{13,15},{14,10},{15,... | collective-permute-start | bytes 663560 | tf_op jit(solution)/shard_map/ppermute | solution.py:77
  68.0 7.3 %collective-permute-start.31 = (bf16[192,576]{1,0:T(8,128)(2,1)S(1)}, bf16[192,576]{1,0:T(8,128)(2,1)S(1)}, u32[]{:S(2)}, u32[]{:S(2)}) collective-permute-start(bf16[192,576]{1,0:T(8,128)(2,1)S(1)} %collective-permute-done.27.refs_5_), channel_id=1, source_target_pairs={{0,2},{1,3},{4,0},{5,1},{8,4},{9,5},{12,8},{13,9},{14,12},{15,13},... | collective-permute-start | bytes 663560 | tf_op jit(solution)/shard_map/ppermute | solution.py:80
  83.3 9.1 %collective-permute-start.38 = (f32[192,1152]{1,0:T(8,128)S(1)}, f32[192,1152]{1,0:T(8,128)S(1)}, u32[]{:S(2)}, u32[]{:S(2)}) collective-permute-start(f32[192,1152]{1,0:T(8,128)S(1)} %get-tuple-element.160), channel_id=1, source_target_pairs={{0,1},{1,0},{2,3},{3,2},{4,5},{5,4},{6,7},{7,6},{8,9},{9,8},{10,11... | collective-permute-start | bytes 2654216 | tf_op jit(solution)/shard_map/ppermute | solution.py:83
  93.7 8.1 %collective-permute-start.40 = (bf16[192,576]{1,0:T(8,128)(2,1)S(1)}, bf16[192,576]{1,0:T(8,128)(2,1)S(1)}, u32[]{:S(2)}, u32[]{:S(2)}) collective-permute-start(bf16[192,576]{1,0:T(8,128)(2,1)S(1)} %get-tuple-element.164), channel_id=1, source_target_pairs={{0,16},{16,0},{1,17},{17,1},{2,18},{18,2},{3,19},{19,3},{4,20},{20... | collective-permute-start | bytes 663560 | tf_op jit(solution)/shard_map/ppermute | solution.py:87
  94.3 7.6 %collective-permute-start.43 = (bf16[8,96,192]{2,1,0:T(8,128)(2,1)S(1)}, bf16[8,96,192]{2,1,0:T(8,128)(2,1)S(1)}, u32[]{:S(2)}, u32[]{:S(2)}) collective-permute-start(bf16[8,96,192]{2,1,0:T(8,128)(2,1)S(1)} %copy-done.5), channel_id=1, source_target_pairs={{0,1},{1,0},{2,3},{3,2},{4,5},{5,4},{6,7},{7,6},{8,9},{9,8},{10,11... | collective-permute-start | bytes 884744 | tf_op jit(solution)/shard_map/ppermute | solution.py:83
  94.3 7.6 %collective-permute-start.44 = (bf16[8,80,192]{2,1,0:T(8,128)(2,1)S(1)}, bf16[8,80,192]{2,1,0:T(8,128)(2,1)S(1)}, u32[]{:S(2)}, u32[]{:S(2)}) collective-permute-start(bf16[8,80,192]{2,1,0:T(8,128)(2,1)S(1)} %copy-done.7), channel_id=1, source_target_pairs={{0,1},{1,0},{2,3},{3,2},{4,5},{5,4},{6,7},{7,6},{8,9},{9,8},{10,11... | collective-permute-start | bytes 737288 | tf_op jit(solution)/shard_map/ppermute | solution.py:83
  94.8 7.1 %collective-permute-start.41 = (bf16[192,576]{1,0:T(8,128)(2,1)S(1)}, bf16[192,576]{1,0:T(8,128)(2,1)S(1)}, u32[]{:S(2)}, u32[]{:S(2)}) collective-permute-start(bf16[192,576]{1,0:T(8,128)(2,1)S(1)} %get-tuple-element.180.do_ref), channel_id=1, source_target_pairs={{0,1},{1,0},{2,3},{3,2},{4,5},{5,4},{6,7},{7,6},{8,9},{9,8},{10,11... | collective-permute-start | bytes 663560 | tf_op jit(solution)/shard_map/ppermute | solution.py:83
  120.0 11.7 %collective-permute-start.53 = (bf16[192,1344]{1,0:T(8,128)(2,1)S(1)}, bf16[192,1344]{1,0:T(8,128)(2,1)S(1)}, u32[]{:S(2)}, u32[]{:S(2)}) collective-permute-start(bf16[192,1344]{1,0:T(8,128)(2,1)S(1)} %get-tuple-element.189), channel_id=1, source_target_pairs={{0,16},{16,0},{1,17},{17,1},{2,18},{18,2},{3,19},{19,3},{4,20},{20... | collective-permute-start | bytes 1548296 | tf_op jit(solution)/shard_map/ppermute | solution.py:87
  125.0 7.6 %collective-permute-start.50 = (bf16[176,576]{1,0:T(8,128)(2,1)S(1)}, bf16[176,576]{1,0:T(8,128)(2,1)S(1)}, u32[]{:S(2)}, u32[]{:S(2)}) collective-permute-start(bf16[176,576]{1,0:T(8,128)(2,1)S(1)} %get-tuple-element.199), channel_id=1, source_target_pairs={{0,4},{1,5},{4,8},{5,9},{8,12},{9,13},{12,14},{13,15},{14,10},{15,... | collective-permute-start | bytes 608264 | tf_op jit(solution)/shard_map/ppermute | solution.py:77
  125.0 7.6 %collective-permute-start.52 = (bf16[176,576]{1,0:T(8,128)(2,1)S(1)}, bf16[176,576]{1,0:T(8,128)(2,1)S(1)}, u32[]{:S(2)}, u32[]{:S(2)}) collective-permute-start(bf16[176,576]{1,0:T(8,128)(2,1)S(1)} %get-tuple-element.198), channel_id=1, source_target_pairs={{0,2},{1,3},{4,0},{5,1},{8,4},{9,5},{12,8},{13,9},{14,12},{15,13},... | collective-permute-start | bytes 608264 | tf_op jit(solution)/shard_map/ppermute | solution.py:80
  (38 other events, 205.0 us)

commit v7 on v6

--- a/solution.py
+++ b/solution.py
@@ -115,21 +115,20 @@
             out[:, b * rp : b * rp + r] = feat[:, b * r : (b + 1) * r]
 
 
-def feature_products(nb, ri, rt, s_ref, do_ref, dg_ref, wi_ref, wt_ref, keep_ref, give_ref):
+def feature_products(nb, ri, rt, own, s_ref, do_ref, dg_ref, wi_ref, wt_ref, out_ref):
     image = s_ref[0] == 0
     do, dg = do_ref[...], dg_ref[...]
     dps = jnp.where(image, do, dg), jnp.where(image, dg, do)
     h = nb // 2
-    for out, tower in ((give_ref, 1 - s_ref[0]), (keep_ref, s_ref[0])):
-        at = 0
-        for dp, w_ref, r in ((dps[0], wi_ref, ri), (dps[1], wt_ref, rt)):
-            if r == w_ref.shape[1]:
-                x = nt(dp, w_ref[pl.ds(tower * h, h)].reshape(h * r, dp.shape[1]))
-            else:
-                x = [nt(dp, w_ref[tower * h + b])[:, :r] for b in range(h)]
-                x = jnp.concatenate(x, axis=1)
-            out[:, at : at + h * r] = x.astype(out.dtype)
-            at += h * r
+    base = (s_ref[0] if own else 1 - s_ref[0]) * h
+    at = 0
+    for dp, w_ref, r in ((dps[0], wi_ref, ri), (dps[1], wt_ref, rt)):
+        if r == w_ref.shape[1]:
+            x = nt(dp, w_ref[pl.ds(base, h)].reshape(h * r, dp.shape[1]))
+        else:
+            x = jnp.concatenate([nt(dp, w_ref[base + b])[:, :r] for b in range(h)], axis=1)
+        out_ref[:, at : at + h * r] = x.astype(out_ref.dtype)
+        at += h * r
 
 
 def finish(keep_ref, got_ref, img_ref, txt_ref):
@@ -377,16 +376,18 @@
     chunk = ((rpi + rpt, half), F32)
     f, b, gf, gb = product(True, [((rpi, half), BF16), ((rpt, half), BF16), chunk, chunk], dps)
     dp_o, dp_got, f, b = tie((dp_o, dp_got, f, b))
-    keep, give = call(
-        functools.partial(feature_products, nb, ri, rt),
-        [((rows, nb * (ri + rt) // 2), F32), ((rows, nb * (ri + rt) // 2), BF16)],
-        [flags],
-        [dp_o, dp_got, wi, wt],
-        3,
-    )
-
+    def feature_part(own, kind):
+        return call(
+            functools.partial(feature_products, nb, ri, rt, own),
+            [((rows, nb * (ri + rt) // 2), kind)],
+            [flags],
+            [dp_o, dp_got, wi, wt],
+            2,
+        )[0]
+
+    keep, give = feature_part(True, F32), feature_part(False, BF16)
     f, b = ring.right(f), ring.left(b)
-    f, *late = tie((f, *dps))
+    f, _, *late = tie((f, give, *dps))
     (g,) = product(False, [((n, rpi + rpt, half), F32)], late)
     for k in range(h - 1, 0, -1):
         pf, pb = (gf, gb) if k == h - 1 else (g[k], g[n - k])
@@ -397,7 +398,9 @@
             f, b = pf + f.astype(F32), pb + b.astype(F32)
         f, b = f.astype(BF16), b.astype(BF16)
         if k == h - 2:
-            f, b, keep, give = tie((f, b, keep, give))
+            f, b = tie((f, b))
+        if k == 1:
+            f, b, keep = tie((f, b, keep))
         f, b = ring.right(f), ring.left(b)
     got = swap(give)
     img_grad, txt_grad = call(

time: 134 us -> 134 us (level)
    ppermute x16, waiting for transfers between devices: 26.6 us -> 25 us  [right(): return lax.ppermute(x, 'batch', self.fwd)]
    pallas_call x14 -> x15, Pallas kernels: 22.3 us -> 23.1 us  [call(): pl.pallas_call(body, out_shape=[jax.ShapeDtypeStruct(s, t) for s, t in ou...]
where the time goes in v7:
time: 134 us; the launch traced here: 133 us
  waiting for transfers between devices  61.5 us (46%)
  starting transfers between devices  41.8 us (31%)
  Pallas kernels  23.1 us (17%)
  local copies, waits for them, and re-layouts  3.82 us (3%)
  between operations  1.61 us (1%)
  other arithmetic  1.5 us (1%)
    ppermute x16, waiting for transfers between devices, right(): return lax.ppermute(x, 'batch', self.fwd)  25 us
    pallas_call x15, Pallas kernels, call(): pl.pallas_call(body, out_shape=[jax.ShapeDtypeStruct(s, t) for s, t in ou...  23.1 us
    ppermute x16, starting transfers between devices, left(): return lax.ppermute(x, 'batch', self.bwd)  18.9 us
    ppermute x5, waiting for transfers between devices, swap(): return lax.ppermute(x, 'tower', [(0, 1), (1, 0)])  17.1 us
    ppermute x16, waiting for transfers between devices, left(): return lax.ppermute(x, 'batch', self.bwd)  16.6 us
    ppermute x16, starting transfers between devices, right(): return lax.ppermute(x, 'batch', self.fwd)  15.1 us
    ppermute x5, starting transfers between devices, swap(): return lax.ppermute(x, 'tower', [(0, 1), (1, 0)])  5.7 us
    unnamed x16, local copies, waits for them, and re-layouts  3.61 us
  transfers between devices with their start and end apart: 54, of which 33 were waited for; matrix products, arithmetic and copies ran while one was open for 0% of the time, Pallas kernels for 11%

profile of v7, /device:TPU:0, one launch (start us, length us, event | category | flops | bytes accessed | tf_op | source)
XLA Modules:
  0.0 133.4 jit_solution(6215190916703884459)
XLA Ops:
  2.4 3.1 %collective-permute-start = (bf16[176,576]{1,0:T(8,128)(2,1)S(1)}, bf16[176,576]{1,0:T(8,128)(2,1)S(1)}, u32[]{:S(2)}, u32[]{:S(2)}) collective-permute-start(bf16[176,576]{1,0:T(8,128)(2,1)S(1)} %maximum_maximum_fusion.refs_0_), channel_id=1, source_target_pairs={{0,4},{1,5},{4,8},{5,9},{8,12},{9,13},{12,14},{13,15},{14,10},{15,... | collective-permute-start | bytes 608264 | tf_op jit(solution)/shard_map/ppermute | solution.py:77
  14.5 4.0 %collective-permute-done.4.refs_7_ = bf16[176,576]{1,0:T(8,128)(2,1)S(1)} collective-permute-done((bf16[176,576]{1,0:T(8,128)(2,1)S(1)}, bf16[176,576]{1,0:T(8,128)(2,1)S(1)}, u32[]{:S(2)}, u32[]{:S(2)}) %collective-permute-start.4) | collective-permute-done | bytes 202784 | tf_op jit(solution)/shard_map/ppermute | solution.py:77
  21.1 3.4 %collective-permute-done.5.refs_6_ = bf16[176,576]{1,0:T(8,128)(2,1)S(1)} collective-permute-done((bf16[176,576]{1,0:T(8,128)(2,1)S(1)}, bf16[176,576]{1,0:T(8,128)(2,1)S(1)}, u32[]{:S(2)}, u32[]{:S(2)}) %collective-permute-start.5) | collective-permute-done | bytes 202784 | tf_op jit(solution)/shard_map/ppermute | solution.py:77
  26.1 1.6 %collective-permute-start.6 = (bf16[96,576]{1,0:T(8,128)(2,1)S(1)}, bf16[96,576]{1,0:T(8,128)(2,1)S(1)}, u32[]{:S(2)}, u32[]{:S(2)}) collective-permute-start(bf16[96,576]{1,0:T(8,128)(2,1)S(1)} %slice.62), channel_id=1, source_target_pairs={{0,4},{1,5},{4,8},{5,9},{8,12},{9,13},{12,14},{13,15},{14,10},{15,... | collective-permute-start | bytes 331784 | tf_op jit(solution)/shard_map/ppermute | solution.py:77
  28.7 4.0 %collective-permute-done.7.refs_5_ = bf16[80,576]{1,0:T(8,128)(2,1)S(1)} collective-permute-done((bf16[80,576]{1,0:T(8,128)(2,1)S(1)}, bf16[80,576]{1,0:T(8,128)(2,1)S(1)}, u32[]{:S(2)}, u32[]{:S(2)}) %collective-permute-start.7) | collective-permute-done | bytes 92192 | tf_op jit(solution)/shard_map/ppermute | solution.py:80
  34.3 3.9 %shard_map.85 = (bf16[16,96,576]{2,1,0:T(8,128)(2,1)}, bf16[16,80,576]{2,1,0:T(8,128)(2,1)}, f32[192,576]{1,0:T(8,128)S(1)}, f32[192,576]{1,0:T(8,128)S(1)}, f32[8,192]{1,0:T(8,128)S(1)}, /*index=5*/f32[8,128]{1,0:T(8,128)S(1)}) custom-call(s32[2,8]{1,0:T(2,128)S(1)} %pad_add_fusion.slot_ref, bf16[192,1536]{1,0:T(8,128)(2,1)S(1)} %get-tuple-element.106.img_ref, ...), custom_call_target="tpu_custom_call" | custom-call | flops 800000000 | bytes 4325376 | tf_op jit(solution)/shard_map/pallas_call | solution.py:37
  39.8 2.1 %collective-permute-done.17.got_ref = f32[8,192]{1,0:T(8,128)S(1)} collective-permute-done((f32[8,192]{1,0:T(8,128)S(1)}, f32[8,192]{1,0:T(8,128)S(1)}, u32[]{:S(2)}, u32[]{:S(2)}) %collective-permute-start.17) | collective-permute-done | bytes 6176 | tf_op jit(solution)/shard_map/ppermute | solution.py:87
  46.3 3.5 %collective-permute-done.18.refs_5_ = bf16[192,576]{1,0:T(8,128)(2,1)S(1)} collective-permute-done((bf16[192,576]{1,0:T(8,128)(2,1)S(1)}, bf16[192,576]{1,0:T(8,128)(2,1)S(1)}, u32[]{:S(2)}, u32[]{:S(2)}) %collective-permute-start.18) | collective-permute-done | bytes 221216 | tf_op jit(solution)/shard_map/ppermute | solution.py:87
  56.3 4.2 %collective-permute-done.24.refs_6_ = bf16[192,576]{1,0:T(8,128)(2,1)S(1)} collective-permute-done((bf16[192,576]{1,0:T(8,128)(2,1)S(1)}, bf16[192,576]{1,0:T(8,128)(2,1)S(1)}, u32[]{:S(2)}, u32[]{:S(2)}) %collective-permute-start.24) | collective-permute-done | bytes 221216 | tf_op jit(solution)/shard_map/ppermute | solution.py:77
  61.1 2.1 %collective-permute-done.26.refs_4_ = bf16[192,576]{1,0:T(8,128)(2,1)S(1)} collective-permute-done((bf16[192,576]{1,0:T(8,128)(2,1)S(1)}, bf16[192,576]{1,0:T(8,128)(2,1)S(1)}, u32[]{:S(2)}, u32[]{:S(2)}) %collective-permute-start.26) | collective-permute-done | bytes 221216 | tf_op jit(solution)/shard_map/ppermute | solution.py:77
  65.7 1.6 %shard_map.87 = (f32[192,1152]{1,0:T(8,128)S(1)}, f32[192,1152]{1,0:T(8,128)S(1)}) custom-call(bf16[192,576]{1,0:T(8,128)(2,1)S(1)} %get-tuple-element.114.refs_0_.mo_ref, bf16[192,576]{1,0:T(8,128)(2,1)S(1)} %collective-permute-done.19.refs_1_.mx_ref, bf16[192,576]{1,0:T(8,128)(2,1)S(1)} %collective-permute-done.20.refs_2_.refs_0_, ...), custom_call_target="tpu_custom_call" | custom-call | flops 440000000 | bytes 1327104 | tf_op jit(solution)/shard_map/pallas_call | solution.py:37
  69.4 2.1 %shard_map.88 = (f32[192,1152]{1,0:T(8,128)S(1)}, f32[192,1152]{1,0:T(8,128)S(1)}) custom-call(bf16[192,576]{1,0:T(8,128)(2,1)S(1)} %get-tuple-element.114.refs_0_.mo_ref, bf16[192,576]{1,0:T(8,128)(2,1)S(1)} %collective-permute-done.19.refs_1_.mx_ref, ...), custom_call_target="tpu_custom_call", output_to_operand_aliasing={{0}: (8, {}), {1}: (9, {})} | custom-call | flops 440000000 | bytes 3538944 | tf_op jit(solution)/shard_map/pallas_call | solution.py:37
  72.6 2.1 %collective-permute-done.30.refs_2_ = bf16[192,576]{1,0:T(8,128)(2,1)S(1)} collective-permute-done((bf16[192,576]{1,0:T(8,128)(2,1)S(1)}, bf16[192,576]{1,0:T(8,128)(2,1)S(1)}, u32[]{:S(2)}, u32[]{:S(2)}) %collective-permute-start.30) | collective-permute-done | bytes 221216 | tf_op jit(solution)/shard_map/ppermute | solution.py:77
  79.4 2.1 %shard_map.89 = (f32[192,1152]{1,0:T(8,128)S(1)}, f32[192,1152]{1,0:T(8,128)S(1)}) custom-call(bf16[192,576]{1,0:T(8,128)(2,1)S(1)} %get-tuple-element.114.refs_0_.mo_ref, bf16[192,576]{1,0:T(8,128)(2,1)S(1)} %collective-permute-done.19.refs_1_.mx_ref, ...), custom_call_target="tpu_custom_call", output_to_operand_aliasing={{0}: (8, {}), {1}: (9, {})} | custom-call | flops 440000000 | bytes 3538944 | tf_op jit(solution)/shard_map/pallas_call | solution.py:37
  85.4 3.7 %collective-permute-done.36.refs_8_ = bf16[96,576]{1,0:T(8,128)(2,1)S(1)} collective-permute-done((bf16[96,576]{1,0:T(8,128)(2,1)S(1)}, bf16[96,576]{1,0:T(8,128)(2,1)S(1)}, u32[]{:S(2)}, u32[]{:S(2)}) %collective-permute-start.36) | collective-permute-done | bytes 110624 | tf_op jit(solution)/shard_map/ppermute | solution.py:77
  94.9 7.0 %collective-permute-done.40.dg_ref = bf16[192,576]{1,0:T(8,128)(2,1)S(1)} collective-permute-done((bf16[192,576]{1,0:T(8,128)(2,1)S(1)}, bf16[192,576]{1,0:T(8,128)(2,1)S(1)}, u32[]{:S(2)}, u32[]{:S(2)}) %collective-permute-start.40) | collective-permute-done | bytes 221216 | tf_op jit(solution)/shard_map/ppermute | solution.py:87
  104.6 1.6 %collective-permute-start.47 = (bf16[80,576]{1,0:T(8,128)(2,1)S(1)}, bf16[80,576]{1,0:T(8,128)(2,1)S(1)}, u32[]{:S(2)}, u32[]{:S(2)}) collective-permute-start(bf16[80,576]{1,0:T(8,128)(2,1)S(1)} %get-tuple-element.182), channel_id=1, source_target_pairs={{0,2},{1,3},{4,0},{5,1},{8,4},{9,5},{12,8},{13,9},{14,12},{15,13},... | collective-permute-start | bytes 276488 | tf_op jit(solution)/shard_map/ppermute | solution.py:80
  106.7 1.6 %shard_map.94 = bf16[192,1344]{1,0:T(8,128)(2,1)S(1)} custom-call(s32[2]{0:T(128)S(1)} %pad_add_fusion.1.s_ref, bf16[192,576]{1,0:T(8,128)(2,1)S(1)} %get-tuple-element.175.do_ref, bf16[192,576]{1,0:T(8,128)(2,1)S(1)} %collective-permute-done.40.dg_ref, bf16[16,96,576]{2,1,0:T(8,128)(2,1)S(1)} %copy-done, bf16[16,80,576]{2,1,0:T(8,128)(2,1)S(1)} %copy-done.1), custom_call_target="tpu_custom_call" | custom-call | flops 400000000 | bytes 3686400 | tf_op jit(solution)/shard_map/pallas_call | solution.py:37
  109.6 1.6 %collective-permute-start.48 = (bf16[176,576]{1,0:T(8,128)(2,1)S(1)}, bf16[176,576]{1,0:T(8,128)(2,1)S(1)}, u32[]{:S(2)}, u32[]{:S(2)}) collective-permute-start(bf16[176,576]{1,0:T(8,128)(2,1)S(1)} %pad_maximum_fusion.1), channel_id=1, source_target_pairs={{0,2},{1,3},{4,0},{5,1},{8,4},{9,5},{12,8},{13,9},{14,12},{15,13},... | collective-permute-start | bytes 608264 | tf_op jit(solution)/shard_map/ppermute | solution.py:80
  113.4 3.0 %collective-permute-done.48 = bf16[176,576]{1,0:T(8,128)(2,1)S(1)} collective-permute-done((bf16[176,576]{1,0:T(8,128)(2,1)S(1)}, bf16[176,576]{1,0:T(8,128)(2,1)S(1)}, u32[]{:S(2)}, u32[]{:S(2)}) %collective-permute-start.48) | collective-permute-done | bytes 202784 | tf_op jit(solution)/shard_map/ppermute | solution.py:80
  120.5 1.6 %shard_map.96.keep_ref = f32[192,1344]{1,0:T(8,128)S(1)} custom-call(s32[2]{0:T(128)S(1)} %pad_add_fusion.1.s_ref, bf16[192,576]{1,0:T(8,128)(2,1)S(1)} %get-tuple-element.175.do_ref, bf16[192,576]{1,0:T(8,128)(2,1)S(1)} %collective-permute-done.40.dg_ref, bf16[16,96,576]{2,1,0:T(8,128)(2,1)S(1)} %copy-done, bf16[16,80,576]{2,1,0:T(8,128)(2,1)S(1)} %copy-done.1), custom_call_target="tpu_custom_call" | custom-call | flops 400000000 | bytes 3686400 | tf_op jit(solution)/shard_map/pallas_call | solution.py:37
  122.1 1.9 %collective-permute-done.49 = bf16[176,576]{1,0:T(8,128)(2,1)S(1)} collective-permute-done((bf16[176,576]{1,0:T(8,128)(2,1)S(1)}, bf16[176,576]{1,0:T(8,128)(2,1)S(1)}, u32[]{:S(2)}, u32[]{:S(2)}) %collective-permute-start.49) | collective-permute-done | bytes 202784 | tf_op jit(solution)/shard_map/ppermute | solution.py:77
  125.0 2.0 %collective-permute-start.52 = (bf16[176,576]{1,0:T(8,128)(2,1)S(1)}, bf16[176,576]{1,0:T(8,128)(2,1)S(1)}, u32[]{:S(2)}, u32[]{:S(2)}) collective-permute-start(bf16[176,576]{1,0:T(8,128)(2,1)S(1)} %get-tuple-element.186), channel_id=1, source_target_pairs={{0,2},{1,3},{4,0},{5,1},{8,4},{9,5},{12,8},{13,9},{14,12},{15,13},... | collective-permute-start | bytes 608264 | tf_op jit(solution)/shard_map/ppermute | solution.py:80
  127.1 4.6 %collective-permute-done.53.got_ref = bf16[192,1344]{1,0:T(8,128)(2,1)S(1)} collective-permute-done((bf16[192,1344]{1,0:T(8,128)(2,1)S(1)}, bf16[192,1344]{1,0:T(8,128)(2,1)S(1)}, u32[]{:S(2)}, u32[]{:S(2)}) %collective-permute-start.53) | collective-permute-done | bytes 516128 | tf_op jit(solution)/shard_map/ppermute | solution.py:87
  (137 shorter events, 63.3 us)
Async XLA Ops:
  2.4 8.5 %collective-permute-start = (bf16[176,576]{1,0:T(8,128)(2,1)S(1)}, bf16[176,576]{1,0:T(8,128)(2,1)S(1)}, u32[]{:S(2)}, u32[]{:S(2)}) collective-permute-start(bf16[176,576]{1,0:T(8,128)(2,1)S(1)} %maximum_maximum_fusion.refs_0_), channel_id=1, source_target_pairs={{0,4},{1,5},{4,8},{5,9},{8,12},{9,13},{12,14},{13,15},{14,10},{15,... | collective-permute-start | bytes 608264 | tf_op jit(solution)/shard_map/ppermute | solution.py:77
  5.5 7.0 %collective-permute-start.1 = (bf16[176,576]{1,0:T(8,128)(2,1)S(1)}, bf16[176,576]{1,0:T(8,128)(2,1)S(1)}, u32[]{:S(2)}, u32[]{:S(2)}) collective-permute-start(bf16[176,576]{1,0:T(8,128)(2,1)S(1)} %maximum_maximum_fusion.refs_0_), channel_id=1, source_target_pairs={{0,2},{1,3},{4,0},{5,1},{8,4},{9,5},{12,8},{13,9},{14,12},{15,13},... | collective-permute-start | bytes 608264 | tf_op jit(solution)/shard_map/ppermute | solution.py:80
  20.6 7.2 %collective-permute-start.16 = (bf16[176,576]{1,0:T(8,128)(2,1)S(1)}, bf16[176,576]{1,0:T(8,128)(2,1)}, u32[]{:S(2)}, u32[]{:S(2)}) collective-permute-start(bf16[176,576]{1,0:T(8,128)(2,1)S(1)} %collective-permute-done.refs_8_), channel_id=1, source_target_pairs={{0,1},{1,0},{2,3},{3,2},{4,5},{5,4},{6,7},{7,6},{8,9},{9,8},{10,11... | collective-permute-start | bytes 608264 | tf_op jit(solution)/shard_map/ppermute | solution.py:83
  21.1 7.1 %collective-permute-start.9 = (bf16[176,576]{1,0:T(8,128)(2,1)S(1)}, bf16[176,576]{1,0:T(8,128)(2,1)}, u32[]{:S(2)}, u32[]{:S(2)}) collective-permute-start(bf16[176,576]{1,0:T(8,128)(2,1)S(1)} %collective-permute-done.1.refs_1_), channel_id=1, source_target_pairs={{0,1},{1,0},{2,3},{3,2},{4,5},{5,4},{6,7},{7,6},{8,9},{9,8},{10,11... | collective-permute-start | bytes 608264 | tf_op jit(solution)/shard_map/ppermute | solution.py:83
  26.1 7.2 %collective-permute-start.15 = (bf16[176,576]{1,0:T(8,128)(2,1)S(1)}, bf16[176,576]{1,0:T(8,128)(2,1)S(1)}, u32[]{:S(2)}, u32[]{:S(2)}) collective-permute-start(bf16[176,576]{1,0:T(8,128)(2,1)S(1)} %collective-permute-done.4.refs_7_), channel_id=1, source_target_pairs={{0,1},{1,0},{2,3},{3,2},{4,5},{5,4},{6,7},{7,6},{8,9},{9,8},{10,11... | collective-permute-start | bytes 608264 | tf_op jit(solution)/shard_map/ppermute | solution.py:83
  42.7 7.1 %collective-permute-start.18 = (bf16[192,576]{1,0:T(8,128)(2,1)S(1)}, bf16[192,576]{1,0:T(8,128)(2,1)S(1)}, u32[]{:S(2)}, u32[]{:S(2)}) collective-permute-start(bf16[192,576]{1,0:T(8,128)(2,1)S(1)} %get-tuple-element.114.refs_0_.mo_ref), channel_id=1, source_target_pairs={{0,16},{16,0},{1,17},{17,1},{2,18},{18,2},{3,19},{19,3},{4,20},{20... | collective-permute-start | bytes 663560 | tf_op jit(solution)/shard_map/ppermute | solution.py:87
  44.3 7.1 %collective-permute-start.22 = (bf16[192,576]{1,0:T(8,128)(2,1)S(1)}, bf16[192,576]{1,0:T(8,128)(2,1)S(1)}, u32[]{:S(2)}, u32[]{:S(2)}) collective-permute-start(bf16[192,576]{1,0:T(8,128)(2,1)S(1)} %get-tuple-element.116.refs_4_), channel_id=1, source_target_pairs={{0,4},{1,5},{4,8},{5,9},{8,12},{9,13},{12,14},{13,15},{14,10},{15,... | collective-permute-start | bytes 663560 | tf_op jit(solution)/shard_map/ppermute | solution.py:77
  52.3 8.2 %collective-permute-start.24 = (bf16[192,576]{1,0:T(8,128)(2,1)S(1)}, bf16[192,576]{1,0:T(8,128)(2,1)S(1)}, u32[]{:S(2)}, u32[]{:S(2)}) collective-permute-start(bf16[192,576]{1,0:T(8,128)(2,1)S(1)} %collective-permute-done.18.refs_5_), channel_id=1, source_target_pairs={{0,4},{1,5},{4,8},{5,9},{8,12},{9,13},{12,14},{13,15},{14,10},{15,... | collective-permute-start | bytes 663560 | tf_op jit(solution)/shard_map/ppermute | solution.py:77
  52.9 8.2 %collective-permute-start.25 = (bf16[192,576]{1,0:T(8,128)(2,1)S(1)}, bf16[192,576]{1,0:T(8,128)(2,1)S(1)}, u32[]{:S(2)}, u32[]{:S(2)}) collective-permute-start(bf16[192,576]{1,0:T(8,128)(2,1)S(1)} %collective-permute-done.18.refs_5_), channel_id=1, source_target_pairs={{0,2},{1,3},{4,0},{5,1},{8,4},{9,5},{12,8},{13,9},{14,12},{15,13},... | collective-permute-start | bytes 663560 | tf_op jit(solution)/shard_map/ppermute | solution.py:80
  54.3 8.8 %collective-permute-start.26 = (bf16[192,576]{1,0:T(8,128)(2,1)S(1)}, bf16[192,576]{1,0:T(8,128)(2,1)S(1)}, u32[]{:S(2)}, u32[]{:S(2)}) collective-permute-start(bf16[192,576]{1,0:T(8,128)(2,1)S(1)} %collective-permute-done.22.refs_4_), channel_id=1, source_target_pairs={{0,4},{1,5},{4,8},{5,9},{8,12},{9,13},{12,14},{13,15},{14,10},{15,... | collective-permute-start | bytes 663560 | tf_op jit(solution)/shard_map/ppermute | solution.py:77
  54.9 8.8 %collective-permute-start.27 = (bf16[192,576]{1,0:T(8,128)(2,1)S(1)}, bf16[192,576]{1,0:T(8,128)(2,1)S(1)}, u32[]{:S(2)}, u32[]{:S(2)}) collective-permute-start(bf16[192,576]{1,0:T(8,128)(2,1)S(1)} %collective-permute-done.23.refs_5_), channel_id=1, source_target_pairs={{0,2},{1,3},{4,0},{5,1},{8,4},{9,5},{12,8},{13,9},{14,12},{15,13},... | collective-permute-start | bytes 663560 | tf_op jit(solution)/shard_map/ppermute | solution.py:80
  56.3 9.4 %collective-permute-start.20 = (bf16[192,576]{1,0:T(8,128)(2,1)S(1)}, bf16[192,576]{1,0:T(8,128)(2,1)S(1)}, u32[]{:S(2)}, u32[]{:S(2)}) collective-permute-start(bf16[192,576]{1,0:T(8,128)(2,1)S(1)} %get-tuple-element.114.refs_0_.mo_ref), channel_id=1, source_target_pairs={{0,1},{1,0},{2,3},{3,2},{4,5},{5,4},{6,7},{7,6},{8,9},{9,8},{10,11... | collective-permute-start | bytes 663560 | tf_op jit(solution)/shard_map/ppermute | solution.py:83
  63.7 8.4 %collective-permute-start.28 = (bf16[192,576]{1,0:T(8,128)(2,1)S(1)}, bf16[192,576]{1,0:T(8,128)(2,1)S(1)}, u32[]{:S(2)}, u32[]{:S(2)}) collective-permute-start(bf16[192,576]{1,0:T(8,128)(2,1)S(1)} %collective-permute-done.24.refs_6_), channel_id=1, source_target_pairs={{0,4},{1,5},{4,8},{5,9},{8,12},{9,13},{12,14},{13,15},{14,10},{15,... | collective-permute-start | bytes 663560 | tf_op jit(solution)/shard_map/ppermute | solution.py:77
  64.3 8.3 %collective-permute-start.29 = (bf16[192,576]{1,0:T(8,128)(2,1)S(1)}, bf16[192,576]{1,0:T(8,128)(2,1)S(1)}, u32[]{:S(2)}, u32[]{:S(2)}) collective-permute-start(bf16[192,576]{1,0:T(8,128)(2,1)S(1)} %collective-permute-done.25.refs_7_), channel_id=1, source_target_pairs={{0,2},{1,3},{4,0},{5,1},{8,4},{9,5},{12,8},{13,9},{14,12},{15,13},... | collective-permute-start | bytes 663560 | tf_op jit(solution)/shard_map/ppermute | solution.py:80
  67.3 7.4 %collective-permute-start.30 = (bf16[192,576]{1,0:T(8,128)(2,1)S(1)}, bf16[192,576]{1,0:T(8,128)(2,1)S(1)}, u32[]{:S(2)}, u32[]{:S(2)}) collective-permute-start(bf16[192,576]{1,0:T(8,128)(2,1)S(1)} %collective-permute-done.26.refs_4_), channel_id=1, source_target_pairs={{0,4},{1,5},{4,8},{5,9},{8,12},{9,13},{12,14},{13,15},{14,10},{15,... | collective-permute-start | bytes 663560 | tf_op jit(solution)/shard_map/ppermute | solution.py:77
  68.0 7.3 %collective-permute-start.31 = (bf16[192,576]{1,0:T(8,128)(2,1)S(1)}, bf16[192,576]{1,0:T(8,128)(2,1)S(1)}, u32[]{:S(2)}, u32[]{:S(2)}) collective-permute-start(bf16[192,576]{1,0:T(8,128)(2,1)S(1)} %collective-permute-done.27.refs_5_), channel_id=1, source_target_pairs={{0,2},{1,3},{4,0},{5,1},{8,4},{9,5},{12,8},{13,9},{14,12},{15,13},... | collective-permute-start | bytes 663560 | tf_op jit(solution)/shard_map/ppermute | solution.py:80
  83.4 9.1 %collective-permute-start.38 = (f32[192,1152]{1,0:T(8,128)S(1)}, f32[192,1152]{1,0:T(8,128)S(1)}, u32[]{:S(2)}, u32[]{:S(2)}) collective-permute-start(f32[192,1152]{1,0:T(8,128)S(1)} %get-tuple-element.159), channel_id=1, source_target_pairs={{0,1},{1,0},{2,3},{3,2},{4,5},{5,4},{6,7},{7,6},{8,9},{9,8},{10,11... | collective-permute-start | bytes 2654216 | tf_op jit(solution)/shard_map/ppermute | solution.py:83
  93.8 8.1 %collective-permute-start.40 = (bf16[192,576]{1,0:T(8,128)(2,1)S(1)}, bf16[192,576]{1,0:T(8,128)(2,1)S(1)}, u32[]{:S(2)}, u32[]{:S(2)}) collective-permute-start(bf16[192,576]{1,0:T(8,128)(2,1)S(1)} %get-tuple-element.163), channel_id=1, source_target_pairs={{0,16},{16,0},{1,17},{17,1},{2,18},{18,2},{3,19},{19,3},{4,20},{20... | collective-permute-start | bytes 663560 | tf_op jit(solution)/shard_map/ppermute | solution.py:87
  94.3 7.6 %collective-permute-start.43 = (bf16[8,96,192]{2,1,0:T(8,128)(2,1)S(1)}, bf16[8,96,192]{2,1,0:T(8,128)(2,1)S(1)}, u32[]{:S(2)}, u32[]{:S(2)}) collective-permute-start(bf16[8,96,192]{2,1,0:T(8,128)(2,1)S(1)} %copy-done.5), channel_id=1, source_target_pairs={{0,1},{1,0},{2,3},{3,2},{4,5},{5,4},{6,7},{7,6},{8,9},{9,8},{10,11... | collective-permute-start | bytes 884744 | tf_op jit(solution)/shard_map/ppermute | solution.py:83
  94.3 7.6 %collective-permute-start.44 = (bf16[8,80,192]{2,1,0:T(8,128)(2,1)S(1)}, bf16[8,80,192]{2,1,0:T(8,128)(2,1)S(1)}, u32[]{:S(2)}, u32[]{:S(2)}) collective-permute-start(bf16[8,80,192]{2,1,0:T(8,128)(2,1)S(1)} %copy-done.7), channel_id=1, source_target_pairs={{0,1},{1,0},{2,3},{3,2},{4,5},{5,4},{6,7},{7,6},{8,9},{9,8},{10,11... | collective-permute-start | bytes 737288 | tf_op jit(solution)/shard_map/ppermute | solution.py:83
  94.8 7.1 %collective-permute-start.41 = (bf16[192,576]{1,0:T(8,128)(2,1)S(1)}, bf16[192,576]{1,0:T(8,128)(2,1)S(1)}, u32[]{:S(2)}, u32[]{:S(2)}) collective-permute-start(bf16[192,576]{1,0:T(8,128)(2,1)S(1)} %get-tuple-element.175.do_ref), channel_id=1, source_target_pairs={{0,1},{1,0},{2,3},{3,2},{4,5},{5,4},{6,7},{7,6},{8,9},{9,8},{10,11... | collective-permute-start | bytes 663560 | tf_op jit(solution)/shard_map/ppermute | solution.py:83
  120.0 11.7 %collective-permute-start.53 = (bf16[192,1344]{1,0:T(8,128)(2,1)S(1)}, bf16[192,1344]{1,0:T(8,128)(2,1)S(1)}, u32[]{:S(2)}, u32[]{:S(2)}) collective-permute-start(bf16[192,1344]{1,0:T(8,128)(2,1)S(1)} %shard_map.94), channel_id=1, source_target_pairs={{0,16},{16,0},{1,17},{17,1},{2,18},{18,2},{3,19},{19,3},{4,20},{20... | collective-permute-start | bytes 1548296 | tf_op jit(solution)/shard_map/ppermute | solution.py:87
  125.0 7.6 %collective-permute-start.51 = (bf16[176,576]{1,0:T(8,128)(2,1)S(1)}, bf16[176,576]{1,0:T(8,128)(2,1)S(1)}, u32[]{:S(2)}, u32[]{:S(2)}) collective-permute-start(bf16[176,576]{1,0:T(8,128)(2,1)S(1)} %get-tuple-element.185), channel_id=1, source_target_pairs={{0,4},{1,5},{4,8},{5,9},{8,12},{9,13},{12,14},{13,15},{14,10},{15,... | collective-permute-start | bytes 608264 | tf_op jit(solution)/shard_map/ppermute | solution.py:77
  125.0 7.5 %collective-permute-start.52 = (bf16[176,576]{1,0:T(8,128)(2,1)S(1)}, bf16[176,576]{1,0:T(8,128)(2,1)S(1)}, u32[]{:S(2)}, u32[]{:S(2)}) collective-permute-start(bf16[176,576]{1,0:T(8,128)(2,1)S(1)} %get-tuple-element.186), channel_id=1, source_target_pairs={{0,2},{1,3},{4,0},{5,1},{8,4},{9,5},{12,8},{13,9},{14,12},{15,13},... | collective-permute-start | bytes 608264 | tf_op jit(solution)/shard_map/ppermute | solution.py:80
  (38 other events, 195.4 us)
